TPU v7x, 32 devices: a whole 2x2x4 slice. The times are simulated.
32 devices in a mesh: gx: 8 (over z, core), gy: 4 (over y, x).
Axes of the slice: x: 2, y: 2, z: 4, core: 2. Of those that a mesh axis runs over, the one named last changes fastest.
Arguments:
- density: bfloat16 [32, 16, 1024], P('gx', 'gy'), may hold values from -6 to 6
- p2m_operator: bfloat16 [64, 56], replicated, may hold values from -0.75 to 0.75
- m2l_table: bfloat16 [7, 7, 7, 56, 56], replicated, may hold values from -0.0625 to 0.0625
- near_table: bfloat16 [3, 3, 3, 64, 64], replicated, may hold values from -0.15625 to 0.15625
- l2p_operator: bfloat16 [56, 64], replicated, may hold values from -0.75 to 0.75
Outputs:
- potential: float32 [32, 16, 1024], P('gx', 'gy')
All inputs are finite; a program needn't handle non-finite values.
Results may differ from a plain program's by a relative error of at most 0.003.
Values may be sent and summed in bfloat16 or wider, within the bound.
No kernel may reach another device: no remote copies, remote signals or barrier semaphores. Data moves between devices by JAX's collectives and lax.ppermute only.
A program may use at most 128 MiB of HBM per device.

v0:
```python
import jax
import jax.numpy as jnp
from jax import lax
from jax.sharding import PartitionSpec as P


def extended_2(cells, sides, width):
    for axis, dim in sides:
        count = lax.axis_size(axis)
        ends = count - 1
        head = lax.slice_in_dim(cells, 0, width, axis=dim)
        tail = lax.slice_in_dim(cells, cells.shape[dim] - width, cells.shape[dim], axis=dim)
        cells = jnp.concatenate(
            [
                lax.ppermute(tail, axis, [(i, (i + 1) % count) for i in range(ends)]),
                cells,
                lax.ppermute(head, axis, [((i + 1) % count, i) for i in range(ends)]),
            ],
            axis=dim,
        )
    return cells


def masked_table(kernel_table):
    offsets = jnp.abs(jnp.arange(7) - 3)
    largest = jnp.maximum(
        jnp.maximum(offsets[:, None, None], offsets[None, :, None]), offsets[None, None, :]
    )
    distant = (largest >= 2).astype(kernel_table.dtype)
    return kernel_table * distant[:, :, :, None, None]


def offset_valid(count, shift):
    parity = jnp.arange(count) % 2
    if shift == 0:
        return (parity == 1).astype(jnp.bfloat16)
    if shift == 6:
        return (parity == 0).astype(jnp.bfloat16)
    return jnp.ones((count,), jnp.bfloat16)


def far_field(extended, table):
    across = extended.shape[0] - 6
    sideways = extended.shape[1] - 6
    height = extended.shape[2] - 6
    surface = extended.shape[-1]
    total = jnp.zeros((across * sideways * height, surface), jnp.float32)
    for shift_x in range(7):
        valid_x = offset_valid(across, shift_x)
        pieces = []
        for shift_y in range(7):
            valid_y = offset_valid(sideways, shift_y)
            for shift_z in range(7):
                valid_z = offset_valid(height, shift_z)
                weight_mask = (
                    valid_x[:, None, None] * valid_y[None, :, None] * valid_z[None, None, :]
                )
                piece = extended[
                    shift_x : shift_x + across,
                    shift_y : shift_y + sideways,
                    shift_z : shift_z + height,
                    :,
                ]
                pieces.append(piece * weight_mask[:, :, :, None])
        stacked = jnp.stack(pieces, 3).reshape(across * sideways * height, 49 * surface)
        total = total + jnp.dot(
            stacked,
            table[shift_x].reshape(49 * surface, surface),
            preferred_element_type=jnp.float32,
        )
    return total


def near_field(padded, near_matrix):
    across = padded.shape[0] - 2
    sideways = padded.shape[1] - 2
    height = padded.shape[2] - 2
    node_count = padded.shape[-1]
    pieces = []
    for offset_x in range(3):
        for offset_y in range(3):
            for offset_z in range(3):
                pieces.append(
                    padded[
                        offset_x : offset_x + across,
                        offset_y : offset_y + sideways,
                        offset_z : offset_z + height,
                        :,
                    ]
                )
    stacked = jnp.concatenate(pieces, axis=-1).reshape(across * sideways * height, 27 * node_count)
    result = jnp.dot(stacked, near_matrix, preferred_element_type=jnp.float32)
    return result.reshape(across, sideways, height, node_count)


def local(density, p2m_operator, m2l_table, near_table, l2p_operator):
    across, sideways, columns = density.shape
    node_count = near_table.shape[-1]
    surface = p2m_operator.shape[1]
    height = columns // node_count
    table = masked_table(m2l_table)
    near_matrix = near_table.reshape(27 * node_count, node_count)
    widened = extended_2(density, (("gx", 0), ("gy", 1)), 2)
    wide_cells = widened.reshape(across + 4, sideways + 4, height, node_count)
    extended = jnp.dot(
        wide_cells.reshape((across + 4) * (sideways + 4) * height, node_count),
        p2m_operator,
        preferred_element_type=jnp.float32,
    ).astype(jnp.bfloat16)
    extended = extended.reshape(across + 4, sideways + 4, height, surface)
    padded = jnp.pad(wide_cells[1:-1, 1:-1], ((0, 0), (0, 0), (1, 1), (0, 0)))
    extended = jnp.pad(extended, ((1, 1), (1, 1), (3, 3), (0, 0)))
    expansion = far_field(extended, table)
    rounded = expansion.astype(jnp.bfloat16)
    close_part = near_field(padded, near_matrix)
    distant_part = jnp.dot(rounded, l2p_operator, preferred_element_type=jnp.float32)
    potential = close_part + distant_part.reshape(across, sideways, height, node_count)
    return potential.reshape(across, sideways, height * node_count)


def solution(mesh):
    placed = (P("gx", "gy", None), P(), P(), P(), P())
    return jax.shard_map(
        local, mesh=mesh, in_specs=placed, out_specs=P("gx", "gy", None), check_vma=False
    )
```

profile of v0, /device:TPU:20, one launch (start us, length us, event | category | flops | bytes accessed | tf_op | source)
XLA Modules:
  0.0 214.5 jit_solution(17125710314664164784)
XLA Ops:
  0.8 1.9 collective-permute-start
  2.7 3.6 %collective-permute-start.1 = (bf16[2,4,1024]{2,1,0:T(4,128)(2,1)S(1)}, bf16[2,4,1024]{2,1,0:T(4,128)(2,1)S(1)}, u32[]{:S(2)}, u32[]{:S(2)}) collective-permute-start(bf16[2,4,1024]{2,1,0:T(4,128)(2,1)S(1)} %get-tuple-element.180), channel_id=1, source_target_pairs={{4,0},{8,4},{12,8},{16,12},{20,16},{24,20},{28,24},{5,1},{9,5},{13... | collective-permute-start | bytes 49160 | tf_op jit(solution)/shard_map/ppermute | solution.py:17
  6.6 3.5 %broadcast_multiply_fusion = bf16[7,7,7,56,56]{4,3,2,1,0:T(8,128)(2,1)S(1)} fusion(bf16[7,7,7,56,56]{4,3,2,1,0:T(8,128)(2,1)} %param.7, bf16[7,7,7]{2,1,0:T(8,128)(2,1)S(1)} %fusion.538), kind=kLoop, calls=%fused_computation.318 | loop fusion | flops 1075648 | bytes 4303278 | tf_op jit(solution)/shard_map/mul | solution.py:30
  10.1 2.0 fusion.539
  12.3 3.3 %collective-permute-start.3 = (bf16[8,2,1024]{2,1,0:T(2,128)(2,1)S(1)}, bf16[8,2,1024]{2,1,0:T(2,128)(2,1)S(1)}, u32[]{:S(2)}, u32[]{:S(2)}) collective-permute-start(bf16[8,2,1024]{2,1,0:T(2,128)(2,1)S(1)} %get-tuple-element.179), channel_id=1, source_target_pairs={{1,0},{2,1},{3,2},{5,4},{6,5},{7,6},{9,8},{10,9},{11,10},{13,12},{... | collective-permute-start | bytes 98312 | tf_op jit(solution)/shard_map/ppermute | solution.py:17
  15.7 3.0 %collective-permute-start.2 = (bf16[8,2,1024]{2,1,0:T(2,128)(2,1)S(1)}, bf16[8,2,1024]{2,1,0:T(2,128)(2,1)S(1)}, u32[]{:S(2)}, u32[]{:S(2)}) collective-permute-start(bf16[8,2,1024]{2,1,0:T(2,128)(2,1)S(1)} %get-tuple-element.178), channel_id=1, source_target_pairs={{0,1},{1,2},{2,3},{4,5},{5,6},{6,7},{8,9},{9,10},{10,11},{12,13},{... | collective-permute-start | bytes 98312 | tf_op jit(solution)/shard_map/ppermute | solution.py:15
  18.8 3.6 %collective-permute-done.2 = bf16[8,2,1024]{2,1,0:T(2,128)(2,1)S(1)} collective-permute-done((bf16[8,2,1024]{2,1,0:T(2,128)(2,1)S(1)}, bf16[8,2,1024]{2,1,0:T(2,128)(2,1)S(1)}, u32[]{:S(2)}, u32[]{:S(2)}) %collective-permute-start.2) | collective-permute-done | bytes 32800 | tf_op jit(solution)/shard_map/ppermute | solution.py:15
  23.6 0.9 fusion.540
  28.8 0.9 constant_dynamic-update-slice_fusion.296
  38.8 0.9 constant_dynamic-update-slice_fusion.290
  110.6 0.9 constant_dynamic-update-slice_fusion.254
  118.2 1.0 constant_dynamic-update-slice_fusion.297
  119.2 1.0 constant_dynamic-update-slice_fusion.201
  123.3 4.1 %copy.10 = bf16[4,4,16,49,56]{4,3,2,1,0:T(8,128)(2,1)} copy(bf16[4,4,16,49,56]{4,2,1,0,3:T(8,128)(2,1)S(1)} %get-tuple-element.222) | data formatting | bytes 2809856 | tf_op jit(solution)/shard_map/stack | solution.py:65
  127.4 5.7 %reshape.236 = bf16[256,2744]{1,0:T(8,128)(2,1)} reshape(bf16[4,4,16,49,56]{4,3,2,1,0:T(8,128)(2,1)} %copy.10) | data formatting | bytes 2809856 | tf_op jit(solution)/shard_map/reshape | solution.py:65
  133.1 0.9 constant_dynamic-update-slice_fusion.248
  134.0 5.9 %copy.11 = bf16[4,4,16,49,56]{4,3,2,1,0:T(8,128)(2,1)} copy(bf16[4,4,16,49,56]{4,2,1,0,3:T(8,128)(2,1)} %get-tuple-element.15) | data formatting | bytes 2809856 | tf_op jit(solution)/shard_map/stack | solution.py:65
  139.8 4.8 %reshape.237 = bf16[256,2744]{1,0:T(8,128)(2,1)S(1)} reshape(bf16[4,4,16,49,56]{4,3,2,1,0:T(8,128)(2,1)} %copy.11) | data formatting | bytes 2809856 | tf_op jit(solution)/shard_map/reshape | solution.py:65
  144.7 5.9 %copy.12 = bf16[4,4,16,49,56]{4,3,2,1,0:T(8,128)(2,1)} copy(bf16[4,4,16,49,56]{4,2,1,0,3:T(8,128)(2,1)} %get-tuple-element.13) | data formatting | bytes 2809856 | tf_op jit(solution)/shard_map/stack | solution.py:65
  150.5 5.7 %reshape.238 = bf16[256,2744]{1,0:T(8,128)(2,1)} reshape(bf16[4,4,16,49,56]{4,3,2,1,0:T(8,128)(2,1)} %copy.12) | data formatting | bytes 2809856 | tf_op jit(solution)/shard_map/reshape | solution.py:65
  156.2 5.9 %copy.13 = bf16[4,4,16,49,56]{4,3,2,1,0:T(8,128)(2,1)} copy(bf16[4,4,16,49,56]{4,2,1,0,3:T(8,128)(2,1)} %get-tuple-element.14) | data formatting | bytes 2809856 | tf_op jit(solution)/shard_map/stack | solution.py:65
  162.1 5.9 %reshape.239 = bf16[256,2744]{1,0:T(8,128)(2,1)} reshape(bf16[4,4,16,49,56]{4,3,2,1,0:T(8,128)(2,1)} %copy.13) | data formatting | bytes 2809856 | tf_op jit(solution)/shard_map/reshape | solution.py:65
  168.0 5.9 %copy.14 = bf16[4,4,16,49,56]{4,3,2,1,0:T(8,128)(2,1)} copy(bf16[4,4,16,49,56]{4,2,1,0,3:T(8,128)(2,1)} %get-tuple-element.16) | data formatting | bytes 2809856 | tf_op jit(solution)/shard_map/stack | solution.py:65
  173.8 5.7 %reshape.240 = bf16[256,2744]{1,0:T(8,128)(2,1)} reshape(bf16[4,4,16,49,56]{4,3,2,1,0:T(8,128)(2,1)} %copy.14) | data formatting | bytes 2809856 | tf_op jit(solution)/shard_map/reshape | solution.py:65
  179.6 5.9 %copy.15 = bf16[4,4,16,49,56]{4,3,2,1,0:T(8,128)(2,1)} copy(bf16[4,4,16,49,56]{4,2,1,0,3:T(8,128)(2,1)} %get-tuple-element.12) | data formatting | bytes 2809856 | tf_op jit(solution)/shard_map/stack | solution.py:65
  185.4 5.7 %reshape.241 = bf16[256,2744]{1,0:T(8,128)(2,1)} reshape(bf16[4,4,16,49,56]{4,3,2,1,0:T(8,128)(2,1)} %copy.15) | data formatting | bytes 2809856 | tf_op jit(solution)/shard_map/reshape | solution.py:65
  191.1 5.9 %copy.16 = bf16[4,4,16,49,56]{4,3,2,1,0:T(8,128)(2,1)} copy(bf16[4,4,16,49,56]{4,2,1,0,3:T(8,128)(2,1)} %copy-done.7) | data formatting | bytes 2809856 | tf_op jit(solution)/shard_map/stack | solution.py:65
  197.0 6.0 %reshape.242 = bf16[256,2744]{1,0:T(8,128)(2,1)} reshape(bf16[4,4,16,49,56]{4,3,2,1,0:T(8,128)(2,1)} %copy.16) | data formatting | bytes 2809856 | tf_op jit(solution)/shard_map/reshape | solution.py:65
  203.0 1.0 pad_slice_fusion.318
  204.1 2.3 %fusion.543 = f32[256,56]{1,0:T(8,128)S(1)} fusion(bf16[256,2744]{1,0:T(8,128)(2,1)} %reshape.236, bf16[2744,56]{1,0:T(8,128)(2,1)} %bitcast.1655), kind=kOutput, calls=%fused_computation.1289 | convolution fusion | flops 78675968 | bytes 1769600 | tf_op jit(solution)/shard_map/dot_general | solution.py:66
  209.2 1.4 fusion.1
  210.5 2.5 %concatenate.11 = bf16[4,4,16,1728]{3,2,1,0:T(8,128)(2,1)S(1)} concatenate(bf16[4,4,16,64]{3,2,1,0:T(8,128)(2,1)} %get-tuple-element.177, bf16[4,4,16,64]{3,2,1,0:T(8,128)(2,1)} %get-tuple-element.117, bf16[4,4,16,64]{3,2,1,0:T(8,128)(2,1)} %get-tuple-element.161, bf16[4,4,16,64]{3,2,1,0:T(8,128)(2,1)} %get-tuple-element.162, bf16[4,4,16,64]{3,2,1,0:T(8,128)(2,1)} %get-tuple-element.116, ...), dimensions={3} | concatenate | bytes 1769472 | tf_op jit(solution)/shard_map/concatenate | solution.py:91
  (297 shorter events, 99.9 us)
Async XLA Ops:
  0.0 213.1 %copy-start = (bf16[3,3,3,64,64]{4,3,2,1,0:T(8,128)(2,1)S(1)}, bf16[3,3,3,64,64]{4,3,2,1,0:T(8,128)(2,1)}, u32[]{:S(2)}) copy-start(bf16[3,3,3,64,64]{4,3,2,1,0:T(8,128)(2,1)} %param.8) | copy-start | bytes 663556
  0.8 11.4 %collective-permute-start = (bf16[2,4,1024]{2,1,0:T(4,128)(2,1)S(1)}, bf16[2,4,1024]{2,1,0:T(4,128)(2,1)S(1)}, u32[]{:S(2)}, u32[]{:S(2)}) collective-permute-start(bf16[2,4,1024]{2,1,0:T(4,128)(2,1)S(1)} %get-tuple-element.181), channel_id=1, source_target_pairs={{0,4},{4,8},{8,12},{12,16},{16,20},{20,24},{24,28},{1,5},{5,9},{9,... | collective-permute-start | bytes 49160 | tf_op jit(solution)/shard_map/ppermute | solution.py:15
  2.7 9.5 %collective-permute-start.1 = (bf16[2,4,1024]{2,1,0:T(4,128)(2,1)S(1)}, bf16[2,4,1024]{2,1,0:T(4,128)(2,1)S(1)}, u32[]{:S(2)}, u32[]{:S(2)}) collective-permute-start(bf16[2,4,1024]{2,1,0:T(4,128)(2,1)S(1)} %get-tuple-element.180), channel_id=1, source_target_pairs={{4,0},{8,4},{12,8},{16,12},{20,16},{24,20},{28,24},{5,1},{9,5},{13... | collective-permute-start | bytes 49160 | tf_op jit(solution)/shard_map/ppermute | solution.py:17
  10.0 2.2 %copy-start.13 = (bf16[4,4,1024]{2,1,0:T(4,128)(2,1)S(1)}, bf16[4,4,1024]{2,1,0:T(4,128)(2,1)}, u32[]{:S(2)}) copy-start(bf16[4,4,1024]{2,1,0:T(4,128)(2,1)} %param.5) | copy-start | bytes 98308
  10.1 14.4 %copy-start.14 = (bf16[64,56]{0,1:T(8,128)(2,1)S(1)}, bf16[64,56]{0,1:T(8,128)(2,1)}, u32[]{:S(2)}) copy-start(bf16[64,56]{0,1:T(8,128)(2,1)} %param.6) | copy-start | bytes 21508
  12.3 6.5 %collective-permute-start.3 = (bf16[8,2,1024]{2,1,0:T(2,128)(2,1)S(1)}, bf16[8,2,1024]{2,1,0:T(2,128)(2,1)S(1)}, u32[]{:S(2)}, u32[]{:S(2)}) collective-permute-start(bf16[8,2,1024]{2,1,0:T(2,128)(2,1)S(1)} %get-tuple-element.179), channel_id=1, source_target_pairs={{1,0},{2,1},{3,2},{5,4},{6,5},{7,6},{9,8},{10,9},{11,10},{13,12},{... | collective-permute-start | bytes 98312 | tf_op jit(solution)/shard_map/ppermute | solution.py:17
  15.7 6.7 %collective-permute-start.2 = (bf16[8,2,1024]{2,1,0:T(2,128)(2,1)S(1)}, bf16[8,2,1024]{2,1,0:T(2,128)(2,1)S(1)}, u32[]{:S(2)}, u32[]{:S(2)}) collective-permute-start(bf16[8,2,1024]{2,1,0:T(2,128)(2,1)S(1)} %get-tuple-element.178), channel_id=1, source_target_pairs={{0,1},{1,2},{2,3},{4,5},{5,6},{6,7},{8,9},{9,10},{10,11},{12,13},{... | collective-permute-start | bytes 98312 | tf_op jit(solution)/shard_map/ppermute | solution.py:15
  118.2 5.1 %copy-start.6 = (bf16[4,4,16,49,56]{4,2,1,0,3:T(8,128)(2,1)}, bf16[4,4,16,49,56]{4,2,1,0,3:T(8,128)(2,1)S(1)}, u32[]{:S(2)}) copy-start(bf16[4,4,16,49,56]{4,2,1,0,3:T(8,128)(2,1)S(1)} %get-tuple-element.40) | copy-start | bytes 4214788
  119.2 4.1 %copy-start.7 = (bf16[4,4,16,49,56]{4,2,1,0,3:T(8,128)(2,1)}, bf16[4,4,16,49,56]{4,2,1,0,3:T(8,128)(2,1)S(1)}, u32[]{:S(2)}) copy-start(bf16[4,4,16,49,56]{4,2,1,0,3:T(8,128)(2,1)S(1)} %get-tuple-element.118) | copy-start | bytes 4214788
  197.0 6.0 %copy-start.12 = (bf16[6,6,16,64]{3,2,1,0:T(8,128)(2,1)S(1)}, bf16[6,6,16,64]{3,2,1,0:T(8,128)(2,1)}, u32[]{:S(2)}) copy-start(bf16[6,6,16,64]{3,2,1,0:T(8,128)(2,1)} %slice.1573) | copy-start | bytes 221188
  203.0 3.4 %copy-start.11 = (bf16[1,7,7,56,56]{4,3,2,1,0:T(8,128)(2,1)S(1)}, bf16[1,7,7,56,56]{4,3,2,1,0:T(8,128)(2,1)}, u32[]{:S(2)}) copy-start(bf16[1,7,7,56,56]{4,3,2,1,0:T(8,128)(2,1)} %get-tuple-element.10) | copy-start | bytes 921988
  203.0 3.9 %copy-start.1 = (bf16[256,2744]{1,0:T(8,128)(2,1)S(1)}, bf16[256,2744]{1,0:T(8,128)(2,1)}, u32[]{:S(2)}) copy-start(bf16[256,2744]{1,0:T(8,128)(2,1)} %reshape.238) | copy-start | bytes 4214788
  203.0 3.9 %copy-start.10 = (bf16[1,7,7,56,56]{4,3,2,1,0:T(8,128)(2,1)S(1)}, bf16[1,7,7,56,56]{4,3,2,1,0:T(8,128)(2,1)}, u32[]{:S(2)}) copy-start(bf16[1,7,7,56,56]{4,3,2,1,0:T(8,128)(2,1)} %get-tuple-element.9) | copy-start | bytes 921988
  204.1 3.4 %copy-start.2 = (bf16[256,2744]{1,0:T(8,128)(2,1)S(1)}, bf16[256,2744]{1,0:T(8,128)(2,1)}, u32[]{:S(2)}) copy-start(bf16[256,2744]{1,0:T(8,128)(2,1)} %reshape.239) | copy-start | bytes 4214788
  204.1 3.4 %copy-start.9 = (bf16[1,7,7,56,56]{4,3,2,1,0:T(8,128)(2,1)S(1)}, bf16[1,7,7,56,56]{4,3,2,1,0:T(8,128)(2,1)}, u32[]{:S(2)}) copy-start(bf16[1,7,7,56,56]{4,3,2,1,0:T(8,128)(2,1)} %get-tuple-element.8) | copy-start | bytes 921988
  206.4 1.7 copy-start.3
  206.4 1.7 copy-start.8
  206.9 1.7 copy-start.4
  207.5 1.7 copy-start.5
where the time goes:
time: 218 us; the launch traced here: 214 us
  local copies, waits for them, and re-layouts  141 us (65%)
  other arithmetic  49.6 us (23%)
  starting transfers between devices  11.9 us (5%)
  matrix products  6.97 us (3%)
  waiting for transfers between devices  3.56 us (2%)
    unnamed x135, local copies, waits for them, and re-layouts  53.2 us
    unnamed x137, other arithmetic  43.1 us
    reshape x7, local copies, waits for them, and re-layouts, far_field(): jnp.stack(pieces, 3).reshape(across * sideways * height, 49 * surface)  39.5 us
    another operation x7, local copies, waits for them, and re-layouts, far_field(): jnp.stack(pieces, 3).reshape(across * sideways * height, 49 * surface)  39.3 us
    ppermute x2, starting transfers between devices, extended_2(): lax.ppermute(head, axis, [((i + 1) % count, i) for i in range(ends)])  6.98 us
    ppermute x2, starting transfers between devices, extended_2(): lax.ppermute(tail, axis, [(i, (i + 1) % count) for i in range(ends)])  4.94 us
    dot_general x6, matrix products, far_field(): jnp.dot(stacked, table[shift_x].reshape(49 * surface, surface), preferred...  4.94 us
  transfers between devices with their start and end apart: 4, of which 1 were waited for; matrix products, arithmetic and copies ran while one was open for 3% of the time, Pallas kernels for 0%

commit v1 on v0

v1 whole, which is shorter than its diff:
```python
import jax
import jax.numpy as jnp
from jax import lax
from jax.experimental import pallas as pl
from jax.experimental.pallas import tpu as pltpu
from jax.sharding import PartitionSpec as P

BF16 = jnp.bfloat16
F32 = jnp.float32
WIDTH = 64
PAIR = 2 * WIDTH
VMEM_LIMIT = 40 * 1024 * 1024


def swapped(cells, axis, odd):
    count = lax.axis_size(axis)
    pairs = []
    for i in range(odd, count - 1, 2):
        pairs += [(i, i + 1), (i + 1, i)]
    return lax.ppermute(cells, axis, pairs)


def exchanged(cells, axis, dim):
    parity = lax.axis_index(axis) % 2
    size = cells.shape[dim]
    odd = swapped(cells, axis, 1)
    even = swapped(cells, axis, 0)

    def head(part):
        return lax.slice_in_dim(part, 0, 2, axis=dim)

    def tail(part):
        return lax.slice_in_dim(part, size - 2, size, axis=dim)

    low = jnp.where(parity == 0, tail(odd), tail(even))
    high = jnp.where(parity == 0, head(even), head(odd))
    return low, high


def sent(cells, axis, dim):
    parity = lax.axis_index(axis) % 2
    size = cells.shape[dim]
    head = lax.slice_in_dim(cells, 0, 2, axis=dim)
    tail = lax.slice_in_dim(cells, size - 2, size, axis=dim)
    even = swapped(jnp.where(parity == 0, tail, head), axis, 0)
    odd = swapped(jnp.where(parity == 0, head, tail), axis, 1)
    low = jnp.where(parity == 0, odd, even)
    high = jnp.where(parity == 0, even, odd)
    return low, high


def widened(density):
    low, high = exchanged(density, "gy", 1)
    wide = jnp.concatenate([low, density, high], axis=1)
    low, high = sent(wide, "gx", 0)
    return jnp.concatenate([low, wide, high], axis=0)


def square(block):
    rows, columns = block.shape
    if columns < WIDTH:
        block = jnp.concatenate([block, jnp.zeros((rows, WIDTH - columns), BF16)], axis=1)
    if rows < WIDTH:
        block = jnp.concatenate([block, jnp.zeros((WIDTH - rows, WIDTH), BF16)], axis=0)
    return block


def pack_kernel(p2m_ref, m2l_ref, near_ref, l2p_ref, far_out, near_out, p2m_out, l2p_out):
    blank = jnp.zeros((WIDTH, WIDTH), BF16)

    def far_blocks(offset_x, offset_y):
        inner = 2 <= offset_x <= 4 and 2 <= offset_y <= 4
        entries = []
        for offset_z in range(7):
            if inner and 2 <= offset_z <= 4:
                entries.append(blank)
            else:
                entries.append(square(m2l_ref[offset_x, offset_y, offset_z]))
        for s in range(6):
            far_out[offset_x, offset_y, s] = jnp.concatenate([entries[s + 1], entries[s]], axis=1)

    for offset_x in range(7):
        for offset_y in range(7):
            far_blocks(offset_x, offset_y)
    for offset_x in range(3):
        near_out[offset_x, 0] = jnp.zeros((2, PAIR, PAIR), BF16)
        near_out[offset_x, 4] = jnp.zeros((2, PAIR, PAIR), BF16)
        for offset_y in range(3):
            before, same, after = [near_ref[offset_x, offset_y, z] for z in range(3)]
            upper = jnp.concatenate([same, before], axis=1)
            lower = jnp.concatenate([after, same], axis=1)
            near_out[offset_x, offset_y + 1, 0] = jnp.concatenate([upper, lower], axis=0)
            upper = jnp.concatenate([blank, after], axis=1)
            lower = jnp.concatenate([before, blank], axis=1)
            near_out[offset_x, offset_y + 1, 1] = jnp.concatenate([upper, lower], axis=0)
    p2m = square(p2m_ref[...])
    p2m_out[...] = jnp.concatenate(
        [jnp.concatenate([p2m, blank], axis=1), jnp.concatenate([blank, p2m], axis=1)], axis=0
    )
    l2p = square(l2p_ref[...])
    double = jnp.concatenate(
        [jnp.concatenate([l2p, blank], axis=1), jnp.concatenate([blank, l2p], axis=1)], axis=0
    )
    empty = jnp.zeros((PAIR, PAIR), BF16)
    l2p_out[...] = jnp.concatenate(
        [jnp.concatenate([double, empty], axis=1), jnp.concatenate([empty, double], axis=1)], axis=0
    )


def packed(p2m_operator, m2l_table, near_table, l2p_operator):
    shapes = [(7, 7, 6, WIDTH, PAIR), (3, 5, 2, PAIR, PAIR), (PAIR, PAIR), (2 * PAIR, 2 * PAIR)]
    return pl.pallas_call(
        pack_kernel,
        out_shape=[pltpu.VMEM(shape, BF16) for shape in shapes],
        in_specs=[pl.BlockSpec(memory_space=pltpu.VMEM)] * 4,
        out_specs=[pl.BlockSpec(memory_space=pltpu.VMEM)] * 4,
        compiler_params=pltpu.CompilerParams(vmem_limit_bytes=VMEM_LIMIT),
        cost_estimate=pl.CostEstimate(flops=4000000, bytes_accessed=10000000, transcendentals=0),
        name="pack",
    )(p2m_operator, m2l_table, near_table, l2p_operator)


def shifted(rows):
    place = lax.broadcasted_iota(jnp.int32, rows.shape, 0) % 8
    before = jnp.where(place == 0, 0.0, jnp.roll(rows, 1, axis=0))
    after = jnp.where(place == 7, 0.0, jnp.roll(rows, -1, axis=0))
    return before, rows, after


def window_rows(slab, first):
    if first == -1:
        blank = jnp.zeros_like(slab[:8])
        parts = [blank, slab[0:8], blank, slab[16:24]]
        return jnp.concatenate(parts, axis=0)
    if first == 5:
        blank = jnp.zeros_like(slab[:8])
        parts = [slab[40:48], blank, slab[56:64], blank]
        return jnp.concatenate(parts, axis=0)
    return slab[8 * first : 8 * first + 32]


def main_kernel(cells_ref, far_ref, near_ref, p2m_ref, l2p_ref, out_ref, rows_ref, out_rows):
    pairs = cells_ref.shape[2] // PAIR
    for x in range(8):
        for pair in range(pairs):
            rows_ref[pl.ds(x * pairs + pair, 8, stride=8 * pairs), :] = cells_ref[
                x, :, pair * PAIR : (pair + 1) * PAIR
            ].astype(F32)
    cells = rows_ref[...]
    multipole = jnp.dot(cells.astype(BF16), p2m_ref[...], preferred_element_type=F32)
    multipole = multipole.astype(BF16).astype(F32)
    sources = shifted(multipole)
    far = jnp.zeros((64, 2 * PAIR), F32)
    for offset_x in range(7):
        chunks = []
        for j in range(6):
            for b in range(3):
                upper = window_rows(sources[b][64 * j : 64 * j + 64], offset_x - 1)
                lower = window_rows(sources[b][64 * j + 128 : 64 * j + 192], offset_x - 1)
                chunks.append(jnp.concatenate([upper, lower], axis=0).astype(BF16))
        weights = jnp.concatenate(
            [
                far_ref[offset_x, 1:7].reshape(36 * WIDTH, PAIR),
                far_ref[offset_x, 0:6].reshape(36 * WIDTH, PAIR),
            ],
            axis=1,
        )
        far += jnp.dot(jnp.concatenate(chunks, axis=1), weights, preferred_element_type=F32)
    before, same, after = shifted(cells)
    lane = lax.broadcasted_iota(jnp.int32, cells.shape, 1)
    beside = jnp.where(lane < WIDTH, after, before)
    total = jnp.dot(far.astype(BF16), l2p_ref[...], preferred_element_type=F32)
    for offset_x in range(3):
        chunks = []
        for j in range(1, 5):
            for kind in (same, beside):
                upper = window_rows(kind[64 * j : 64 * j + 64], offset_x + 1)
                lower = window_rows(kind[64 * j + 128 : 64 * j + 192], offset_x + 1)
                chunks.append(jnp.concatenate([upper, lower], axis=0).astype(BF16))
        weights = jnp.concatenate(
            [
                near_ref[offset_x, 1:5].reshape(8 * PAIR, PAIR),
                near_ref[offset_x, 0:4].reshape(8 * PAIR, PAIR),
            ],
            axis=1,
        )
        total += jnp.dot(jnp.concatenate(chunks, axis=1), weights, preferred_element_type=F32)
    for y in range(4):
        out_rows[32 * y : 32 * y + 32, :] = total[
            32 * (y // 2) : 32 * (y // 2) + 32, PAIR * (y % 2) : PAIR * (y % 2) + PAIR
        ]
    for x in range(4):
        for pair in range(pairs):
            out_ref[x, :, pair * PAIR : (pair + 1) * PAIR] = out_rows[
                pl.ds(x * pairs + pair, 4, stride=4 * pairs), :
            ]


def local(density, p2m_operator, m2l_table, near_table, l2p_operator):
    tables = packed(p2m_operator, m2l_table, near_table, l2p_operator)
    cells = widened(density)
    return pl.pallas_call(
        main_kernel,
        out_shape=jax.ShapeDtypeStruct(density.shape, F32),
        in_specs=[pl.BlockSpec(memory_space=pltpu.VMEM)] * 5,
        out_specs=pl.BlockSpec(memory_space=pltpu.VMEM),
        scratch_shapes=[pltpu.VMEM((512, PAIR), F32), pltpu.VMEM((128, PAIR), F32)],
        compiler_params=pltpu.CompilerParams(vmem_limit_bytes=VMEM_LIMIT),
        cost_estimate=pl.CostEstimate(flops=600000000, bytes_accessed=10000000, transcendentals=0),
        name="main",
    )(cells, *tables)


def solution(mesh):
    placed = (P("gx", "gy", None), P(), P(), P(), P())
    return jax.shard_map(
        local, mesh=mesh, in_specs=placed, out_specs=P("gx", "gy", None), check_vma=False
    )
```

time: 218 us -> 23.5 us (0.11)
  the two profiles are of different devices: /device:TPU:20 before, /device:TPU:0 now
where the time goes in v1:
time: 23.5 us; the launch traced here: 23 us
  starting transfers between devices  10.2 us (43%)
  local copies, waits for them, and re-layouts  4.92 us (21%)
  Pallas kernels  4.52 us (19%)
  waiting for transfers between devices  2.37 us (10%)
  other arithmetic  0.96 us (4%)
    ppermute x4, starting transfers between devices, swapped(): return lax.ppermute(cells, axis, pairs)  10.2 us
    unnamed x9, local copies, waits for them, and re-layouts  4.92 us
    pallas_call x1, Pallas kernels, local(): pl.pallas_call(main_kernel, out_shape=jax.ShapeDtypeStruct(density.shape,...  3.14 us
    ppermute x4, waiting for transfers between devices, swapped(): return lax.ppermute(cells, axis, pairs)  2.37 us
    pallas_call x1, Pallas kernels, packed(): pl.pallas_call(pack_kernel, out_shape=[pltpu.VMEM(shape, BF16) for shape...  1.38 us
    concatenate x1, other arithmetic, widened(): wide = jnp.concatenate([low, density, high], axis=1)  0.82 us
  transfers between devices with their start and end apart: 4, of which 1 were waited for; matrix products, arithmetic and copies ran while one was open for 3% of the time, Pallas kernels for 6%

profile of v1, /device:TPU:0, one launch (start us, length us, event | category | flops | bytes accessed | tf_op | source)
XLA Modules:
  0.0 23.0 jit_solution(2188937767454802434)
XLA Ops:
  0.0 0.0 copy-start.3
  0.0 0.8 %collective-permute-start = (bf16[4,4,1024]{2,1,0:T(4,128)(2,1)}, bf16[4,4,1024]{2,1,0:T(4,128)(2,1)S(1)}, u32[]{:S(2)}, u32[]{:S(2)}) collective-permute-start(bf16[4,4,1024]{2,1,0:T(4,128)(2,1)} %param.5), channel_id=1, source_target_pairs={{1,2},{2,1},{5,6},{6,5},{9,10},{10,9},{13,14},{14,13},{17,18},{18,... | collective-permute-start | bytes 98312 | tf_op jit(solution)/shard_map/ppermute | solution.py:20
  0.8 5.7 %collective-permute-start.1 = (bf16[4,4,1024]{2,1,0:T(4,128)(2,1)}, bf16[4,4,1024]{2,1,0:T(4,128)(2,1)S(1)}, u32[]{:S(2)}, u32[]{:S(2)}) collective-permute-start(bf16[4,4,1024]{2,1,0:T(4,128)(2,1)} %param.5), channel_id=1, source_target_pairs={{0,1},{1,0},{2,3},{3,2},{4,5},{5,4},{6,7},{7,6},{8,9},{9,8},{10,11... | collective-permute-start | bytes 98312 | tf_op jit(solution)/shard_map/ppermute | solution.py:20
  6.5 0.0 collective-permute-done
  6.5 2.4 %collective-permute-done.1 = bf16[4,4,1024]{2,1,0:T(4,128)(2,1)S(1)} collective-permute-done((bf16[4,4,1024]{2,1,0:T(4,128)(2,1)}, bf16[4,4,1024]{2,1,0:T(4,128)(2,1)S(1)}, u32[]{:S(2)}, u32[]{:S(2)}) %collective-permute-start.1) | collective-permute-done | bytes 32800 | tf_op jit(solution)/shard_map/ppermute | solution.py:20
  8.9 0.1 broadcast_select_fusion.1
  9.0 0.8 %pad_maximum_fusion.1 = bf16[4,8,1024]{2,1,0:T(8,128)(2,1)S(1)} fusion(bf16[4,2,1024]{2,1,0:T(2,128)(2,1)S(1)} %get-tuple-element.18, bf16[4,4,1024]{2,1,0:T(4,128)(2,1)} %param.5, bf16[4,2,1024]{2,1,0:T(2,128)(2,1)S(1)} %get-tuple-element.17), kind=kLoop, calls=%fused_computation.1 | loop fusion | flops 196608 | bytes 131072 | tf_op jit(solution)/shard_map/concatenate | solution.py:54
  9.8 0.7 %collective-permute-start.2 = (bf16[2,8,1024]{2,1,0:T(8,128)(2,1)S(1)}, bf16[2,8,1024]{2,1,0:T(8,128)(2,1)S(1)}, u32[]{:S(2)}, u32[]{:S(2)}) collective-permute-start(bf16[2,8,1024]{2,1,0:T(8,128)(2,1)S(1)} %get-tuple-element.15), channel_id=1, source_target_pairs={{4,8},{8,4},{12,16},{16,12},{20,24},{24,20},{5,9},{9,5},{13,17},{1... | collective-permute-start | bytes 98312 | tf_op jit(solution)/shard_map/ppermute | solution.py:20
  10.5 3.0 %collective-permute-start.3 = (bf16[2,8,1024]{2,1,0:T(8,128)(2,1)S(1)}, bf16[2,8,1024]{2,1,0:T(8,128)(2,1)S(1)}, u32[]{:S(2)}, u32[]{:S(2)}) collective-permute-start(bf16[2,8,1024]{2,1,0:T(8,128)(2,1)S(1)} %get-tuple-element.16), channel_id=1, source_target_pairs={{0,4},{4,0},{8,12},{12,8},{16,20},{20,16},{24,28},{28,24},{1,5},{5... | collective-permute-start | bytes 98312 | tf_op jit(solution)/shard_map/ppermute | solution.py:20
  13.5 0.8 %copy.6.p2m_ref = bf16[64,56]{1,0:T(8,128)(2,1)S(1)} copy(bf16[64,56]{0,1:T(8,128)(2,1)} %param.6) | data formatting | bytes 14336 | tf_op args[1]
  14.3 0.0 copy-start
  14.3 2.4 %copy-done = bf16[7,7,7,56,56]{4,3,2,1,0:T(8,128)(2,1)S(1)} copy-done((bf16[7,7,7,56,56]{4,3,2,1,0:T(8,128)(2,1)S(1)}, bf16[7,7,7,56,56]{4,3,2,1,0:T(8,128)(2,1)}, u32[]{:S(2)}) %copy-start) | copy-done | bytes 2151320
  16.7 0.0 copy-start.1
  16.7 1.0 %copy-done.1 = bf16[3,3,3,64,64]{4,3,2,1,0:T(8,128)(2,1)S(1)} copy-done((bf16[3,3,3,64,64]{4,3,2,1,0:T(8,128)(2,1)S(1)}, bf16[3,3,3,64,64]{4,3,2,1,0:T(8,128)(2,1)}, u32[]{:S(2)}) %copy-start.1) | copy-done | bytes 221208
  17.7 0.0 copy-start.2
  17.7 0.7 %copy-done.2 = bf16[56,64]{1,0:T(8,128)(2,1)S(1)} copy-done((bf16[56,64]{1,0:T(8,128)(2,1)S(1)}, bf16[56,64]{1,0:T(8,128)(2,1)}, u32[]{:S(2)}) %copy-start.2) | copy-done | bytes 7192
  18.4 1.4 %pack.1 = (bf16[7,7,6,64,128]{4,3,2,1,0:T(8,128)(2,1)S(1)}, bf16[3,5,2,128,128]{4,3,2,1,0:T(8,128)(2,1)S(1)}, bf16[128,128]{1,0:T(8,128)(2,1)S(1)}, bf16[256,256]{1,0:T(8,128)(2,1)S(1)}) custom-call(bf16[64,56]{1,0:T(8,128)(2,1)S(1)} %copy.6.p2m_ref, bf16[7,7,7,56,56]{4,3,2,1,0:T(8,128)(2,1)S(1)} %copy-done, bf16[3,3,3,64,64]{4,3,2,1,0:T(8,128)(2,1)S(1)} %copy-done.1, ...), custom_call_target="tpu_custom_call" | custom-call | flops 4000000 | bytes 10000000 | tf_op jit(solution)/shard_map/pack/pallas_call | solution.py:112
  19.8 0.0 collective-permute-done.2
  19.8 0.0 collective-permute-done.3
  19.8 0.0 copy-done.3
  19.8 0.1 pad_maximum_fusion.cells_ref
  19.9 3.1 %main.1 = f32[4,4,1024]{2,1,0:T(4,128)} custom-call(bf16[8,8,1024]{2,1,0:T(8,128)(2,1)S(1)} %pad_maximum_fusion.cells_ref, bf16[7,7,6,64,128]{4,3,2,1,0:T(8,128)(2,1)S(1)} %get-tuple-element.9.far_ref, bf16[3,5,2,128,128]{4,3,2,1,0:T(8,128)(2,1)S(1)} %get-tuple-element.10.near_ref, bf16[128,128]{1,0:T(8,128)(2,1)S(1)} %get-tuple-element.11.p2m_ref, ...), custom_call_target="tpu_custom_call" | custom-call | flops 600000000 | bytes 10000000 | tf_op jit(solution)/shard_map/main/pallas_call | solution.py:202
  (2 shorter events, 0.0 us)
Async XLA Ops:
  0.0 19.8 %copy-start.3 = (bf16[4,4,1024]{2,1,0:T(4,128)(2,1)S(1)}, bf16[4,4,1024]{2,1,0:T(4,128)(2,1)}, u32[]{:S(2)}) copy-start(bf16[4,4,1024]{2,1,0:T(4,128)(2,1)} %param.5) | copy-start | bytes 98308
  0.0 6.5 %collective-permute-start = (bf16[4,4,1024]{2,1,0:T(4,128)(2,1)}, bf16[4,4,1024]{2,1,0:T(4,128)(2,1)S(1)}, u32[]{:S(2)}, u32[]{:S(2)}) collective-permute-start(bf16[4,4,1024]{2,1,0:T(4,128)(2,1)} %param.5), channel_id=1, source_target_pairs={{1,2},{2,1},{5,6},{6,5},{9,10},{10,9},{13,14},{14,13},{17,18},{18,... | collective-permute-start | bytes 98312 | tf_op jit(solution)/shard_map/ppermute | solution.py:20
  0.8 8.1 %collective-permute-start.1 = (bf16[4,4,1024]{2,1,0:T(4,128)(2,1)}, bf16[4,4,1024]{2,1,0:T(4,128)(2,1)S(1)}, u32[]{:S(2)}, u32[]{:S(2)}) collective-permute-start(bf16[4,4,1024]{2,1,0:T(4,128)(2,1)} %param.5), channel_id=1, source_target_pairs={{0,1},{1,0},{2,3},{3,2},{4,5},{5,4},{6,7},{7,6},{8,9},{9,8},{10,11... | collective-permute-start | bytes 98312 | tf_op jit(solution)/shard_map/ppermute | solution.py:20
  9.8 10.0 %collective-permute-start.2 = (bf16[2,8,1024]{2,1,0:T(8,128)(2,1)S(1)}, bf16[2,8,1024]{2,1,0:T(8,128)(2,1)S(1)}, u32[]{:S(2)}, u32[]{:S(2)}) collective-permute-start(bf16[2,8,1024]{2,1,0:T(8,128)(2,1)S(1)} %get-tuple-element.15), channel_id=1, source_target_pairs={{4,8},{8,4},{12,16},{16,12},{20,24},{24,20},{5,9},{9,5},{13,17},{1... | collective-permute-start | bytes 98312 | tf_op jit(solution)/shard_map/ppermute | solution.py:20
  10.5 9.3 %collective-permute-start.3 = (bf16[2,8,1024]{2,1,0:T(8,128)(2,1)S(1)}, bf16[2,8,1024]{2,1,0:T(8,128)(2,1)S(1)}, u32[]{:S(2)}, u32[]{:S(2)}) collective-permute-start(bf16[2,8,1024]{2,1,0:T(8,128)(2,1)S(1)} %get-tuple-element.16), channel_id=1, source_target_pairs={{0,4},{4,0},{8,12},{12,8},{16,20},{20,16},{24,28},{28,24},{1,5},{5... | collective-permute-start | bytes 98312 | tf_op jit(solution)/shard_map/ppermute | solution.py:20
  14.3 2.4 %copy-start = (bf16[7,7,7,56,56]{4,3,2,1,0:T(8,128)(2,1)S(1)}, bf16[7,7,7,56,56]{4,3,2,1,0:T(8,128)(2,1)}, u32[]{:S(2)}) copy-start(bf16[7,7,7,56,56]{4,3,2,1,0:T(8,128)(2,1)} %m2l_ref.1) | copy-start | bytes 6453892
  16.7 1.0 %copy-start.1 = (bf16[3,3,3,64,64]{4,3,2,1,0:T(8,128)(2,1)S(1)}, bf16[3,3,3,64,64]{4,3,2,1,0:T(8,128)(2,1)}, u32[]{:S(2)}) copy-start(bf16[3,3,3,64,64]{4,3,2,1,0:T(8,128)(2,1)} %near_ref.1) | copy-start | bytes 663556
  17.7 0.7 %copy-start.2 = (bf16[56,64]{1,0:T(8,128)(2,1)S(1)}, bf16[56,64]{1,0:T(8,128)(2,1)}, u32[]{:S(2)}) copy-start(bf16[56,64]{1,0:T(8,128)(2,1)} %l2p_ref.1) | copy-start | bytes 21508

commit v2 on v1

v2 whole, which is shorter than its diff:
```python
import jax
import jax.numpy as jnp
from jax import lax
from jax.experimental import pallas as pl
from jax.experimental.pallas import tpu as pltpu
from jax.sharding import PartitionSpec as P

BF16 = jnp.bfloat16
F32 = jnp.float32
WIDTH = 64
PAIR = 2 * WIDTH
VMEM_LIMIT = 40 * 1024 * 1024


def swapped(cells, axis, odd):
    count = lax.axis_size(axis)
    pairs = []
    for i in range(odd, count - 1, 2):
        pairs += [(i, i + 1), (i + 1, i)]
    return lax.ppermute(cells, axis, pairs)


def exchanged(cells, axis, dim):
    parity = lax.axis_index(axis) % 2
    size = cells.shape[dim]
    odd = swapped(cells, axis, 1)
    even = swapped(cells, axis, 0)

    def head(part):
        return lax.slice_in_dim(part, 0, 2, axis=dim)

    def tail(part):
        return lax.slice_in_dim(part, size - 2, size, axis=dim)

    low = jnp.where(parity == 0, tail(odd), tail(even))
    high = jnp.where(parity == 0, head(even), head(odd))
    return low, high


def sent(cells, axis, dim):
    parity = lax.axis_index(axis) % 2
    size = cells.shape[dim]
    head = lax.slice_in_dim(cells, 0, 2, axis=dim)
    tail = lax.slice_in_dim(cells, size - 2, size, axis=dim)
    even = swapped(jnp.where(parity == 0, tail, head), axis, 0)
    odd = swapped(jnp.where(parity == 0, head, tail), axis, 1)
    low = jnp.where(parity == 0, odd, even)
    high = jnp.where(parity == 0, even, odd)
    return low, high


def widened(low, own, high):
    wide = jnp.concatenate([low, own, high], axis=1)
    low, high = sent(wide, "gx", 0)
    return jnp.concatenate([low, wide, high], axis=0)


def square(block):
    rows, columns = block.shape
    if columns < WIDTH:
        block = jnp.concatenate([block, jnp.zeros((rows, WIDTH - columns), BF16)], axis=1)
    if rows < WIDTH:
        block = jnp.concatenate([block, jnp.zeros((WIDTH - rows, WIDTH), BF16)], axis=0)
    return block


def pack_kernel(
    own_hbm, p2m_hbm, m2l_hbm, near_hbm, l2p_hbm,
    own_out, far_out, near_out, p2m_out, l2p_out,
    p2m_ref, m2l_ref, near_ref, l2p_ref, sems,
):
    copies = [
        pltpu.make_async_copy(m2l_hbm.at[offset_x], m2l_ref.at[offset_x], sems.at[offset_x])
        for offset_x in range(7)
    ]
    pieces = ((near_hbm, near_ref), (p2m_hbm, p2m_ref), (l2p_hbm, l2p_ref), (own_hbm, own_out))
    for index, (source, target) in enumerate(pieces):
        copies.append(pltpu.make_async_copy(source, target, sems.at[7 + index]))
    for copy in copies:
        copy.start()
    blank = jnp.zeros((WIDTH, WIDTH), BF16)

    def far_blocks(offset_x, offset_y):
        inner = 2 <= offset_x <= 4 and 2 <= offset_y <= 4
        entries = []
        for offset_z in range(7):
            if inner and 2 <= offset_z <= 4:
                entries.append(blank)
            else:
                entries.append(square(m2l_ref[offset_x, offset_y, offset_z]))
        for s in range(6):
            far_out[offset_x, offset_y, s] = jnp.concatenate([entries[s + 1], entries[s]], axis=1)

    for offset_x in range(7):
        copies[offset_x].wait()
        for offset_y in range(7):
            far_blocks(offset_x, offset_y)
    for copy in copies[7:]:
        copy.wait()
    for offset_x in range(3):
        for offset_y in range(3):
            before, same, after = [near_ref[offset_x, offset_y, z] for z in range(3)]
            upper = jnp.concatenate([same, before], axis=1)
            lower = jnp.concatenate([after, same], axis=1)
            near_out[offset_x, offset_y, 0] = jnp.concatenate([upper, lower], axis=0)
            upper = jnp.concatenate([blank, after], axis=1)
            lower = jnp.concatenate([before, blank], axis=1)
            near_out[offset_x, offset_y, 1] = jnp.concatenate([upper, lower], axis=0)
    p2m = square(p2m_ref[...])
    p2m_out[...] = jnp.concatenate(
        [jnp.concatenate([p2m, blank], axis=1), jnp.concatenate([blank, p2m], axis=1)], axis=0
    )
    l2p = square(l2p_ref[...])
    l2p_out[...] = jnp.concatenate(
        [jnp.concatenate([l2p, blank], axis=1), jnp.concatenate([blank, l2p], axis=1)], axis=0
    )


def packed(density, p2m_operator, m2l_table, near_table, l2p_operator):
    shapes = [density.shape, (7, 7, 6, WIDTH, PAIR), (3, 3, 2, PAIR, PAIR), (PAIR, PAIR), (PAIR, PAIR)]
    return pl.pallas_call(
        pack_kernel,
        out_shape=[pltpu.VMEM(shape, BF16) for shape in shapes],
        in_specs=[pl.BlockSpec(memory_space=pltpu.HBM)] * 5,
        out_specs=[pl.BlockSpec(memory_space=pltpu.VMEM)] * 5,
        scratch_shapes=[
            pltpu.VMEM(p2m_operator.shape[::-1], BF16),
            pltpu.VMEM(m2l_table.shape, BF16),
            pltpu.VMEM(near_table.shape, BF16),
            pltpu.VMEM(l2p_operator.shape, BF16),
            pltpu.SemaphoreType.DMA((11,)),
        ],
        compiler_params=pltpu.CompilerParams(vmem_limit_bytes=VMEM_LIMIT),
        cost_estimate=pl.CostEstimate(flops=4000000, bytes_accessed=10000000, transcendentals=0),
        name="pack",
    )(
        *(
            pltpu.with_memory_space_constraint(array, pltpu.HBM)
            for array in (density, p2m_operator.T, m2l_table, near_table, l2p_operator)
        )
    )


def shifted(rows):
    place = lax.broadcasted_iota(jnp.int32, rows.shape, 0) % 8
    before = jnp.where(place == 0, 0.0, jnp.roll(rows, 1, axis=0))
    after = jnp.where(place == 7, 0.0, jnp.roll(rows, -1, axis=0))
    return before, rows, after


def parity_window(slabs, offset, size):
    first = offset - 1
    if 0 <= first <= 4:
        return slabs[size * first : size * first + 4 * size]
    blank = jnp.zeros((size, slabs.shape[1]), slabs.dtype)
    if first < 0:
        parts = [blank, slabs[0:size], blank, slabs[2 * size : 3 * size]]
    else:
        parts = [slabs[5 * size : 6 * size], blank, slabs[7 * size : 8 * size], blank]
    return jnp.concatenate(parts, axis=0)


def main_kernel(cells_ref, far_ref, near_ref, p2m_ref, l2p_ref, out_ref, rows_ref, out_rows, far_rows, near_rows):
    pairs = cells_ref.shape[2] // PAIR
    for x in range(8):
        for pair in range(pairs):
            rows_ref[pl.ds(x * pairs + pair, 8, stride=8 * pairs), :] = cells_ref[
                x, :, pair * PAIR : (pair + 1) * PAIR
            ].astype(F32)
    cells = rows_ref[...]
    multipole = lax.dot_general(
        cells.astype(BF16), p2m_ref[...], (((1,), (1,)), ((), ())), preferred_element_type=F32
    )
    multipole = multipole.astype(BF16).astype(F32)
    sources = shifted(multipole)
    for offset_x in range(7):
        for b in range(3):
            for y in range(8):
                far_rows[offset_x, b, 32 * y : 32 * y + 32] = parity_window(
                    sources[b][64 * y : 64 * y + 64], offset_x, 8
                ).astype(BF16)
    before, same, after = shifted(cells)
    lane = lax.broadcasted_iota(jnp.int32, cells.shape, 1)
    beside = jnp.where(lane < WIDTH, after, before)
    for offset_x in range(3):
        for k, kind in enumerate((same, beside)):
            for y in range(1, 7):
                near_rows[offset_x, k, 32 * (y - 1) : 32 * y] = kind[
                    64 * y + 8 * (offset_x + 1) : 64 * y + 8 * (offset_x + 5)
                ].astype(BF16)
    far = jnp.zeros((128, PAIR), F32)
    for offset_x in range(7):
        chunks, weights = [], []
        for offset_y in range(7):
            inner = 2 <= offset_x <= 4 and 2 <= offset_y <= 4
            for b in range(3):
                if inner and b == 1:
                    continue
                chunks.append(parity_window(far_rows[offset_x, b], offset_y, 32))
                weights.append(far_ref[offset_x, offset_y, 2 * b : 2 * b + 2].reshape(PAIR, PAIR))
        far += jnp.dot(
            jnp.concatenate(chunks, axis=1), jnp.concatenate(weights, axis=0), preferred_element_type=F32
        )
    total = jnp.dot(far.astype(BF16), l2p_ref[...], preferred_element_type=F32)
    for offset_x in range(3):
        chunks = []
        for offset_y in range(3):
            for k in range(2):
                chunks.append(near_rows[offset_x, k, 32 * offset_y : 32 * offset_y + 128])
        total += jnp.dot(
            jnp.concatenate(chunks, axis=1),
            near_ref[offset_x].reshape(6 * PAIR, PAIR),
            preferred_element_type=F32,
        )
    out_rows[...] = total
    for x in range(4):
        for pair in range(pairs):
            out_ref[x, :, pair * PAIR : (pair + 1) * PAIR] = out_rows[
                pl.ds(x * pairs + pair, 4, stride=4 * pairs), :
            ]


def local(density, p2m_operator, m2l_table, near_table, l2p_operator):
    low, high = exchanged(density, "gy", 1)
    own, *tables = packed(density, p2m_operator, m2l_table, near_table, l2p_operator)
    cells = widened(low, own, high)
    return pl.pallas_call(
        main_kernel,
        out_shape=jax.ShapeDtypeStruct(density.shape, F32),
        in_specs=[pl.BlockSpec(memory_space=pltpu.VMEM)] * 5,
        out_specs=pl.BlockSpec(memory_space=pltpu.VMEM),
        scratch_shapes=[
            pltpu.VMEM((512, PAIR), F32),
            pltpu.VMEM((128, PAIR), F32),
            pltpu.VMEM((7, 3, 256, PAIR), BF16),
            pltpu.VMEM((3, 2, 192, PAIR), BF16),
        ],
        compiler_params=pltpu.CompilerParams(vmem_limit_bytes=VMEM_LIMIT),
        cost_estimate=pl.CostEstimate(flops=600000000, bytes_accessed=10000000, transcendentals=0),
        name="main",
    )(cells, *tables)


def solution(mesh):
    placed = (P("gx", "gy", None), P(), P(), P(), P())
    return jax.shard_map(
        local, mesh=mesh, in_specs=placed, out_specs=P("gx", "gy", None), check_vma=False
    )
```

time: 23.5 us -> 17.2 us (0.73)
  the two profiles are of different devices: /device:TPU:0 before, /device:TPU:1 now
where the time goes in v2:
time: 17.2 us; the launch traced here: 17 us
  starting transfers between devices  9.61 us (56%)
  Pallas kernels  5.64 us (33%)
  waiting for transfers between devices  1.51 us (9%)
  other arithmetic  0.2 us (1%)
    ppermute x4, starting transfers between devices, swapped(): return lax.ppermute(cells, axis, pairs)  9.61 us
    pallas_call x1, Pallas kernels, packed(): pl.pallas_call(pack_kernel, out_shape=[pltpu.VMEM(shape, BF16) for shape...  3.01 us
    pallas_call x1, Pallas kernels, local(): pl.pallas_call(main_kernel, out_shape=jax.ShapeDtypeStruct(density.shape,...  2.63 us
    ppermute x4, waiting for transfers between devices, swapped(): return lax.ppermute(cells, axis, pairs)  1.51 us
  transfers between devices with their start and end apart: 4, of which 1 were waited for; matrix products, arithmetic and copies ran while one was open for 0% of the time, Pallas kernels for 18%

profile of v2, /device:TPU:1, one launch (start us, length us, event | category | flops | bytes accessed | tf_op | source)
XLA Modules:
  0.0 17.0 jit_solution(3009418630752414750)
XLA Ops:
  0.0 0.7 %collective-permute-start = (bf16[4,4,1024]{2,1,0:T(4,128)(2,1)}, bf16[4,4,1024]{2,1,0:T(4,128)(2,1)S(1)}, u32[]{:S(2)}, u32[]{:S(2)}) collective-permute-start(bf16[4,4,1024]{2,1,0:T(4,128)(2,1)} %own_hbm.1), channel_id=1, source_target_pairs={{1,2},{2,1},{5,6},{6,5},{9,10},{10,9},{13,14},{14,13},{17,18},{18,... | collective-permute-start | bytes 98312 | tf_op jit(solution)/shard_map/ppermute | solution.py:20
  0.7 4.6 %collective-permute-start.1 = (bf16[4,4,1024]{2,1,0:T(4,128)(2,1)}, bf16[4,4,1024]{2,1,0:T(4,128)(2,1)S(1)}, u32[]{:S(2)}, u32[]{:S(2)}) collective-permute-start(bf16[4,4,1024]{2,1,0:T(4,128)(2,1)} %own_hbm.1), channel_id=1, source_target_pairs={{0,1},{1,0},{2,3},{3,2},{4,5},{5,4},{6,7},{7,6},{8,9},{9,8},{10,11... | collective-permute-start | bytes 98312 | tf_op jit(solution)/shard_map/ppermute | solution.py:20
  5.2 3.0 %pack.1 = (bf16[4,4,1024]{2,1,0:T(4,128)(2,1)S(1)}, bf16[7,7,6,64,128]{4,3,2,1,0:T(8,128)(2,1)S(1)}, bf16[3,3,2,128,128]{4,3,2,1,0:T(8,128)(2,1)S(1)}, bf16[128,128]{1,0:T(8,128)(2,1)S(1)}, bf16[128,128]{1,0:T(8,128)(2,1)S(1)}) custom-call(bf16[4,4,1024]{2,1,0:T(4,128)(2,1)} %own_hbm.1, bf16[56,64]{1,0:T(8,128)(2,1)} %bitcast.1, ...), custom_call_target="tpu_custom_call" | custom-call | flops 4000000 | bytes 10000000 | tf_op jit(solution)/shard_map/pack/pallas_call | solution.py:121
  8.2 0.0 collective-permute-done
  8.3 0.0 collective-permute-done.1
  8.3 0.1 broadcast_select_fusion.1
  8.3 0.1 pad_maximum_fusion.1
  8.4 4.3 %collective-permute-start.2 = (bf16[2,8,1024]{2,1,0:T(8,128)(2,1)S(1)}, bf16[2,8,1024]{2,1,0:T(8,128)(2,1)S(1)}, u32[]{:S(2)}, u32[]{:S(2)}) collective-permute-start(bf16[2,8,1024]{2,1,0:T(8,128)(2,1)S(1)} %get-tuple-element.17), channel_id=1, source_target_pairs={{4,8},{8,4},{12,16},{16,12},{20,24},{24,20},{5,9},{9,5},{13,17},{1... | collective-permute-start | bytes 98312 | tf_op jit(solution)/shard_map/ppermute | solution.py:20
  12.7 0.1 collective-permute-start.3
  12.8 1.5 %collective-permute-done.2 = bf16[2,8,1024]{2,1,0:T(8,128)(2,1)S(1)} collective-permute-done((bf16[2,8,1024]{2,1,0:T(8,128)(2,1)S(1)}, bf16[2,8,1024]{2,1,0:T(8,128)(2,1)S(1)}, u32[]{:S(2)}, u32[]{:S(2)}) %collective-permute-start.2) | collective-permute-done | bytes 32800 | tf_op jit(solution)/shard_map/ppermute | solution.py:20
  14.3 0.0 collective-permute-done.3
  14.3 0.1 pad_maximum_fusion.cells_ref
  14.4 2.6 %main.1 = f32[4,4,1024]{2,1,0:T(4,128)} custom-call(bf16[8,8,1024]{2,1,0:T(8,128)(2,1)S(1)} %pad_maximum_fusion.cells_ref, bf16[7,7,6,64,128]{4,3,2,1,0:T(8,128)(2,1)S(1)} %get-tuple-element.11.far_ref, bf16[3,3,2,128,128]{4,3,2,1,0:T(8,128)(2,1)S(1)} %get-tuple-element.12.near_ref, bf16[128,128]{1,0:T(8,128)(2,1)S(1)} %get-tuple-element.13.p2m_ref, ...), custom_call_target="tpu_custom_call" | custom-call | flops 600000000 | bytes 10000000 | tf_op jit(solution)/shard_map/main/pallas_call | solution.py:227
  (2 shorter events, 0.0 us)
Async XLA Ops:
  0.0 8.2 %collective-permute-start = (bf16[4,4,1024]{2,1,0:T(4,128)(2,1)}, bf16[4,4,1024]{2,1,0:T(4,128)(2,1)S(1)}, u32[]{:S(2)}, u32[]{:S(2)}) collective-permute-start(bf16[4,4,1024]{2,1,0:T(4,128)(2,1)} %own_hbm.1), channel_id=1, source_target_pairs={{1,2},{2,1},{5,6},{6,5},{9,10},{10,9},{13,14},{14,13},{17,18},{18,... | collective-permute-start | bytes 98312 | tf_op jit(solution)/shard_map/ppermute | solution.py:20
  0.7 7.6 %collective-permute-start.1 = (bf16[4,4,1024]{2,1,0:T(4,128)(2,1)}, bf16[4,4,1024]{2,1,0:T(4,128)(2,1)S(1)}, u32[]{:S(2)}, u32[]{:S(2)}) collective-permute-start(bf16[4,4,1024]{2,1,0:T(4,128)(2,1)} %own_hbm.1), channel_id=1, source_target_pairs={{0,1},{1,0},{2,3},{3,2},{4,5},{5,4},{6,7},{7,6},{8,9},{9,8},{10,11... | collective-permute-start | bytes 98312 | tf_op jit(solution)/shard_map/ppermute | solution.py:20
  8.4 5.9 %collective-permute-start.2 = (bf16[2,8,1024]{2,1,0:T(8,128)(2,1)S(1)}, bf16[2,8,1024]{2,1,0:T(8,128)(2,1)S(1)}, u32[]{:S(2)}, u32[]{:S(2)}) collective-permute-start(bf16[2,8,1024]{2,1,0:T(8,128)(2,1)S(1)} %get-tuple-element.17), channel_id=1, source_target_pairs={{4,8},{8,4},{12,16},{16,12},{20,24},{24,20},{5,9},{9,5},{13,17},{1... | collective-permute-start | bytes 98312 | tf_op jit(solution)/shard_map/ppermute | solution.py:20
  12.7 1.6 %collective-permute-start.3 = (bf16[2,8,1024]{2,1,0:T(8,128)(2,1)S(1)}, bf16[2,8,1024]{2,1,0:T(8,128)(2,1)S(1)}, u32[]{:S(2)}, u32[]{:S(2)}) collective-permute-start(bf16[2,8,1024]{2,1,0:T(8,128)(2,1)S(1)} %get-tuple-element.18), channel_id=1, source_target_pairs={{0,4},{4,0},{8,12},{12,8},{16,20},{20,16},{24,28},{28,24},{1,5},{5... | collective-permute-start | bytes 98312 | tf_op jit(solution)/shard_map/ppermute | solution.py:20

commit v3 on v2

--- a/solution.py
+++ b/solution.py
@@ -12,16 +12,35 @@
 VMEM_LIMIT = 40 * 1024 * 1024
 
 
+AXES = ("gx", "gy")
+
+
 def swapped(cells, axis, odd):
-    count = lax.axis_size(axis)
+    sizes = [lax.axis_size(name) for name in AXES]
+    dim = AXES.index(axis)
     pairs = []
-    for i in range(odd, count - 1, 2):
-        pairs += [(i, i + 1), (i + 1, i)]
-    return lax.ppermute(cells, axis, pairs)
+    for place in range(sizes[0] * sizes[1]):
+        at = list(divmod(place, sizes[1]))
+        partner = (at[dim] - odd) ^ 1
+        if at[dim] >= odd and partner + odd < sizes[dim]:
+            at[dim] = partner + odd
+        elif (at[1 - dim] ^ 1) < sizes[1 - dim]:
+            at[1 - dim] ^= 1
+        else:
+            continue
+        pairs.append((place, at[0] * sizes[1] + at[1]))
+    return lax.ppermute(cells, AXES, pairs)
+
+
+def chosen(axis, even_low, odd_low, even_high, odd_high):
+    place = lax.axis_index(axis)
+    lower = place % 2 == 0
+    low = jnp.where(place == 0, 0, jnp.where(lower, odd_low, even_low))
+    high = jnp.where(place == lax.axis_size(axis) - 1, 0, jnp.where(lower, even_high, odd_high))
+    return low.astype(BF16), high.astype(BF16)
 
 
 def exchanged(cells, axis, dim):
-    parity = lax.axis_index(axis) % 2
     size = cells.shape[dim]
     odd = swapped(cells, axis, 1)
     even = swapped(cells, axis, 0)
@@ -32,27 +51,17 @@
     def tail(part):
         return lax.slice_in_dim(part, size - 2, size, axis=dim)
 
-    low = jnp.where(parity == 0, tail(odd), tail(even))
-    high = jnp.where(parity == 0, head(even), head(odd))
-    return low, high
-
-
-def sent(cells, axis, dim):
-    parity = lax.axis_index(axis) % 2
+    return chosen(axis, tail(even), tail(odd), head(even), head(odd))
+
+
+def traded(cells, axis, dim):
+    lower = lax.axis_index(axis) % 2 == 0
     size = cells.shape[dim]
     head = lax.slice_in_dim(cells, 0, 2, axis=dim)
     tail = lax.slice_in_dim(cells, size - 2, size, axis=dim)
-    even = swapped(jnp.where(parity == 0, tail, head), axis, 0)
-    odd = swapped(jnp.where(parity == 0, head, tail), axis, 1)
-    low = jnp.where(parity == 0, odd, even)
-    high = jnp.where(parity == 0, even, odd)
-    return low, high
-
-
-def widened(low, own, high):
-    wide = jnp.concatenate([low, own, high], axis=1)
-    low, high = sent(wide, "gx", 0)
-    return jnp.concatenate([low, wide, high], axis=0)
+    even = swapped(jnp.where(lower, tail, head), axis, 0)
+    odd = swapped(jnp.where(lower, head, tail), axis, 1)
+    return even, odd
 
 
 def square(block):
@@ -160,13 +169,27 @@
     return jnp.concatenate(parts, axis=0)
 
 
-def main_kernel(cells_ref, far_ref, near_ref, p2m_ref, l2p_ref, out_ref, rows_ref, out_rows, far_rows, near_rows):
-    pairs = cells_ref.shape[2] // PAIR
+def main_kernel(
+    own_ref, even_ref, odd_ref, far_ref, near_ref, p2m_ref, l2p_ref,
+    out_ref, rows_ref, out_rows, far_rows, near_rows,
+):
+    pairs = own_ref.shape[2] // PAIR
+    place = lax.axis_index("gx")
+    lower = lax.rem(place, 2) == 0
     for x in range(8):
         for pair in range(pairs):
-            rows_ref[pl.ds(x * pairs + pair, 8, stride=8 * pairs), :] = cells_ref[
-                x, :, pair * PAIR : (pair + 1) * PAIR
-            ].astype(F32)
+            lanes = slice(pair * PAIR, (pair + 1) * PAIR)
+            if 2 <= x < 6:
+                cells = own_ref[x - 2, :, lanes].astype(F32)
+            else:
+                even = even_ref[x % 2, :, lanes].astype(F32)
+                odd = odd_ref[x % 2, :, lanes].astype(F32)
+                if x < 2:
+                    cells = jnp.where(place == 0, 0.0, jnp.where(lower, odd, even))
+                else:
+                    last = place == lax.axis_size("gx") - 1
+                    cells = jnp.where(last, 0.0, jnp.where(lower, even, odd))
+            rows_ref[pl.ds(x * pairs + pair, 8, stride=8 * pairs), :] = cells
     cells = rows_ref[...]
     multipole = lax.dot_general(
         cells.astype(BF16), p2m_ref[...], (((1,), (1,)), ((), ())), preferred_element_type=F32
@@ -223,11 +246,12 @@
 def local(density, p2m_operator, m2l_table, near_table, l2p_operator):
     low, high = exchanged(density, "gy", 1)
     own, *tables = packed(density, p2m_operator, m2l_table, near_table, l2p_operator)
-    cells = widened(low, own, high)
+    wide = jnp.concatenate([low, own, high], axis=1)
+    even, odd = traded(wide, "gx", 0)
     return pl.pallas_call(
         main_kernel,
         out_shape=jax.ShapeDtypeStruct(density.shape, F32),
-        in_specs=[pl.BlockSpec(memory_space=pltpu.VMEM)] * 5,
+        in_specs=[pl.BlockSpec(memory_space=pltpu.VMEM)] * 7,
         out_specs=pl.BlockSpec(memory_space=pltpu.VMEM),
         scratch_shapes=[
             pltpu.VMEM((512, PAIR), F32),
@@ -238,7 +262,7 @@
         compiler_params=pltpu.CompilerParams(vmem_limit_bytes=VMEM_LIMIT),
         cost_estimate=pl.CostEstimate(flops=600000000, bytes_accessed=10000000, transcendentals=0),
         name="main",
-    )(cells, *tables)
+    )(wide, even, odd, *tables)
 
 
 def solution(mesh):

time: 17.2 us -> 14.4 us (0.84)
  the two profiles are of different devices: /device:TPU:1 before, /device:TPU:0 now
where the time goes in v3:
time: 14.4 us; the launch traced here: 14.2 us
  starting transfers between devices  6.19 us (43%)
  Pallas kernels  5.64 us (39%)
  waiting for transfers between devices  2.23 us (15%)
    ppermute x4, starting transfers between devices, swapped(): return lax.ppermute(cells, AXES, pairs)  6.19 us
    pallas_call x1, Pallas kernels, packed(): pl.pallas_call(pack_kernel, out_shape=[pltpu.VMEM(shape, BF16) for shape...  3.01 us
    pallas_call x1, Pallas kernels, local(): pl.pallas_call(main_kernel, out_shape=jax.ShapeDtypeStruct(density.shape,...  2.62 us
    ppermute x4, waiting for transfers between devices, swapped(): return lax.ppermute(cells, AXES, pairs)  2.23 us
  transfers between devices with their start and end apart: 4, of which 1 were waited for; matrix products, arithmetic and copies ran while one was open for 0% of the time, Pallas kernels for 21%

profile of v3, /device:TPU:0, one launch (start us, length us, event | category | flops | bytes accessed | tf_op | source)
XLA Modules:
  0.0 14.2 jit_solution(9974597605423069946)
XLA Ops:
  0.0 0.5 %collective-permute-start = (bf16[4,4,1024]{2,1,0:T(4,128)(2,1)}, bf16[4,4,1024]{2,1,0:T(4,128)(2,1)S(1)}, u32[]{:S(2)}, u32[]{:S(2)}) collective-permute-start(bf16[4,4,1024]{2,1,0:T(4,128)(2,1)} %own_hbm.1), channel_id=1, source_target_pairs={{0,4},{1,2},{2,1},{3,7},{4,0},{5,6},{6,5},{7,3},{8,12},{9,10},{10,... | collective-permute-start | bytes 98312 | tf_op jit(solution)/shard_map/ppermute | solution.py:32
  0.5 4.0 %collective-permute-start.1 = (bf16[4,4,1024]{2,1,0:T(4,128)(2,1)}, bf16[4,4,1024]{2,1,0:T(4,128)(2,1)S(1)}, u32[]{:S(2)}, u32[]{:S(2)}) collective-permute-start(bf16[4,4,1024]{2,1,0:T(4,128)(2,1)} %own_hbm.1), channel_id=1, source_target_pairs={{0,1},{1,0},{2,3},{3,2},{4,5},{5,4},{6,7},{7,6},{8,9},{9,8},{10,11... | collective-permute-start | bytes 98312 | tf_op jit(solution)/shard_map/ppermute | solution.py:32
  4.4 3.0 %pack.1 = (bf16[4,4,1024]{2,1,0:T(4,128)(2,1)S(1)}, bf16[7,7,6,64,128]{4,3,2,1,0:T(8,128)(2,1)S(1)}, bf16[3,3,2,128,128]{4,3,2,1,0:T(8,128)(2,1)S(1)}, bf16[128,128]{1,0:T(8,128)(2,1)S(1)}, bf16[128,128]{1,0:T(8,128)(2,1)S(1)}) custom-call(bf16[4,4,1024]{2,1,0:T(4,128)(2,1)} %own_hbm.1, bf16[56,64]{1,0:T(8,128)(2,1)} %bitcast.1, ...), custom_call_target="tpu_custom_call" | custom-call | flops 4000000 | bytes 10000000 | tf_op jit(solution)/shard_map/pack/pallas_call | solution.py:130
  7.4 0.0 collective-permute-done
  7.5 0.0 collective-permute-done.1
  7.5 0.1 broadcast_select_fusion.5
  7.5 0.1 pad_maximum_fusion.own_ref
  7.6 1.1 %collective-permute-start.3 = (bf16[2,8,1024]{2,1,0:T(8,128)(2,1)S(1)}, bf16[2,8,1024]{2,1,0:T(8,128)(2,1)S(1)}, u32[]{:S(2)}, u32[]{:S(2)}) collective-permute-start(bf16[2,8,1024]{2,1,0:T(8,128)(2,1)S(1)} %get-tuple-element.15), channel_id=1, source_target_pairs={{0,1},{1,0},{2,3},{3,2},{4,8},{5,9},{6,10},{7,11},{8,4},{9,5},{10,... | collective-permute-start | bytes 98312 | tf_op jit(solution)/shard_map/ppermute | solution.py:32
  8.8 0.6 %collective-permute-start.2 = (bf16[2,8,1024]{2,1,0:T(8,128)(2,1)S(1)}, bf16[2,8,1024]{2,1,0:T(8,128)(2,1)S(1)}, u32[]{:S(2)}, u32[]{:S(2)}) collective-permute-start(bf16[2,8,1024]{2,1,0:T(8,128)(2,1)S(1)} %get-tuple-element.16), channel_id=1, source_target_pairs={{0,4},{1,5},{2,6},{3,7},{4,0},{5,1},{6,2},{7,3},{8,12},{9,13},{10,... | collective-permute-start | bytes 98312 | tf_op jit(solution)/shard_map/ppermute | solution.py:32
  9.4 2.2 %collective-permute-done.3.odd_ref = bf16[2,8,1024]{2,1,0:T(8,128)(2,1)S(1)} collective-permute-done((bf16[2,8,1024]{2,1,0:T(8,128)(2,1)S(1)}, bf16[2,8,1024]{2,1,0:T(8,128)(2,1)S(1)}, u32[]{:S(2)}, u32[]{:S(2)}) %collective-permute-start.3) | collective-permute-done | bytes 32800 | tf_op jit(solution)/shard_map/ppermute | solution.py:32
  11.6 0.0 collective-permute-done.2.even_ref
  11.6 2.6 %main.1 = f32[4,4,1024]{2,1,0:T(4,128)} custom-call(bf16[4,8,1024]{2,1,0:T(8,128)(2,1)S(1)} %pad_maximum_fusion.own_ref, bf16[2,8,1024]{2,1,0:T(8,128)(2,1)S(1)} %collective-permute-done.2.even_ref, bf16[2,8,1024]{2,1,0:T(8,128)(2,1)S(1)} %collective-permute-done.3.odd_ref, bf16[7,7,6,64,128]{4,3,2,1,0:T(8,128)(2,1)S(1)} %get-tuple-element.11.far_ref, ...), custom_call_target="tpu_custom_call" | custom-call | flops 600000000 | bytes 10000000 | tf_op jit(solution)/shard_map/main/pallas_call | solution.py:251
  (1 shorter events, 0.0 us)
Async XLA Ops:
  0.0 7.5 %collective-permute-start = (bf16[4,4,1024]{2,1,0:T(4,128)(2,1)}, bf16[4,4,1024]{2,1,0:T(4,128)(2,1)S(1)}, u32[]{:S(2)}, u32[]{:S(2)}) collective-permute-start(bf16[4,4,1024]{2,1,0:T(4,128)(2,1)} %own_hbm.1), channel_id=1, source_target_pairs={{0,4},{1,2},{2,1},{3,7},{4,0},{5,6},{6,5},{7,3},{8,12},{9,10},{10,... | collective-permute-start | bytes 98312 | tf_op jit(solution)/shard_map/ppermute | solution.py:32
  0.5 7.0 %collective-permute-start.1 = (bf16[4,4,1024]{2,1,0:T(4,128)(2,1)}, bf16[4,4,1024]{2,1,0:T(4,128)(2,1)S(1)}, u32[]{:S(2)}, u32[]{:S(2)}) collective-permute-start(bf16[4,4,1024]{2,1,0:T(4,128)(2,1)} %own_hbm.1), channel_id=1, source_target_pairs={{0,1},{1,0},{2,3},{3,2},{4,5},{5,4},{6,7},{7,6},{8,9},{9,8},{10,11... | collective-permute-start | bytes 98312 | tf_op jit(solution)/shard_map/ppermute | solution.py:32
  7.6 4.0 %collective-permute-start.3 = (bf16[2,8,1024]{2,1,0:T(8,128)(2,1)S(1)}, bf16[2,8,1024]{2,1,0:T(8,128)(2,1)S(1)}, u32[]{:S(2)}, u32[]{:S(2)}) collective-permute-start(bf16[2,8,1024]{2,1,0:T(8,128)(2,1)S(1)} %get-tuple-element.15), channel_id=1, source_target_pairs={{0,1},{1,0},{2,3},{3,2},{4,8},{5,9},{6,10},{7,11},{8,4},{9,5},{10,... | collective-permute-start | bytes 98312 | tf_op jit(solution)/shard_map/ppermute | solution.py:32
  8.8 2.8 %collective-permute-start.2 = (bf16[2,8,1024]{2,1,0:T(8,128)(2,1)S(1)}, bf16[2,8,1024]{2,1,0:T(8,128)(2,1)S(1)}, u32[]{:S(2)}, u32[]{:S(2)}) collective-permute-start(bf16[2,8,1024]{2,1,0:T(8,128)(2,1)S(1)} %get-tuple-element.16), channel_id=1, source_target_pairs={{0,4},{1,5},{2,6},{3,7},{4,0},{5,1},{6,2},{7,3},{8,12},{9,13},{10,... | collective-permute-start | bytes 98312 | tf_op jit(solution)/shard_map/ppermute | solution.py:32

commit v4 on v3

v4 whole, which is shorter than its diff:
```python
import jax
import jax.numpy as jnp
from jax import lax
from jax.experimental import pallas as pl
from jax.experimental.pallas import tpu as pltpu
from jax.sharding import PartitionSpec as P

BF16 = jnp.bfloat16
F32 = jnp.float32
WIDTH = 64
PAIR = 2 * WIDTH
VMEM_LIMIT = 40 * 1024 * 1024
SMALL_LIMIT = 8 * 1024 * 1024


AXES = ("gx", "gy")


def swapped(cells, axis, odd):
    sizes = [lax.axis_size(name) for name in AXES]
    dim = AXES.index(axis)
    pairs = []
    for place in range(sizes[0] * sizes[1]):
        at = list(divmod(place, sizes[1]))
        partner = (at[dim] - odd) ^ 1
        if at[dim] >= odd and partner + odd < sizes[dim]:
            at[dim] = partner + odd
        elif (at[1 - dim] ^ 1) < sizes[1 - dim]:
            at[1 - dim] ^= 1
        else:
            continue
        pairs.append((place, at[0] * sizes[1] + at[1]))
    return lax.ppermute(cells, AXES, pairs)


def square(block):
    rows, columns = block.shape
    if columns < WIDTH:
        block = jnp.concatenate([block, jnp.zeros((rows, WIDTH - columns), BF16)], axis=1)
    if rows < WIDTH:
        block = jnp.concatenate([block, jnp.zeros((WIDTH - rows, WIDTH), BF16)], axis=0)
    return block


def first_kernel(out_ref):
    out_ref[...] = jnp.zeros_like(out_ref)


def first():
    return pl.pallas_call(
        first_kernel,
        out_shape=pltpu.VMEM((8, PAIR), F32),
        out_specs=pl.BlockSpec(memory_space=pltpu.VMEM),
        compiler_params=pltpu.CompilerParams(vmem_limit_bytes=1024 * 1024),
        cost_estimate=pl.CostEstimate(flops=10000000000, bytes_accessed=1000, transcendentals=0),
        name="first",
    )()


def pack_kernel(first_ref, p2m_ref, m2l_ref, near_ref, l2p_ref, far_out, near_out, p2m_out, l2p_out):
    blank = jnp.zeros((WIDTH, WIDTH), BF16)

    def far_blocks(offset_x, offset_y):
        inner = 2 <= offset_x <= 4 and 2 <= offset_y <= 4
        entries = []
        for offset_z in range(7):
            if inner and 2 <= offset_z <= 4:
                entries.append(blank)
            else:
                entries.append(square(m2l_ref[offset_x, offset_y, offset_z]))
        for s in range(6):
            far_out[offset_x, offset_y, s] = jnp.concatenate([entries[s + 1], entries[s]], axis=1)

    for offset_x in range(7):
        for offset_y in range(7):
            far_blocks(offset_x, offset_y)
    for offset_x in range(3):
        for offset_y in range(3):
            before, same, after = [near_ref[offset_x, offset_y, z] for z in range(3)]
            upper = jnp.concatenate([same, before], axis=1)
            lower = jnp.concatenate([after, same], axis=1)
            near_out[offset_x, offset_y, 0] = jnp.concatenate([upper, lower], axis=0)
            upper = jnp.concatenate([blank, after], axis=1)
            lower = jnp.concatenate([before, blank], axis=1)
            near_out[offset_x, offset_y, 1] = jnp.concatenate([upper, lower], axis=0)
    p2m = square(p2m_ref[...])
    p2m_out[...] = jnp.concatenate(
        [jnp.concatenate([p2m, blank], axis=1), jnp.concatenate([blank, p2m], axis=1)], axis=0
    )
    l2p = square(l2p_ref[...])
    l2p_out[...] = jnp.concatenate(
        [jnp.concatenate([l2p, blank], axis=1), jnp.concatenate([blank, l2p], axis=1)], axis=0
    )


def packed(start, p2m_operator, m2l_table, near_table, l2p_operator):
    shapes = [(7, 7, 6, WIDTH, PAIR), (3, 3, 2, PAIR, PAIR), (PAIR, PAIR), (PAIR, PAIR)]
    return pl.pallas_call(
        pack_kernel,
        out_shape=[pltpu.VMEM(shape, BF16) for shape in shapes],
        in_specs=[pl.BlockSpec(memory_space=pltpu.VMEM)] * 5,
        out_specs=[pl.BlockSpec(memory_space=pltpu.VMEM)] * 4,
        compiler_params=pltpu.CompilerParams(vmem_limit_bytes=VMEM_LIMIT),
        cost_estimate=pl.CostEstimate(flops=4000000, bytes_accessed=10000000, transcendentals=0),
        name="pack",
    )(start, p2m_operator.T, m2l_table, near_table, l2p_operator)


def from_neighbours(axis, even_low, odd_low, even_high, odd_high):
    place = lax.axis_index(axis)
    lower = lax.rem(place, 2) == 0
    low = jnp.where(place == 0, 0.0, jnp.where(lower, odd_low, even_low))
    last = place == lax.axis_size(axis) - 1
    high = jnp.where(last, 0.0, jnp.where(lower, even_high, odd_high))
    return low, high


def join_kernel(after_ref, own_ref, odd_ref, even_ref, own_out, odd_out, even_out, rows_ref):
    pairs = own_ref.shape[2] // PAIR
    for pair in range(pairs):
        lanes = slice(pair * PAIR, (pair + 1) * PAIR)

        def part(ref, x):
            return ref[x, :, lanes].astype(F32)

        for x in range(8):
            if 2 <= x < 6:
                cells = part(own_ref, x - 2)
            else:
                low, high = from_neighbours(
                    "gx",
                    *((part(even_ref, 2 + x), part(odd_ref, 2 + x)) if x < 2 else (0.0, 0.0)),
                    *((part(even_ref, x - 6), part(odd_ref, x - 6)) if x > 5 else (0.0, 0.0)),
                )
                cells = low if x < 2 else high
            rows_ref[pl.ds(x * pairs + pair, 4, stride=8 * pairs), :] = cells
    rows = rows_ref[...]
    own_out[...] = rows.astype(BF16)
    lower = lax.rem(lax.axis_index("gy"), 2) == 0
    head, tail = rows[:128], rows[128:]
    even_out[...] = jnp.where(lower, tail, head).astype(BF16)
    odd_out[...] = jnp.where(lower, head, tail).astype(BF16)


def joined(after, own, odd, even):
    return pl.pallas_call(
        join_kernel,
        out_shape=[pltpu.VMEM((rows, PAIR), BF16) for rows in (256, 128, 128)],
        in_specs=[pl.BlockSpec(memory_space=pltpu.VMEM)] * 4,
        out_specs=[pl.BlockSpec(memory_space=pltpu.VMEM)] * 3,
        scratch_shapes=[pltpu.VMEM((256, PAIR), F32)],
        compiler_params=pltpu.CompilerParams(vmem_limit_bytes=SMALL_LIMIT),
        cost_estimate=pl.CostEstimate(flops=1000000, bytes_accessed=100000, transcendentals=0),
        name="join",
    )(after, own, odd, even)


def shifted(rows):
    place = lax.broadcasted_iota(jnp.int32, rows.shape, 0) % 8
    before = jnp.where(place == 0, 0.0, jnp.roll(rows, 1, axis=0))
    after = jnp.where(place == 7, 0.0, jnp.roll(rows, -1, axis=0))
    return before, rows, after


def column_windows(cells, p2m_ref, far_rows, near_rows):
    multipole = lax.dot_general(
        cells.astype(BF16), p2m_ref[...], (((1,), (1,)), ((), ())), preferred_element_type=F32
    )
    sources = shifted(multipole.astype(BF16).astype(F32))
    blank = jnp.zeros((8, PAIR), F32)
    for b in range(3):
        for y in range(4):
            slab = sources[b][64 * y : 64 * y + 64]
            for offset_x in range(7):
                if offset_x == 0:
                    window = jnp.concatenate([blank, slab[0:8], blank, slab[16:24]], axis=0)
                elif offset_x == 6:
                    window = jnp.concatenate([slab[40:48], blank, slab[56:64], blank], axis=0)
                else:
                    window = slab[8 * (offset_x - 1) : 8 * (offset_x + 3)]
                far_rows[offset_x, b, 32 * y : 32 * y + 32] = window.astype(BF16)
    before, same, after = shifted(cells)
    lane = lax.broadcasted_iota(jnp.int32, cells.shape, 1)
    beside = jnp.where(lane < WIDTH, after, before)
    for k, kind in enumerate((same, beside)):
        for y in range(4):
            for offset_x in range(3):
                near_rows[offset_x, k, 32 * y : 32 * y + 32] = kind[
                    64 * y + 8 * (offset_x + 1) : 64 * y + 8 * (offset_x + 5)
                ].astype(BF16)


def spans(places, first, offset, parity):
    found = [
        (target, places.index(target + offset + first))
        for target in range(4)
        if target + offset + first in places
        and not (parity and ((offset == 0 and target % 2 == 0) or (offset == 6 and target % 2 == 1)))
    ]
    return found


def add_products(far, near, places, far_rows, near_rows, far_ref, near_ref):
    for offset_y in range(7):
        found = spans(places, -1, offset_y, True)
        if not found:
            continue
        rows = slice(32 * found[0][1], 32 * found[-1][1] + 32)
        chunks, weights = [], []
        for offset_x in range(7):
            inner = 2 <= offset_x <= 4 and 2 <= offset_y <= 4
            for b in range(3):
                if inner and b == 1:
                    continue
                chunks.append(far_rows[offset_x, b, rows])
                weights.append(far_ref[offset_x, offset_y, 2 * b : 2 * b + 2].reshape(PAIR, PAIR))
        product = jnp.dot(
            jnp.concatenate(chunks, axis=1), jnp.concatenate(weights, axis=0), preferred_element_type=F32
        )
        for index, (target, _) in enumerate(found):
            far[target] += product[32 * index : 32 * index + 32]
    for offset_y in range(3):
        found = spans(places, 1, offset_y, False)
        if not found:
            continue
        rows = slice(32 * found[0][1], 32 * found[-1][1] + 32)
        chunks = [near_rows[offset_x, k, rows] for offset_x in range(3) for k in range(2)]
        weights = [near_ref[offset_x, offset_y].reshape(2 * PAIR, PAIR) for offset_x in range(3)]
        product = jnp.dot(
            jnp.concatenate(chunks, axis=1), jnp.concatenate(weights, axis=0), preferred_element_type=F32
        )
        for index, (target, _) in enumerate(found):
            near[target] += product[32 * index : 32 * index + 32]


def inner_kernel(own_ref, far_ref, near_ref, p2m_ref, far_out, near_out, far_rows, near_rows):
    column_windows(own_ref[...].astype(F32), p2m_ref, far_rows, near_rows)
    far = [jnp.zeros((32, PAIR), F32) for _ in range(4)]
    near = [jnp.zeros((32, PAIR), F32) for _ in range(4)]
    add_products(far, near, [2, 3, 4, 5], far_rows, near_rows, far_ref, near_ref)
    for y in range(4):
        far_out[32 * y : 32 * y + 32] = far[y]
        near_out[32 * y : 32 * y + 32] = near[y]


def outer_kernel(
    odd_ref, even_ref, far_part, near_part, far_ref, near_ref, p2m_ref, l2p_ref,
    out_ref, out_rows, far_rows, near_rows,
):
    pairs = out_ref.shape[2] // PAIR
    even, odd = even_ref[...].astype(F32), odd_ref[...].astype(F32)
    low, high = from_neighbours("gy", even, odd, even, odd)
    column_windows(jnp.concatenate([low, high], axis=0), p2m_ref, far_rows, near_rows)
    far = [far_part[32 * y : 32 * y + 32] for y in range(4)]
    near = [near_part[32 * y : 32 * y + 32] for y in range(4)]
    add_products(far, near, [0, 1, 6, 7], far_rows, near_rows, far_ref, near_ref)
    rounded = jnp.concatenate(far, axis=0).astype(BF16)
    total = jnp.concatenate(near, axis=0)
    out_rows[...] = total + jnp.dot(rounded, l2p_ref[...], preferred_element_type=F32)
    for x in range(4):
        for pair in range(pairs):
            out_ref[x, :, pair * PAIR : (pair + 1) * PAIR] = out_rows[
                pl.ds(x * pairs + pair, 4, stride=4 * pairs), :
            ]


def inner(own, far, near, p2m):
    return pl.pallas_call(
        inner_kernel,
        out_shape=[pltpu.VMEM((128, PAIR), F32)] * 2,
        in_specs=[pl.BlockSpec(memory_space=pltpu.VMEM)] * 4,
        out_specs=[pl.BlockSpec(memory_space=pltpu.VMEM)] * 2,
        scratch_shapes=[pltpu.VMEM((7, 3, 128, PAIR), BF16), pltpu.VMEM((3, 2, 128, PAIR), BF16)],
        compiler_params=pltpu.CompilerParams(vmem_limit_bytes=VMEM_LIMIT),
        cost_estimate=pl.CostEstimate(flops=400000000, bytes_accessed=6000000, transcendentals=0),
        name="inner",
    )(own, far, near, p2m)


def outer(shape, odd, even, far_part, near_part, far, near, p2m, l2p):
    return pl.pallas_call(
        outer_kernel,
        out_shape=jax.ShapeDtypeStruct(shape, F32),
        in_specs=[pl.BlockSpec(memory_space=pltpu.VMEM)] * 8,
        out_specs=pl.BlockSpec(memory_space=pltpu.VMEM),
        scratch_shapes=[
            pltpu.VMEM((128, PAIR), F32),
            pltpu.VMEM((7, 3, 128, PAIR), BF16),
            pltpu.VMEM((3, 2, 128, PAIR), BF16),
        ],
        compiler_params=pltpu.CompilerParams(vmem_limit_bytes=VMEM_LIMIT),
        cost_estimate=pl.CostEstimate(flops=400000000, bytes_accessed=6000000, transcendentals=0),
        name="outer",
    )(odd, even, far_part, near_part, far, near, p2m, l2p)


def local(density, p2m_operator, m2l_table, near_table, l2p_operator):
    odd, even = swapped(density, "gx", 1), swapped(density, "gx", 0)
    far, near, p2m, l2p = packed(first(), p2m_operator, m2l_table, near_table, l2p_operator)
    own, to_odd, to_even = joined(p2m, density, odd, even)
    odd, even = swapped(to_odd, "gy", 1), swapped(to_even, "gy", 0)
    parts = inner(own, far, near, p2m)
    return outer(density.shape, odd, even, *parts, far, near, p2m, l2p)


def solution(mesh):
    placed = (P("gx", "gy", None), P(), P(), P(), P())
    return jax.shard_map(
        local, mesh=mesh, in_specs=placed, out_specs=P("gx", "gy", None), check_vma=False
    )
```

time: 14.4 us -> 12.9 us (0.90)
  Pallas kernels: 5.64 us -> 4.45 us
  waiting for transfers between devices: 2.23 us -> 1.46 us
  starting transfers between devices: 6.19 us -> 6.79 us
    pallas_call x1, Pallas kernels: 3.01 us -> 1.34 us  [packed(): pl.pallas_call(pack_kernel, out_shape=[pltpu.VMEM(shape, BF16) for shape...]
    ppermute x4, waiting for transfers between devices: 2.23 us -> 1.46 us  [swapped(): return lax.ppermute(cells, AXES, pairs)]
    ppermute x4, starting transfers between devices: 6.19 us -> 6.79 us  [swapped(): return lax.ppermute(cells, AXES, pairs)]
    pallas_call x1 -> x4, Pallas kernels: 2.62 us -> 3.11 us  [the longest x1 1.7 us: outer(): pl.pallas_call(outer_kernel, out_shape=jax.ShapeDtypeStruct(shape, F32),...]
  transfers between devices with their start and end apart: 4 -> 4, of which waited for: 1 -> 2; matrix products, arithmetic and copies ran while one was open for 0% -> 0% of each run, Pallas kernels for 21% -> 21%
where the time goes in v4:
time: 12.9 us; the launch traced here: 12.8 us
  starting transfers between devices  6.79 us (53%)
  Pallas kernels  4.45 us (34%)
  waiting for transfers between devices  1.46 us (11%)
    ppermute x4, starting transfers between devices, swapped(): return lax.ppermute(cells, AXES, pairs)  6.79 us
    pallas_call x1, Pallas kernels, outer(): pl.pallas_call(outer_kernel, out_shape=jax.ShapeDtypeStruct(shape, F32),...  1.7 us
    ppermute x4, waiting for transfers between devices, swapped(): return lax.ppermute(cells, AXES, pairs)  1.46 us
    pallas_call x1, Pallas kernels, packed(): pl.pallas_call(pack_kernel, out_shape=[pltpu.VMEM(shape, BF16) for shape...  1.34 us
    pallas_call x1, Pallas kernels, inner(): pl.pallas_call(inner_kernel, out_shape=[pltpu.VMEM((128, PAIR), F32)] * 2...  1.3 us
  transfers between devices with their start and end apart: 4, of which 2 were waited for; matrix products, arithmetic and copies ran while one was open for 0% of the time, Pallas kernels for 21%

profile of v4, /device:TPU:0, one launch (start us, length us, event | category | flops | bytes accessed | tf_op | source)
XLA Modules:
  0.0 12.8 jit_solution(10851569179677730738)
XLA Ops:
  0.0 0.0 copy-start.4
  0.0 0.0 copy-start.1
  0.0 0.0 copy-start
  0.0 0.0 copy-start.3
  0.0 3.0 %collective-permute-start = (bf16[4,4,1024]{2,1,0:T(4,128)(2,1)}, bf16[4,4,1024]{2,1,0:T(4,128)(2,1)S(1)}, u32[]{:S(2)}, u32[]{:S(2)}) collective-permute-start(bf16[4,4,1024]{2,1,0:T(4,128)(2,1)} %own_ref.1), channel_id=1, source_target_pairs={{0,1},{1,0},{2,3},{3,2},{4,8},{5,9},{6,10},{7,11},{8,4},{9,5},{10,... | collective-permute-start | bytes 98312 | tf_op jit(solution)/shard_map/ppermute | solution.py:33
  3.0 0.2 %collective-permute-start.1 = (bf16[4,4,1024]{2,1,0:T(4,128)(2,1)}, bf16[4,4,1024]{2,1,0:T(4,128)(2,1)S(1)}, u32[]{:S(2)}, u32[]{:S(2)}) collective-permute-start(bf16[4,4,1024]{2,1,0:T(4,128)(2,1)} %own_ref.1), channel_id=1, source_target_pairs={{0,4},{1,5},{2,6},{3,7},{4,0},{5,1},{6,2},{7,3},{8,12},{9,13},{10,... | collective-permute-start | bytes 98312 | tf_op jit(solution)/shard_map/ppermute | solution.py:33
  3.2 0.0 copy-start.2
  3.2 0.0 copy-done.4
  3.2 0.0 copy-done.1
  3.2 0.0 copy-done
  3.2 0.0 copy-done.3
  3.3 1.3 %pack.1 = (bf16[7,7,6,64,128]{4,3,2,1,0:T(8,128)(2,1)S(1)}, bf16[3,3,2,128,128]{4,3,2,1,0:T(8,128)(2,1)S(1)}, bf16[128,128]{1,0:T(8,128)(2,1)S(1)}, bf16[128,128]{1,0:T(8,128)(2,1)S(1)}) custom-call(f32[8,128]{1,0:T(8,128)S(1)} %first.1.first_ref, bf16[56,64]{1,0:T(8,128)(2,1)S(1)} %bitcast.1, bf16[7,7,7,56,56]{4,3,2,1,0:T(8,128)(2,1)S(1)} %copy-done, ...), custom_call_target="tpu_custom_call" | custom-call | flops 4000000 | bytes 10000000 | tf_op jit(solution)/shard_map/pack/pallas_call | solution.py:98
  4.6 0.5 %collective-permute-done.odd_ref = bf16[4,4,1024]{2,1,0:T(4,128)(2,1)S(1)} collective-permute-done((bf16[4,4,1024]{2,1,0:T(4,128)(2,1)}, bf16[4,4,1024]{2,1,0:T(4,128)(2,1)S(1)}, u32[]{:S(2)}, u32[]{:S(2)}) %collective-permute-start) | collective-permute-done | bytes 32800 | tf_op jit(solution)/shard_map/ppermute | solution.py:33
  5.1 0.0 collective-permute-done.1.even_ref
  5.1 0.0 copy-done.2
  5.1 0.1 join.1
  5.3 0.2 %collective-permute-start.2 = (bf16[128,128]{1,0:T(8,128)(2,1)S(1)}, bf16[128,128]{1,0:T(8,128)(2,1)S(1)}, u32[]{:S(2)}, u32[]{:S(2)}) collective-permute-start(bf16[128,128]{1,0:T(8,128)(2,1)S(1)} %get-tuple-element.15), channel_id=1, source_target_pairs={{0,4},{1,2},{2,1},{3,7},{4,0},{5,6},{6,5},{7,3},{8,12},{9,10},{10,... | collective-permute-start | bytes 98312 | tf_op jit(solution)/shard_map/ppermute | solution.py:33
  5.4 3.4 %collective-permute-start.3 = (bf16[128,128]{1,0:T(8,128)(2,1)S(1)}, bf16[128,128]{1,0:T(8,128)(2,1)S(1)}, u32[]{:S(2)}, u32[]{:S(2)}) collective-permute-start(bf16[128,128]{1,0:T(8,128)(2,1)S(1)} %get-tuple-element.16), channel_id=1, source_target_pairs={{0,1},{1,0},{2,3},{3,2},{4,5},{5,4},{6,7},{7,6},{8,9},{9,8},{10,11... | collective-permute-start | bytes 98312 | tf_op jit(solution)/shard_map/ppermute | solution.py:33
  8.8 1.3 %inner.1 = (f32[128,128]{1,0:T(8,128)S(1)}, f32[128,128]{1,0:T(8,128)S(1)}) custom-call(bf16[256,128]{1,0:T(8,128)(2,1)S(1)} %get-tuple-element.17.own_ref, bf16[7,7,6,64,128]{4,3,2,1,0:T(8,128)(2,1)S(1)} %get-tuple-element.18.far_ref, bf16[3,3,2,128,128]{4,3,2,1,0:T(8,128)(2,1)S(1)} %get-tuple-element.19.near_ref, ...), custom_call_target="tpu_custom_call" | custom-call | flops 400000000 | bytes 6000000 | tf_op jit(solution)/shard_map/inner/pallas_call | solution.py:268
  10.1 0.0 collective-permute-done.2.odd_ref
  10.1 0.9 %collective-permute-done.3.even_ref = bf16[128,128]{1,0:T(8,128)(2,1)S(1)} collective-permute-done((bf16[128,128]{1,0:T(8,128)(2,1)S(1)}, bf16[128,128]{1,0:T(8,128)(2,1)S(1)}, u32[]{:S(2)}, u32[]{:S(2)}) %collective-permute-start.3) | collective-permute-done | bytes 32800 | tf_op jit(solution)/shard_map/ppermute | solution.py:33
  11.1 1.7 %outer.1 = f32[4,4,1024]{2,1,0:T(4,128)} custom-call(bf16[128,128]{1,0:T(8,128)(2,1)S(1)} %collective-permute-done.2.odd_ref, bf16[128,128]{1,0:T(8,128)(2,1)S(1)} %collective-permute-done.3.even_ref, f32[128,128]{1,0:T(8,128)S(1)} %get-tuple-element.20.far_part, f32[128,128]{1,0:T(8,128)S(1)} %get-tuple-element.21.near_part, ...), custom_call_target="tpu_custom_call" | custom-call | flops 400000000 | bytes 6000000 | tf_op jit(solution)/shard_map/outer/pallas_call | solution.py:281
  (1 shorter events, 0.0 us)
Async XLA Ops:
  0.0 3.2 %copy-start.4 = (bf16[56,64]{1,0:T(8,128)(2,1)S(1)}, bf16[56,64]{1,0:T(8,128)(2,1)}, u32[]{:S(2)}) copy-start(bf16[56,64]{1,0:T(8,128)(2,1)} %l2p_ref.1) | copy-start | bytes 21508
  0.0 3.2 %copy-start.1 = (bf16[3,3,3,64,64]{4,3,2,1,0:T(8,128)(2,1)S(1)}, bf16[3,3,3,64,64]{4,3,2,1,0:T(8,128)(2,1)}, u32[]{:S(2)}) copy-start(bf16[3,3,3,64,64]{4,3,2,1,0:T(8,128)(2,1)} %near_ref.1) | copy-start | bytes 663556
  0.0 3.2 %copy-start = (bf16[7,7,7,56,56]{4,3,2,1,0:T(8,128)(2,1)S(1)}, bf16[7,7,7,56,56]{4,3,2,1,0:T(8,128)(2,1)}, u32[]{:S(2)}) copy-start(bf16[7,7,7,56,56]{4,3,2,1,0:T(8,128)(2,1)} %m2l_ref.1) | copy-start | bytes 6453892
  0.0 3.2 %copy-start.3 = (bf16[64,56]{0,1:T(8,128)(2,1)S(1)}, bf16[64,56]{0,1:T(8,128)(2,1)}, u32[]{:S(2)}) copy-start(bf16[64,56]{0,1:T(8,128)(2,1)} %param.6) | copy-start | bytes 21508
  0.0 5.1 %collective-permute-start = (bf16[4,4,1024]{2,1,0:T(4,128)(2,1)}, bf16[4,4,1024]{2,1,0:T(4,128)(2,1)S(1)}, u32[]{:S(2)}, u32[]{:S(2)}) collective-permute-start(bf16[4,4,1024]{2,1,0:T(4,128)(2,1)} %own_ref.1), channel_id=1, source_target_pairs={{0,1},{1,0},{2,3},{3,2},{4,8},{5,9},{6,10},{7,11},{8,4},{9,5},{10,... | collective-permute-start | bytes 98312 | tf_op jit(solution)/shard_map/ppermute | solution.py:33
  3.0 2.1 %collective-permute-start.1 = (bf16[4,4,1024]{2,1,0:T(4,128)(2,1)}, bf16[4,4,1024]{2,1,0:T(4,128)(2,1)S(1)}, u32[]{:S(2)}, u32[]{:S(2)}) collective-permute-start(bf16[4,4,1024]{2,1,0:T(4,128)(2,1)} %own_ref.1), channel_id=1, source_target_pairs={{0,4},{1,5},{2,6},{3,7},{4,0},{5,1},{6,2},{7,3},{8,12},{9,13},{10,... | collective-permute-start | bytes 98312 | tf_op jit(solution)/shard_map/ppermute | solution.py:33
  3.2 1.9 %copy-start.2 = (bf16[4,4,1024]{2,1,0:T(4,128)(2,1)S(1)}, bf16[4,4,1024]{2,1,0:T(4,128)(2,1)}, u32[]{:S(2)}) copy-start(bf16[4,4,1024]{2,1,0:T(4,128)(2,1)} %own_ref.1) | copy-start | bytes 98308
  5.3 4.9 %collective-permute-start.2 = (bf16[128,128]{1,0:T(8,128)(2,1)S(1)}, bf16[128,128]{1,0:T(8,128)(2,1)S(1)}, u32[]{:S(2)}, u32[]{:S(2)}) collective-permute-start(bf16[128,128]{1,0:T(8,128)(2,1)S(1)} %get-tuple-element.15), channel_id=1, source_target_pairs={{0,4},{1,2},{2,1},{3,7},{4,0},{5,6},{6,5},{7,3},{8,12},{9,10},{10,... | collective-permute-start | bytes 98312 | tf_op jit(solution)/shard_map/ppermute | solution.py:33
  5.4 5.6 %collective-permute-start.3 = (bf16[128,128]{1,0:T(8,128)(2,1)S(1)}, bf16[128,128]{1,0:T(8,128)(2,1)S(1)}, u32[]{:S(2)}, u32[]{:S(2)}) collective-permute-start(bf16[128,128]{1,0:T(8,128)(2,1)S(1)} %get-tuple-element.16), channel_id=1, source_target_pairs={{0,1},{1,0},{2,3},{3,2},{4,5},{5,4},{6,7},{7,6},{8,9},{9,8},{10,11... | collective-permute-start | bytes 98312 | tf_op jit(solution)/shard_map/ppermute | solution.py:33

commit v5 on v4

--- a/solution.py
+++ b/solution.py
@@ -168,8 +168,9 @@
     )
     sources = shifted(multipole.astype(BF16).astype(F32))
     blank = jnp.zeros((8, PAIR), F32)
+    count = cells.shape[0] // 64
     for b in range(3):
-        for y in range(4):
+        for y in range(count):
             slab = sources[b][64 * y : 64 * y + 64]
             for offset_x in range(7):
                 if offset_x == 0:
@@ -183,7 +184,7 @@
     lane = lax.broadcasted_iota(jnp.int32, cells.shape, 1)
     beside = jnp.where(lane < WIDTH, after, before)
     for k, kind in enumerate((same, beside)):
-        for y in range(4):
+        for y in range(count):
             for offset_x in range(3):
                 near_rows[offset_x, k, 32 * y : 32 * y + 32] = kind[
                     64 * y + 8 * (offset_x + 1) : 64 * y + 8 * (offset_x + 5)
@@ -218,7 +219,7 @@
             jnp.concatenate(chunks, axis=1), jnp.concatenate(weights, axis=0), preferred_element_type=F32
         )
         for index, (target, _) in enumerate(found):
-            far[target] += product[32 * index : 32 * index + 32]
+            far[32 * target : 32 * target + 32] += product[32 * index : 32 * index + 32]
     for offset_y in range(3):
         found = spans(places, 1, offset_y, False)
         if not found:
@@ -230,36 +231,52 @@
             jnp.concatenate(chunks, axis=1), jnp.concatenate(weights, axis=0), preferred_element_type=F32
         )
         for index, (target, _) in enumerate(found):
-            near[target] += product[32 * index : 32 * index + 32]
+            near[32 * target : 32 * target + 32] += product[32 * index : 32 * index + 32]
 
 
 def inner_kernel(own_ref, far_ref, near_ref, p2m_ref, far_out, near_out, far_rows, near_rows):
     column_windows(own_ref[...].astype(F32), p2m_ref, far_rows, near_rows)
-    far = [jnp.zeros((32, PAIR), F32) for _ in range(4)]
-    near = [jnp.zeros((32, PAIR), F32) for _ in range(4)]
-    add_products(far, near, [2, 3, 4, 5], far_rows, near_rows, far_ref, near_ref)
-    for y in range(4):
-        far_out[32 * y : 32 * y + 32] = far[y]
-        near_out[32 * y : 32 * y + 32] = near[y]
+    far_out[...] = jnp.zeros_like(far_out)
+    near_out[...] = jnp.zeros_like(near_out)
+    add_products(far_out, near_out, [2, 3, 4, 5], far_rows, near_rows, far_ref, near_ref)
+
+
+def add_halo(cells_ref, odd, far, near, far_ref, near_ref, p2m_ref, far_rows, near_rows):
+    place = lax.axis_index("gy")
+    before = lax.rem(place, 2) == (0 if odd else 1)
+    outside = place == jnp.where(before, 0, lax.axis_size("gy") - 1)
+    cells = jnp.where(outside, 0.0, cells_ref[...].astype(F32))
+    column_windows(cells, p2m_ref, far_rows, near_rows)
+
+    @pl.when(before)
+    def _():
+        add_products(far, near, [0, 1], far_rows, near_rows, far_ref, near_ref)
+
+    @pl.when(jnp.logical_not(before))
+    def _():
+        add_products(far, near, [6, 7], far_rows, near_rows, far_ref, near_ref)
 
 
 def outer_kernel(
-    odd_ref, even_ref, far_part, near_part, far_ref, near_ref, p2m_ref, l2p_ref,
-    out_ref, out_rows, far_rows, near_rows,
+    cells_ref, far_part, near_part, far_ref, near_ref, p2m_ref, far_out, near_out, far_rows, near_rows
+):
+    far_out[...] = far_part[...]
+    near_out[...] = near_part[...]
+    add_halo(cells_ref, False, far_out, near_out, far_ref, near_ref, p2m_ref, far_rows, near_rows)
+
+
+def last_kernel(
+    far_part, near_part, cells_ref, far_ref, near_ref, p2m_ref, l2p_ref,
+    out_ref, far, near, far_rows, near_rows,
 ):
     pairs = out_ref.shape[2] // PAIR
-    even, odd = even_ref[...].astype(F32), odd_ref[...].astype(F32)
-    low, high = from_neighbours("gy", even, odd, even, odd)
-    column_windows(jnp.concatenate([low, high], axis=0), p2m_ref, far_rows, near_rows)
-    far = [far_part[32 * y : 32 * y + 32] for y in range(4)]
-    near = [near_part[32 * y : 32 * y + 32] for y in range(4)]
-    add_products(far, near, [0, 1, 6, 7], far_rows, near_rows, far_ref, near_ref)
-    rounded = jnp.concatenate(far, axis=0).astype(BF16)
-    total = jnp.concatenate(near, axis=0)
-    out_rows[...] = total + jnp.dot(rounded, l2p_ref[...], preferred_element_type=F32)
+    far[...] = far_part[...]
+    near[...] = near_part[...]
+    add_halo(cells_ref, True, far, near, far_ref, near_ref, p2m_ref, far_rows, near_rows)
+    near[...] += jnp.dot(far[...].astype(BF16), l2p_ref[...], preferred_element_type=F32)
     for x in range(4):
         for pair in range(pairs):
-            out_ref[x, :, pair * PAIR : (pair + 1) * PAIR] = out_rows[
+            out_ref[x, :, pair * PAIR : (pair + 1) * PAIR] = near[
                 pl.ds(x * pairs + pair, 4, stride=4 * pairs), :
             ]
 
@@ -277,21 +294,35 @@
     )(own, far, near, p2m)
 
 
-def outer(shape, odd, even, far_part, near_part, far, near, p2m, l2p):
+def outer(cells, far_part, near_part, far, near, p2m):
     return pl.pallas_call(
         outer_kernel,
+        out_shape=[pltpu.VMEM((128, PAIR), F32)] * 2,
+        in_specs=[pl.BlockSpec(memory_space=pltpu.VMEM)] * 6,
+        out_specs=[pl.BlockSpec(memory_space=pltpu.VMEM)] * 2,
+        scratch_shapes=[pltpu.VMEM((7, 3, 64, PAIR), BF16), pltpu.VMEM((3, 2, 64, PAIR), BF16)],
+        compiler_params=pltpu.CompilerParams(vmem_limit_bytes=VMEM_LIMIT),
+        cost_estimate=pl.CostEstimate(flops=200000000, bytes_accessed=3000000, transcendentals=0),
+        name="outer",
+    )(cells, far_part, near_part, far, near, p2m)
+
+
+def last(shape, cells, far_part, near_part, far, near, p2m, l2p):
+    return pl.pallas_call(
+        last_kernel,
         out_shape=jax.ShapeDtypeStruct(shape, F32),
-        in_specs=[pl.BlockSpec(memory_space=pltpu.VMEM)] * 8,
+        in_specs=[pl.BlockSpec(memory_space=pltpu.VMEM)] * 7,
         out_specs=pl.BlockSpec(memory_space=pltpu.VMEM),
         scratch_shapes=[
             pltpu.VMEM((128, PAIR), F32),
-            pltpu.VMEM((7, 3, 128, PAIR), BF16),
-            pltpu.VMEM((3, 2, 128, PAIR), BF16),
+            pltpu.VMEM((128, PAIR), F32),
+            pltpu.VMEM((7, 3, 64, PAIR), BF16),
+            pltpu.VMEM((3, 2, 64, PAIR), BF16),
         ],
         compiler_params=pltpu.CompilerParams(vmem_limit_bytes=VMEM_LIMIT),
-        cost_estimate=pl.CostEstimate(flops=400000000, bytes_accessed=6000000, transcendentals=0),
-        name="outer",
-    )(odd, even, far_part, near_part, far, near, p2m, l2p)
+        cost_estimate=pl.CostEstimate(flops=200000000, bytes_accessed=3000000, transcendentals=0),
+        name="last",
+    )(far_part, near_part, cells, far, near, p2m, l2p)
 
 
 def local(density, p2m_operator, m2l_table, near_table, l2p_operator):
@@ -300,7 +331,8 @@
     own, to_odd, to_even = joined(p2m, density, odd, even)
     odd, even = swapped(to_odd, "gy", 1), swapped(to_even, "gy", 0)
     parts = inner(own, far, near, p2m)
-    return outer(density.shape, odd, even, *parts, far, near, p2m, l2p)
+    parts = outer(even, *parts, far, near, p2m)
+    return last(density.shape, odd, *parts, far, near, p2m, l2p)
 
 
 def solution(mesh):

time: 12.9 us -> 12.3 us (0.953)
  the two profiles are of different devices: /device:TPU:0 before, /device:TPU:4 now
where the time goes in v5:
time: 12.3 us; the launch traced here: 12.2 us
  Pallas kernels  4.9 us (40%)
  starting transfers between devices  3.33 us (27%)
  waiting for transfers between devices  3.12 us (25%)
  local copies, waits for them, and re-layouts  0.78 us (6%)
    ppermute x4, starting transfers between devices, swapped(): return lax.ppermute(cells, AXES, pairs)  3.33 us
    ppermute x4, waiting for transfers between devices, swapped(): return lax.ppermute(cells, AXES, pairs)  3.12 us
    pallas_call x1, Pallas kernels, last(): pl.pallas_call(last_kernel, out_shape=jax.ShapeDtypeStruct(shape, F32), i...  1.48 us
    pallas_call x1, Pallas kernels, packed(): pl.pallas_call(pack_kernel, out_shape=[pltpu.VMEM(shape, BF16) for shape...  1.34 us
    pallas_call x1, Pallas kernels, inner(): pl.pallas_call(inner_kernel, out_shape=[pltpu.VMEM((128, PAIR), F32)] * 2...  1.3 us
    unnamed x10, local copies, waits for them, and re-layouts  0.78 us
    pallas_call x1, Pallas kernels, outer(): pl.pallas_call(outer_kernel, out_shape=[pltpu.VMEM((128, PAIR), F32)] * 2...  0.68 us
  transfers between devices with their start and end apart: 4, of which 3 were waited for; matrix products, arithmetic and copies ran while one was open for 0% of the time, Pallas kernels for 27%

profile of v5, /device:TPU:4, one launch (start us, length us, event | category | flops | bytes accessed | tf_op | source)
XLA Modules:
  0.0 12.2 jit_solution(7532048541092099247)
XLA Ops:
  0.0 0.0 copy-start.4
  0.0 0.0 copy-start.1
  0.0 0.0 copy-start
  0.0 0.0 copy-start.3
  0.0 1.6 %collective-permute-start = (bf16[4,4,1024]{2,1,0:T(4,128)(2,1)}, bf16[4,4,1024]{2,1,0:T(4,128)(2,1)S(1)}, u32[]{:S(2)}, u32[]{:S(2)}) collective-permute-start(bf16[4,4,1024]{2,1,0:T(4,128)(2,1)} %own_ref.1), channel_id=1, source_target_pairs={{0,1},{1,0},{2,3},{3,2},{4,8},{5,9},{6,10},{7,11},{8,4},{9,5},{10,... | collective-permute-start | bytes 98312 | tf_op jit(solution)/shard_map/ppermute | solution.py:33
  1.6 0.2 %collective-permute-start.1 = (bf16[4,4,1024]{2,1,0:T(4,128)(2,1)}, bf16[4,4,1024]{2,1,0:T(4,128)(2,1)S(1)}, u32[]{:S(2)}, u32[]{:S(2)}) collective-permute-start(bf16[4,4,1024]{2,1,0:T(4,128)(2,1)} %own_ref.1), channel_id=1, source_target_pairs={{0,4},{1,5},{2,6},{3,7},{4,0},{5,1},{6,2},{7,3},{8,12},{9,13},{10,... | collective-permute-start | bytes 98312 | tf_op jit(solution)/shard_map/ppermute | solution.py:33
  1.8 0.0 copy-start.2
  1.8 0.0 copy-done.4
  1.8 0.0 copy-done.1
  1.8 0.8 %copy-done = bf16[7,7,7,56,56]{4,3,2,1,0:T(8,128)(2,1)S(1)} copy-done((bf16[7,7,7,56,56]{4,3,2,1,0:T(8,128)(2,1)S(1)}, bf16[7,7,7,56,56]{4,3,2,1,0:T(8,128)(2,1)}, u32[]{:S(2)}) %copy-start) | copy-done | bytes 2151320
  2.6 0.0 copy-done.3
  2.6 1.3 %pack.1 = (bf16[7,7,6,64,128]{4,3,2,1,0:T(8,128)(2,1)S(1)}, bf16[3,3,2,128,128]{4,3,2,1,0:T(8,128)(2,1)S(1)}, bf16[128,128]{1,0:T(8,128)(2,1)S(1)}, bf16[128,128]{1,0:T(8,128)(2,1)S(1)}) custom-call(f32[8,128]{1,0:T(8,128)S(1)} %first.1.first_ref, bf16[56,64]{1,0:T(8,128)(2,1)S(1)} %bitcast.1, bf16[7,7,7,56,56]{4,3,2,1,0:T(8,128)(2,1)S(1)} %copy-done, ...), custom_call_target="tpu_custom_call" | custom-call | flops 4000000 | bytes 10000000 | tf_op jit(solution)/shard_map/pack/pallas_call | solution.py:98
  3.9 0.3 %collective-permute-done.odd_ref = bf16[4,4,1024]{2,1,0:T(4,128)(2,1)S(1)} collective-permute-done((bf16[4,4,1024]{2,1,0:T(4,128)(2,1)}, bf16[4,4,1024]{2,1,0:T(4,128)(2,1)S(1)}, u32[]{:S(2)}, u32[]{:S(2)}) %collective-permute-start) | collective-permute-done | bytes 32800 | tf_op jit(solution)/shard_map/ppermute | solution.py:33
  4.2 0.0 collective-permute-done.1.even_ref
  4.2 0.0 copy-done.2
  4.2 0.1 join.1
  4.3 1.6 %collective-permute-start.2 = (bf16[128,128]{1,0:T(8,128)(2,1)S(1)}, bf16[128,128]{1,0:T(8,128)(2,1)S(1)}, u32[]{:S(2)}, u32[]{:S(2)}) collective-permute-start(bf16[128,128]{1,0:T(8,128)(2,1)S(1)} %get-tuple-element.17), channel_id=1, source_target_pairs={{0,1},{1,0},{2,3},{3,2},{4,5},{5,4},{6,7},{7,6},{8,9},{9,8},{10,11... | collective-permute-start | bytes 98312 | tf_op jit(solution)/shard_map/ppermute | solution.py:33
  5.9 0.0 collective-permute-start.3
  5.9 1.3 %inner.1 = (f32[128,128]{1,0:T(8,128)S(1)}, f32[128,128]{1,0:T(8,128)S(1)}) custom-call(bf16[256,128]{1,0:T(8,128)(2,1)S(1)} %get-tuple-element.18.own_ref, bf16[7,7,6,64,128]{4,3,2,1,0:T(8,128)(2,1)S(1)} %get-tuple-element.19.far_ref, bf16[3,3,2,128,128]{4,3,2,1,0:T(8,128)(2,1)S(1)} %get-tuple-element.20.near_ref, ...), custom_call_target="tpu_custom_call" | custom-call | flops 400000000 | bytes 6000000 | tf_op jit(solution)/shard_map/inner/pallas_call | solution.py:285
  7.2 1.1 %collective-permute-done.2.cells_ref = bf16[128,128]{1,0:T(8,128)(2,1)S(1)} collective-permute-done((bf16[128,128]{1,0:T(8,128)(2,1)S(1)}, bf16[128,128]{1,0:T(8,128)(2,1)S(1)}, u32[]{:S(2)}, u32[]{:S(2)}) %collective-permute-start.2) | collective-permute-done | bytes 32800 | tf_op jit(solution)/shard_map/ppermute | solution.py:33
  8.3 0.7 %outer.1 = (f32[128,128]{1,0:T(8,128)S(1)}, f32[128,128]{1,0:T(8,128)S(1)}) custom-call(bf16[128,128]{1,0:T(8,128)(2,1)S(1)} %collective-permute-done.2.cells_ref, f32[128,128]{1,0:T(8,128)S(1)} %get-tuple-element.21.far_part, f32[128,128]{1,0:T(8,128)S(1)} %get-tuple-element.22.near_part, bf16[7,7,6,64,128]{4,3,2,1,0:T(8,128)(2,1)S(1)} %get-tuple-element.19.far_ref, ...), custom_call_target="tpu_custom_call" | custom-call | flops 200000000 | bytes 3000000 | tf_op jit(solution)/shard_map/outer/pallas_call | solution.py:298
  9.0 1.7 %collective-permute-done.3.cells_ref = bf16[128,128]{1,0:T(8,128)(2,1)S(1)} collective-permute-done((bf16[128,128]{1,0:T(8,128)(2,1)S(1)}, bf16[128,128]{1,0:T(8,128)(2,1)S(1)}, u32[]{:S(2)}, u32[]{:S(2)}) %collective-permute-start.3) | collective-permute-done | bytes 32800 | tf_op jit(solution)/shard_map/ppermute | solution.py:33
  10.7 1.5 %last.1 = f32[4,4,1024]{2,1,0:T(4,128)} custom-call(f32[128,128]{1,0:T(8,128)S(1)} %get-tuple-element.23.far_part, f32[128,128]{1,0:T(8,128)S(1)} %get-tuple-element.24.near_part, bf16[128,128]{1,0:T(8,128)(2,1)S(1)} %collective-permute-done.3.cells_ref, bf16[7,7,6,64,128]{4,3,2,1,0:T(8,128)(2,1)S(1)} %get-tuple-element.19.far_ref, ...), custom_call_target="tpu_custom_call" | custom-call | flops 200000000 | bytes 3000000 | tf_op jit(solution)/shard_map/last/pallas_call | solution.py:311
  (1 shorter events, 0.0 us)
Async XLA Ops:
  0.0 1.8 %copy-start.4 = (bf16[56,64]{1,0:T(8,128)(2,1)S(1)}, bf16[56,64]{1,0:T(8,128)(2,1)}, u32[]{:S(2)}) copy-start(bf16[56,64]{1,0:T(8,128)(2,1)} %l2p_ref.1) | copy-start | bytes 21508
  0.0 1.8 %copy-start.1 = (bf16[3,3,3,64,64]{4,3,2,1,0:T(8,128)(2,1)S(1)}, bf16[3,3,3,64,64]{4,3,2,1,0:T(8,128)(2,1)}, u32[]{:S(2)}) copy-start(bf16[3,3,3,64,64]{4,3,2,1,0:T(8,128)(2,1)} %near_ref.1) | copy-start | bytes 663556
  0.0 2.6 %copy-start = (bf16[7,7,7,56,56]{4,3,2,1,0:T(8,128)(2,1)S(1)}, bf16[7,7,7,56,56]{4,3,2,1,0:T(8,128)(2,1)}, u32[]{:S(2)}) copy-start(bf16[7,7,7,56,56]{4,3,2,1,0:T(8,128)(2,1)} %m2l_ref.1) | copy-start | bytes 6453892
  0.0 2.5 %copy-start.3 = (bf16[64,56]{0,1:T(8,128)(2,1)S(1)}, bf16[64,56]{0,1:T(8,128)(2,1)}, u32[]{:S(2)}) copy-start(bf16[64,56]{0,1:T(8,128)(2,1)} %param.6) | copy-start | bytes 21508
  0.0 4.2 %collective-permute-start = (bf16[4,4,1024]{2,1,0:T(4,128)(2,1)}, bf16[4,4,1024]{2,1,0:T(4,128)(2,1)S(1)}, u32[]{:S(2)}, u32[]{:S(2)}) collective-permute-start(bf16[4,4,1024]{2,1,0:T(4,128)(2,1)} %own_ref.1), channel_id=1, source_target_pairs={{0,1},{1,0},{2,3},{3,2},{4,8},{5,9},{6,10},{7,11},{8,4},{9,5},{10,... | collective-permute-start | bytes 98312 | tf_op jit(solution)/shard_map/ppermute | solution.py:33
  1.6 2.6 %collective-permute-start.1 = (bf16[4,4,1024]{2,1,0:T(4,128)(2,1)}, bf16[4,4,1024]{2,1,0:T(4,128)(2,1)S(1)}, u32[]{:S(2)}, u32[]{:S(2)}) collective-permute-start(bf16[4,4,1024]{2,1,0:T(4,128)(2,1)} %own_ref.1), channel_id=1, source_target_pairs={{0,4},{1,5},{2,6},{3,7},{4,0},{5,1},{6,2},{7,3},{8,12},{9,13},{10,... | collective-permute-start | bytes 98312 | tf_op jit(solution)/shard_map/ppermute | solution.py:33
  1.8 2.4 %copy-start.2 = (bf16[4,4,1024]{2,1,0:T(4,128)(2,1)S(1)}, bf16[4,4,1024]{2,1,0:T(4,128)(2,1)}, u32[]{:S(2)}) copy-start(bf16[4,4,1024]{2,1,0:T(4,128)(2,1)} %own_ref.1) | copy-start | bytes 98308
  4.3 4.0 %collective-permute-start.2 = (bf16[128,128]{1,0:T(8,128)(2,1)S(1)}, bf16[128,128]{1,0:T(8,128)(2,1)S(1)}, u32[]{:S(2)}, u32[]{:S(2)}) collective-permute-start(bf16[128,128]{1,0:T(8,128)(2,1)S(1)} %get-tuple-element.17), channel_id=1, source_target_pairs={{0,1},{1,0},{2,3},{3,2},{4,5},{5,4},{6,7},{7,6},{8,9},{9,8},{10,11... | collective-permute-start | bytes 98312 | tf_op jit(solution)/shard_map/ppermute | solution.py:33
  5.9 4.8 %collective-permute-start.3 = (bf16[128,128]{1,0:T(8,128)(2,1)S(1)}, bf16[128,128]{1,0:T(8,128)(2,1)S(1)}, u32[]{:S(2)}, u32[]{:S(2)}) collective-permute-start(bf16[128,128]{1,0:T(8,128)(2,1)S(1)} %get-tuple-element.25), channel_id=1, source_target_pairs={{0,4},{1,2},{2,1},{3,7},{4,0},{5,6},{6,5},{7,3},{8,12},{9,10},{10,... | collective-permute-start | bytes 98312 | tf_op jit(solution)/shard_map/ppermute | solution.py:33

commit v6 on v5

--- a/solution.py
+++ b/solution.py
@@ -1,3 +1,5 @@
+import functools
+
 import jax
 import jax.numpy as jnp
 from jax import lax
@@ -16,15 +18,16 @@
 AXES = ("gx", "gy")
 
 
-def swapped(cells, axis, odd):
+def swapped(cells, axis, first, step):
     sizes = [lax.axis_size(name) for name in AXES]
     dim = AXES.index(axis)
     pairs = []
     for place in range(sizes[0] * sizes[1]):
         at = list(divmod(place, sizes[1]))
-        partner = (at[dim] - odd) ^ 1
-        if at[dim] >= odd and partner + odd < sizes[dim]:
-            at[dim] = partner + odd
+        if at[dim] % step == first and at[dim] + 1 < sizes[dim]:
+            at[dim] += 1
+        elif at[dim] > 0 and (at[dim] - 1) % step == first:
+            at[dim] -= 1
         elif (at[1 - dim] ^ 1) < sizes[1 - dim]:
             at[1 - dim] ^= 1
         else:
@@ -115,7 +118,7 @@
     return low, high
 
 
-def join_kernel(after_ref, own_ref, odd_ref, even_ref, own_out, odd_out, even_out, rows_ref):
+def join_kernel(after_ref, own_ref, odd_ref, even_ref, own_out, odd_out, even_out, again_out, rows_ref):
     pairs = own_ref.shape[2] // PAIR
     for pair in range(pairs):
         lanes = slice(pair * PAIR, (pair + 1) * PAIR)
@@ -140,14 +143,15 @@
     head, tail = rows[:128], rows[128:]
     even_out[...] = jnp.where(lower, tail, head).astype(BF16)
     odd_out[...] = jnp.where(lower, head, tail).astype(BF16)
+    again_out[...] = jnp.where(lower, tail, head).astype(BF16)
 
 
 def joined(after, own, odd, even):
     return pl.pallas_call(
         join_kernel,
-        out_shape=[pltpu.VMEM((rows, PAIR), BF16) for rows in (256, 128, 128)],
+        out_shape=[pltpu.VMEM((rows, PAIR), BF16) for rows in (256, 128, 128, 128)],
         in_specs=[pl.BlockSpec(memory_space=pltpu.VMEM)] * 4,
-        out_specs=[pl.BlockSpec(memory_space=pltpu.VMEM)] * 3,
+        out_specs=[pl.BlockSpec(memory_space=pltpu.VMEM)] * 4,
         scratch_shapes=[pltpu.VMEM((256, PAIR), F32)],
         compiler_params=pltpu.CompilerParams(vmem_limit_bytes=SMALL_LIMIT),
         cost_estimate=pl.CostEstimate(flops=1000000, bytes_accessed=100000, transcendentals=0),
@@ -241,38 +245,41 @@
     add_products(far_out, near_out, [2, 3, 4, 5], far_rows, near_rows, far_ref, near_ref)
 
 
-def add_halo(cells_ref, odd, far, near, far_ref, near_ref, p2m_ref, far_rows, near_rows):
+def add_halo(cells_ref, trade, far, near, far_ref, near_ref, p2m_ref, far_rows, near_rows):
     place = lax.axis_index("gy")
-    before = lax.rem(place, 2) == (0 if odd else 1)
-    outside = place == jnp.where(before, 0, lax.axis_size("gy") - 1)
-    cells = jnp.where(outside, 0.0, cells_ref[...].astype(F32))
-    column_windows(cells, p2m_ref, far_rows, near_rows)
+    first, step = trade
+    after = jnp.logical_and(lax.rem(place, step) == first, place + 1 < lax.axis_size("gy"))
+    before = jnp.logical_and(lax.rem(place + step - 1, step) == first, place > 0)
+
+    @pl.when(jnp.logical_or(before, after))
+    def _():
+        column_windows(cells_ref[...].astype(F32), p2m_ref, far_rows, near_rows)
 
     @pl.when(before)
     def _():
         add_products(far, near, [0, 1], far_rows, near_rows, far_ref, near_ref)
 
-    @pl.when(jnp.logical_not(before))
+    @pl.when(after)
     def _():
         add_products(far, near, [6, 7], far_rows, near_rows, far_ref, near_ref)
 
 
 def outer_kernel(
-    cells_ref, far_part, near_part, far_ref, near_ref, p2m_ref, far_out, near_out, far_rows, near_rows
+    trade, far_part, near_part, cells_ref, far_ref, near_ref, p2m_ref, far_out, near_out, far_rows, near_rows
 ):
     far_out[...] = far_part[...]
     near_out[...] = near_part[...]
-    add_halo(cells_ref, False, far_out, near_out, far_ref, near_ref, p2m_ref, far_rows, near_rows)
+    add_halo(cells_ref, trade, far_out, near_out, far_ref, near_ref, p2m_ref, far_rows, near_rows)
 
 
 def last_kernel(
-    far_part, near_part, cells_ref, far_ref, near_ref, p2m_ref, l2p_ref,
+    trade, far_part, near_part, cells_ref, far_ref, near_ref, p2m_ref, l2p_ref,
     out_ref, far, near, far_rows, near_rows,
 ):
     pairs = out_ref.shape[2] // PAIR
     far[...] = far_part[...]
     near[...] = near_part[...]
-    add_halo(cells_ref, True, far, near, far_ref, near_ref, p2m_ref, far_rows, near_rows)
+    add_halo(cells_ref, trade, far, near, far_ref, near_ref, p2m_ref, far_rows, near_rows)
     near[...] += jnp.dot(far[...].astype(BF16), l2p_ref[...], preferred_element_type=F32)
     for x in range(4):
         for pair in range(pairs):
@@ -294,9 +301,9 @@
     )(own, far, near, p2m)
 
 
-def outer(cells, far_part, near_part, far, near, p2m):
-    return pl.pallas_call(
-        outer_kernel,
+def outer(trade, far_part, near_part, cells, far, near, p2m):
+    return pl.pallas_call(
+        functools.partial(outer_kernel, trade),
         out_shape=[pltpu.VMEM((128, PAIR), F32)] * 2,
         in_specs=[pl.BlockSpec(memory_space=pltpu.VMEM)] * 6,
         out_specs=[pl.BlockSpec(memory_space=pltpu.VMEM)] * 2,
@@ -304,12 +311,12 @@
         compiler_params=pltpu.CompilerParams(vmem_limit_bytes=VMEM_LIMIT),
         cost_estimate=pl.CostEstimate(flops=200000000, bytes_accessed=3000000, transcendentals=0),
         name="outer",
-    )(cells, far_part, near_part, far, near, p2m)
-
-
-def last(shape, cells, far_part, near_part, far, near, p2m, l2p):
-    return pl.pallas_call(
-        last_kernel,
+    )(far_part, near_part, cells, far, near, p2m)
+
+
+def last(trade, shape, far_part, near_part, cells, far, near, p2m, l2p):
+    return pl.pallas_call(
+        functools.partial(last_kernel, trade),
         out_shape=jax.ShapeDtypeStruct(shape, F32),
         in_specs=[pl.BlockSpec(memory_space=pltpu.VMEM)] * 7,
         out_specs=pl.BlockSpec(memory_space=pltpu.VMEM),
@@ -326,13 +333,15 @@
 
 
 def local(density, p2m_operator, m2l_table, near_table, l2p_operator):
-    odd, even = swapped(density, "gx", 1), swapped(density, "gx", 0)
+    odd, even = swapped(density, "gx", 1, 2), swapped(density, "gx", 0, 2)
     far, near, p2m, l2p = packed(first(), p2m_operator, m2l_table, near_table, l2p_operator)
-    own, to_odd, to_even = joined(p2m, density, odd, even)
-    odd, even = swapped(to_odd, "gy", 1), swapped(to_even, "gy", 0)
+    own, to_odd, *to_even = joined(p2m, density, odd, even)
+    trades = ((0, 4), (1, 2), (2, 4))
+    halos = [swapped(part, "gy", *trade) for part, trade in zip((to_even[0], to_odd, to_even[1]), trades)]
     parts = inner(own, far, near, p2m)
-    parts = outer(even, *parts, far, near, p2m)
-    return last(density.shape, odd, *parts, far, near, p2m, l2p)
+    for trade, halo in zip(trades[:-1], halos):
+        parts = outer(trade, *parts, halo, far, near, p2m)
+    return last(trades[-1], density.shape, *parts, halos[-1], far, near, p2m, l2p)
 
 
 def solution(mesh):

time: 12.3 us -> 11.7 us (0.951)
  the two profiles are of different devices: /device:TPU:4 before, /device:TPU:12 now
where the time goes in v6:
time: 11.7 us; the launch traced here: 11.5 us
  Pallas kernels  4.96 us (42%)
  starting transfers between devices  3.81 us (33%)
  waiting for transfers between devices  1.86 us (16%)
  local copies, waits for them, and re-layouts  0.78 us (7%)
    ppermute x5, starting transfers between devices, swapped(): return lax.ppermute(cells, AXES, pairs)  3.81 us
    ppermute x5, waiting for transfers between devices, swapped(): return lax.ppermute(cells, AXES, pairs)  1.86 us
    pallas_call x1, Pallas kernels, last(): pl.pallas_call(functools.partial(last_kernel, trade), out_shape=jax.Shape...  1.51 us
    pallas_call x1, Pallas kernels, packed(): pl.pallas_call(pack_kernel, out_shape=[pltpu.VMEM(shape, BF16) for shape...  1.34 us
    pallas_call x1, Pallas kernels, inner(): pl.pallas_call(inner_kernel, out_shape=[pltpu.VMEM((128, PAIR), F32)] * 2...  1.3 us
    unnamed x10, local copies, waits for them, and re-layouts  0.78 us
    pallas_call x2, Pallas kernels, outer(): pl.pallas_call(functools.partial(outer_kernel, trade), out_shape=[pltpu.V...  0.71 us
  transfers between devices with their start and end apart: 5, of which 2 were waited for; matrix products, arithmetic and copies ran while one was open for 0% of the time, Pallas kernels for 29%

profile of v6, /device:TPU:12, one launch (start us, length us, event | category | flops | bytes accessed | tf_op | source)
XLA Modules:
  0.0 11.5 jit_solution(13709628770018137894)
XLA Ops:
  0.0 0.0 copy-start.4
  0.0 0.0 copy-start.1
  0.0 0.0 copy-start
  0.0 0.0 copy-start.3
  0.0 0.1 collective-permute-start
  0.1 1.7 %collective-permute-start.1 = (bf16[4,4,1024]{2,1,0:T(4,128)(2,1)}, bf16[4,4,1024]{2,1,0:T(4,128)(2,1)S(1)}, u32[]{:S(2)}, u32[]{:S(2)}) collective-permute-start(bf16[4,4,1024]{2,1,0:T(4,128)(2,1)} %own_ref.1), channel_id=1, source_target_pairs={{0,4},{1,5},{2,6},{3,7},{4,0},{5,1},{6,2},{7,3},{8,12},{9,13},{10,... | collective-permute-start | bytes 98312 | tf_op jit(solution)/shard_map/ppermute | solution.py:36
  1.8 0.0 copy-start.2
  1.8 0.0 copy-done.4
  1.8 0.0 copy-done.1
  1.8 0.8 %copy-done = bf16[7,7,7,56,56]{4,3,2,1,0:T(8,128)(2,1)S(1)} copy-done((bf16[7,7,7,56,56]{4,3,2,1,0:T(8,128)(2,1)S(1)}, bf16[7,7,7,56,56]{4,3,2,1,0:T(8,128)(2,1)}, u32[]{:S(2)}) %copy-start) | copy-done | bytes 2151320
  2.6 0.0 copy-done.3
  2.6 1.3 %pack.1 = (bf16[7,7,6,64,128]{4,3,2,1,0:T(8,128)(2,1)S(1)}, bf16[3,3,2,128,128]{4,3,2,1,0:T(8,128)(2,1)S(1)}, bf16[128,128]{1,0:T(8,128)(2,1)S(1)}, bf16[128,128]{1,0:T(8,128)(2,1)S(1)}) custom-call(f32[8,128]{1,0:T(8,128)S(1)} %first.1.first_ref, bf16[56,64]{1,0:T(8,128)(2,1)S(1)} %bitcast.1, bf16[7,7,7,56,56]{4,3,2,1,0:T(8,128)(2,1)S(1)} %copy-done, ...), custom_call_target="tpu_custom_call" | custom-call | flops 4000000 | bytes 10000000 | tf_op jit(solution)/shard_map/pack/pallas_call | solution.py:101
  3.9 0.0 collective-permute-done.odd_ref
  3.9 0.0 collective-permute-done.1.even_ref
  3.9 0.0 copy-done.2
  3.9 0.1 join.1
  4.0 0.1 collective-permute-start.2
  4.1 2.0 %collective-permute-start.3 = (bf16[128,128]{1,0:T(8,128)(2,1)S(1)}, bf16[128,128]{1,0:T(8,128)(2,1)S(1)}, u32[]{:S(2)}, u32[]{:S(2)}) collective-permute-start(bf16[128,128]{1,0:T(8,128)(2,1)S(1)} %get-tuple-element.28), channel_id=1, source_target_pairs={{0,4},{1,2},{2,1},{3,7},{4,0},{5,6},{6,5},{7,3},{8,12},{9,10},{10,... | collective-permute-start | bytes 98312 | tf_op jit(solution)/shard_map/ppermute | solution.py:36
  6.1 0.0 collective-permute-start.4
  6.1 1.3 %inner.1 = (f32[128,128]{1,0:T(8,128)S(1)}, f32[128,128]{1,0:T(8,128)S(1)}) custom-call(bf16[256,128]{1,0:T(8,128)(2,1)S(1)} %get-tuple-element.20.own_ref, bf16[7,7,6,64,128]{4,3,2,1,0:T(8,128)(2,1)S(1)} %get-tuple-element.21.far_ref, bf16[3,3,2,128,128]{4,3,2,1,0:T(8,128)(2,1)S(1)} %get-tuple-element.22.near_ref, ...), custom_call_target="tpu_custom_call" | custom-call | flops 400000000 | bytes 6000000 | tf_op jit(solution)/shard_map/inner/pallas_call | solution.py:292
  7.4 0.0 collective-permute-done.2.cells_ref
  7.5 1.5 %collective-permute-done.3.cells_ref = bf16[128,128]{1,0:T(8,128)(2,1)S(1)} collective-permute-done((bf16[128,128]{1,0:T(8,128)(2,1)S(1)}, bf16[128,128]{1,0:T(8,128)(2,1)S(1)}, u32[]{:S(2)}, u32[]{:S(2)}) %collective-permute-start.3) | collective-permute-done | bytes 32800 | tf_op jit(solution)/shard_map/ppermute | solution.py:36
  9.0 0.7 %outer.3 = (f32[128,128]{1,0:T(8,128)S(1)}, f32[128,128]{1,0:T(8,128)S(1)}) custom-call(f32[128,128]{1,0:T(8,128)S(1)} %get-tuple-element.26.far_part, f32[128,128]{1,0:T(8,128)S(1)} %get-tuple-element.27.near_part, bf16[128,128]{1,0:T(8,128)(2,1)S(1)} %collective-permute-done.3.cells_ref, bf16[7,7,6,64,128]{4,3,2,1,0:T(8,128)(2,1)S(1)} %get-tuple-element.21.far_ref, ...), custom_call_target="tpu_custom_call" | custom-call | flops 200000000 | bytes 3000000 | tf_op jit(solution)/shard_map/outer/pallas_call | solution.py:305
  9.7 0.3 %collective-permute-done.4.cells_ref = bf16[128,128]{1,0:T(8,128)(2,1)S(1)} collective-permute-done((bf16[128,128]{1,0:T(8,128)(2,1)S(1)}, bf16[128,128]{1,0:T(8,128)(2,1)S(1)}, u32[]{:S(2)}, u32[]{:S(2)}) %collective-permute-start.4) | collective-permute-done | bytes 32800 | tf_op jit(solution)/shard_map/ppermute | solution.py:36
  10.0 1.5 %last.1 = f32[4,4,1024]{2,1,0:T(4,128)} custom-call(f32[128,128]{1,0:T(8,128)S(1)} %get-tuple-element.29.far_part, f32[128,128]{1,0:T(8,128)S(1)} %get-tuple-element.30.near_part, bf16[128,128]{1,0:T(8,128)(2,1)S(1)} %collective-permute-done.4.cells_ref, bf16[7,7,6,64,128]{4,3,2,1,0:T(8,128)(2,1)S(1)} %get-tuple-element.21.far_ref, ...), custom_call_target="tpu_custom_call" | custom-call | flops 200000000 | bytes 3000000 | tf_op jit(solution)/shard_map/last/pallas_call | solution.py:318
  (2 shorter events, 0.0 us)
Async XLA Ops:
  0.0 1.8 %copy-start.4 = (bf16[56,64]{1,0:T(8,128)(2,1)S(1)}, bf16[56,64]{1,0:T(8,128)(2,1)}, u32[]{:S(2)}) copy-start(bf16[56,64]{1,0:T(8,128)(2,1)} %l2p_ref.1) | copy-start | bytes 21508
  0.0 1.8 %copy-start.1 = (bf16[3,3,3,64,64]{4,3,2,1,0:T(8,128)(2,1)S(1)}, bf16[3,3,3,64,64]{4,3,2,1,0:T(8,128)(2,1)}, u32[]{:S(2)}) copy-start(bf16[3,3,3,64,64]{4,3,2,1,0:T(8,128)(2,1)} %near_ref.1) | copy-start | bytes 663556
  0.0 2.6 %copy-start = (bf16[7,7,7,56,56]{4,3,2,1,0:T(8,128)(2,1)S(1)}, bf16[7,7,7,56,56]{4,3,2,1,0:T(8,128)(2,1)}, u32[]{:S(2)}) copy-start(bf16[7,7,7,56,56]{4,3,2,1,0:T(8,128)(2,1)} %m2l_ref.1) | copy-start | bytes 6453892
  0.0 2.5 %copy-start.3 = (bf16[64,56]{0,1:T(8,128)(2,1)S(1)}, bf16[64,56]{0,1:T(8,128)(2,1)}, u32[]{:S(2)}) copy-start(bf16[64,56]{0,1:T(8,128)(2,1)} %param.6) | copy-start | bytes 21508
  0.0 3.9 %collective-permute-start = (bf16[4,4,1024]{2,1,0:T(4,128)(2,1)}, bf16[4,4,1024]{2,1,0:T(4,128)(2,1)S(1)}, u32[]{:S(2)}, u32[]{:S(2)}) collective-permute-start(bf16[4,4,1024]{2,1,0:T(4,128)(2,1)} %own_ref.1), channel_id=1, source_target_pairs={{0,1},{1,0},{2,3},{3,2},{4,8},{5,9},{6,10},{7,11},{8,4},{9,5},{10,... | collective-permute-start | bytes 98312 | tf_op jit(solution)/shard_map/ppermute | solution.py:36
  0.1 3.8 %collective-permute-start.1 = (bf16[4,4,1024]{2,1,0:T(4,128)(2,1)}, bf16[4,4,1024]{2,1,0:T(4,128)(2,1)S(1)}, u32[]{:S(2)}, u32[]{:S(2)}) collective-permute-start(bf16[4,4,1024]{2,1,0:T(4,128)(2,1)} %own_ref.1), channel_id=1, source_target_pairs={{0,4},{1,5},{2,6},{3,7},{4,0},{5,1},{6,2},{7,3},{8,12},{9,13},{10,... | collective-permute-start | bytes 98312 | tf_op jit(solution)/shard_map/ppermute | solution.py:36
  1.8 2.1 %copy-start.2 = (bf16[4,4,1024]{2,1,0:T(4,128)(2,1)S(1)}, bf16[4,4,1024]{2,1,0:T(4,128)(2,1)}, u32[]{:S(2)}) copy-start(bf16[4,4,1024]{2,1,0:T(4,128)(2,1)} %own_ref.1) | copy-start | bytes 98308
  4.0 3.4 %collective-permute-start.2 = (bf16[128,128]{1,0:T(8,128)(2,1)S(1)}, bf16[128,128]{1,0:T(8,128)(2,1)S(1)}, u32[]{:S(2)}, u32[]{:S(2)}) collective-permute-start(bf16[128,128]{1,0:T(8,128)(2,1)S(1)} %get-tuple-element.25), channel_id=1, source_target_pairs={{0,1},{1,0},{2,6},{3,7},{4,5},{5,4},{6,2},{7,3},{8,9},{9,8},{10,14... | collective-permute-start | bytes 98312 | tf_op jit(solution)/shard_map/ppermute | solution.py:36
  4.1 4.9 %collective-permute-start.3 = (bf16[128,128]{1,0:T(8,128)(2,1)S(1)}, bf16[128,128]{1,0:T(8,128)(2,1)S(1)}, u32[]{:S(2)}, u32[]{:S(2)}) collective-permute-start(bf16[128,128]{1,0:T(8,128)(2,1)S(1)} %get-tuple-element.28), channel_id=1, source_target_pairs={{0,4},{1,2},{2,1},{3,7},{4,0},{5,6},{6,5},{7,3},{8,12},{9,10},{10,... | collective-permute-start | bytes 98312 | tf_op jit(solution)/shard_map/ppermute | solution.py:36
  6.1 3.9 %collective-permute-start.4 = (bf16[128,128]{1,0:T(8,128)(2,1)S(1)}, bf16[128,128]{1,0:T(8,128)(2,1)S(1)}, u32[]{:S(2)}, u32[]{:S(2)}) collective-permute-start(bf16[128,128]{1,0:T(8,128)(2,1)S(1)} %get-tuple-element.31), channel_id=1, source_target_pairs={{0,4},{1,5},{2,3},{3,2},{4,0},{5,1},{6,7},{7,6},{8,12},{9,13},{10,... | collective-permute-start | bytes 98312 | tf_op jit(solution)/shard_map/ppermute | solution.py:36

commit v7 on v6

--- a/solution.py
+++ b/solution.py
@@ -60,23 +60,21 @@
     )()
 
 
-def pack_kernel(first_ref, p2m_ref, m2l_ref, near_ref, l2p_ref, far_out, near_out, p2m_out, l2p_out):
+def far_blocks(m2l_ref, offset_x, offset_y):
+    inner = 2 <= offset_x <= 4 and 2 <= offset_y <= 4
     blank = jnp.zeros((WIDTH, WIDTH), BF16)
-
-    def far_blocks(offset_x, offset_y):
-        inner = 2 <= offset_x <= 4 and 2 <= offset_y <= 4
-        entries = []
-        for offset_z in range(7):
-            if inner and 2 <= offset_z <= 4:
-                entries.append(blank)
-            else:
-                entries.append(square(m2l_ref[offset_x, offset_y, offset_z]))
-        for s in range(6):
-            far_out[offset_x, offset_y, s] = jnp.concatenate([entries[s + 1], entries[s]], axis=1)
-
-    for offset_x in range(7):
-        for offset_y in range(7):
-            far_blocks(offset_x, offset_y)
+    entries = [
+        blank if inner and 2 <= offset_z <= 4 else square(m2l_ref[offset_x, offset_y, offset_z])
+        for offset_z in range(7)
+    ]
+    blocks = [jnp.concatenate([entries[s + 1], entries[s]], axis=1) for s in range(6)]
+    return [
+        None if inner and b == 1 else jnp.concatenate(blocks[2 * b : 2 * b + 2], axis=0) for b in range(3)
+    ]
+
+
+def pack_kernel(first_ref, p2m_ref, near_ref, l2p_ref, near_out, p2m_out, l2p_out):
+    blank = jnp.zeros((WIDTH, WIDTH), BF16)
     for offset_x in range(3):
         for offset_y in range(3):
             before, same, after = [near_ref[offset_x, offset_y, z] for z in range(3)]
@@ -96,17 +94,17 @@
     )
 
 
-def packed(start, p2m_operator, m2l_table, near_table, l2p_operator):
-    shapes = [(7, 7, 6, WIDTH, PAIR), (3, 3, 2, PAIR, PAIR), (PAIR, PAIR), (PAIR, PAIR)]
+def packed(start, p2m_operator, near_table, l2p_operator):
+    shapes = [(3, 3, 2, PAIR, PAIR), (PAIR, PAIR), (PAIR, PAIR)]
     return pl.pallas_call(
         pack_kernel,
         out_shape=[pltpu.VMEM(shape, BF16) for shape in shapes],
-        in_specs=[pl.BlockSpec(memory_space=pltpu.VMEM)] * 5,
-        out_specs=[pl.BlockSpec(memory_space=pltpu.VMEM)] * 4,
-        compiler_params=pltpu.CompilerParams(vmem_limit_bytes=VMEM_LIMIT),
+        in_specs=[pl.BlockSpec(memory_space=pltpu.VMEM)] * 4,
+        out_specs=[pl.BlockSpec(memory_space=pltpu.VMEM)] * 3,
+        compiler_params=pltpu.CompilerParams(vmem_limit_bytes=SMALL_LIMIT),
         cost_estimate=pl.CostEstimate(flops=4000000, bytes_accessed=10000000, transcendentals=0),
         name="pack",
-    )(start, p2m_operator.T, m2l_table, near_table, l2p_operator)
+    )(start, p2m_operator.T, near_table, l2p_operator)
 
 
 def from_neighbours(axis, even_low, odd_low, even_high, odd_high):
@@ -195,57 +193,50 @@
                 ].astype(BF16)
 
 
-def spans(places, first, offset, parity):
-    found = [
-        (target, places.index(target + offset + first))
-        for target in range(4)
-        if target + offset + first in places
-        and not (parity and ((offset == 0 and target % 2 == 0) or (offset == 6 and target % 2 == 1)))
-    ]
-    return found
-
-
-def add_products(far, near, places, far_rows, near_rows, far_ref, near_ref):
-    for offset_y in range(7):
-        found = spans(places, -1, offset_y, True)
-        if not found:
-            continue
-        rows = slice(32 * found[0][1], 32 * found[-1][1] + 32)
-        chunks, weights = [], []
-        for offset_x in range(7):
-            inner = 2 <= offset_x <= 4 and 2 <= offset_y <= 4
-            for b in range(3):
-                if inner and b == 1:
-                    continue
+def far_product(far_rows, rows, blocks):
+    chunks, weights = [], []
+    for offset_x in range(7):
+        for b, block in enumerate(blocks(offset_x)):
+            if block is not None:
                 chunks.append(far_rows[offset_x, b, rows])
-                weights.append(far_ref[offset_x, offset_y, 2 * b : 2 * b + 2].reshape(PAIR, PAIR))
-        product = jnp.dot(
-            jnp.concatenate(chunks, axis=1), jnp.concatenate(weights, axis=0), preferred_element_type=F32
-        )
-        for index, (target, _) in enumerate(found):
-            far[32 * target : 32 * target + 32] += product[32 * index : 32 * index + 32]
-    for offset_y in range(3):
-        found = spans(places, 1, offset_y, False)
-        if not found:
-            continue
-        rows = slice(32 * found[0][1], 32 * found[-1][1] + 32)
-        chunks = [near_rows[offset_x, k, rows] for offset_x in range(3) for k in range(2)]
-        weights = [near_ref[offset_x, offset_y].reshape(2 * PAIR, PAIR) for offset_x in range(3)]
-        product = jnp.dot(
-            jnp.concatenate(chunks, axis=1), jnp.concatenate(weights, axis=0), preferred_element_type=F32
-        )
-        for index, (target, _) in enumerate(found):
-            near[32 * target : 32 * target + 32] += product[32 * index : 32 * index + 32]
-
-
-def inner_kernel(own_ref, far_ref, near_ref, p2m_ref, far_out, near_out, far_rows, near_rows):
+                weights.append(block)
+    return jnp.dot(
+        jnp.concatenate(chunks, axis=1), jnp.concatenate(weights, axis=0), preferred_element_type=F32
+    )
+
+
+def near_product(near_rows, rows, near_ref, offset_y):
+    chunks = [near_rows[offset_x, k, rows] for offset_x in range(3) for k in range(2)]
+    weights = [near_ref[offset_x, offset_y].reshape(2 * PAIR, PAIR) for offset_x in range(3)]
+    return jnp.dot(
+        jnp.concatenate(chunks, axis=1), jnp.concatenate(weights, axis=0), preferred_element_type=F32
+    )
+
+
+def inner_kernel(own_ref, m2l_ref, near_ref, p2m_ref, far_out, near_out, table_out, far_rows, near_rows):
     column_windows(own_ref[...].astype(F32), p2m_ref, far_rows, near_rows)
     far_out[...] = jnp.zeros_like(far_out)
-    near_out[...] = jnp.zeros_like(near_out)
-    add_products(far_out, near_out, [2, 3, 4, 5], far_rows, near_rows, far_ref, near_ref)
-
-
-def add_halo(cells_ref, trade, far, near, far_ref, near_ref, p2m_ref, far_rows, near_rows):
+    for offset_y in range(7):
+        targets = [3] if offset_y == 0 else [0] if offset_y == 6 else [
+            target for target in range(4) if 0 <= target + offset_y - 3 <= 3
+        ]
+        start = targets[0] + offset_y - 3
+
+        def packing(offset_x):
+            blocks = far_blocks(m2l_ref, offset_x, offset_y)
+            if offset_y != 3:
+                for b, block in enumerate(blocks):
+                    table_out[offset_x, offset_y, b] = jnp.zeros((PAIR, PAIR), BF16) if block is None else block
+            return blocks
+
+        product = far_product(far_rows, slice(32 * start, 32 * (start + len(targets))), packing)
+        far_out[32 * targets[0] : 32 * (targets[-1] + 1)] += product
+    near_out[...] = near_product(near_rows, slice(0, 128), near_ref, 1)
+    near_out[32:128] += near_product(near_rows, slice(0, 96), near_ref, 0)
+    near_out[0:96] += near_product(near_rows, slice(32, 128), near_ref, 2)
+
+
+def add_halo(cells_ref, trade, far, near, table_ref, near_ref, p2m_ref, far_rows, near_rows):
     place = lax.axis_index("gy")
     first, step = trade
     after = jnp.logical_and(lax.rem(place, step) == first, place + 1 < lax.axis_size("gy"))
@@ -253,15 +244,18 @@
 
     @pl.when(jnp.logical_or(before, after))
     def _():
+        side = jnp.where(before, 0, 1)
         column_windows(cells_ref[...].astype(F32), p2m_ref, far_rows, near_rows)
 
-    @pl.when(before)
-    def _():
-        add_products(far, near, [0, 1], far_rows, near_rows, far_ref, near_ref)
-
-    @pl.when(after)
-    def _():
-        add_products(far, near, [6, 7], far_rows, near_rows, far_ref, near_ref)
+        def blocks(index):
+            return lambda offset_x: [table_ref[offset_x, 4 * side + index, b] for b in range(3)]
+
+        pair = far_product(far_rows, slice(0, 64), blocks(1))
+        odd = far_product(far_rows, slice(0, 32), blocks(0))
+        even = far_product(far_rows, slice(32, 64), blocks(2))
+        far[pl.ds(pl.multiple_of(64 * side, 64), 64)] += pair + jnp.concatenate([even, odd], axis=0)
+        rows = pl.ds(pl.multiple_of(32 - 32 * side, 32), 32)
+        near[pl.ds(pl.multiple_of(96 * side, 32), 32)] += near_product(near_rows, rows, near_ref, 2 * side)
 
 
 def outer_kernel(
@@ -288,17 +282,21 @@
             ]
 
 
-def inner(own, far, near, p2m):
+def inner(own, m2l_table, near, p2m):
     return pl.pallas_call(
         inner_kernel,
-        out_shape=[pltpu.VMEM((128, PAIR), F32)] * 2,
+        out_shape=[
+            pltpu.VMEM((128, PAIR), F32),
+            pltpu.VMEM((128, PAIR), F32),
+            pltpu.VMEM((7, 7, 3, PAIR, PAIR), BF16),
+        ],
         in_specs=[pl.BlockSpec(memory_space=pltpu.VMEM)] * 4,
-        out_specs=[pl.BlockSpec(memory_space=pltpu.VMEM)] * 2,
+        out_specs=[pl.BlockSpec(memory_space=pltpu.VMEM)] * 3,
         scratch_shapes=[pltpu.VMEM((7, 3, 128, PAIR), BF16), pltpu.VMEM((3, 2, 128, PAIR), BF16)],
         compiler_params=pltpu.CompilerParams(vmem_limit_bytes=VMEM_LIMIT),
         cost_estimate=pl.CostEstimate(flops=400000000, bytes_accessed=6000000, transcendentals=0),
         name="inner",
-    )(own, far, near, p2m)
+    )(own, m2l_table, near, p2m)
 
 
 def outer(trade, far_part, near_part, cells, far, near, p2m):
@@ -334,11 +332,11 @@
 
 def local(density, p2m_operator, m2l_table, near_table, l2p_operator):
     odd, even = swapped(density, "gx", 1, 2), swapped(density, "gx", 0, 2)
-    far, near, p2m, l2p = packed(first(), p2m_operator, m2l_table, near_table, l2p_operator)
+    near, p2m, l2p = packed(first(), p2m_operator, near_table, l2p_operator)
     own, to_odd, *to_even = joined(p2m, density, odd, even)
     trades = ((0, 4), (1, 2), (2, 4))
     halos = [swapped(part, "gy", *trade) for part, trade in zip((to_even[0], to_odd, to_even[1]), trades)]
-    parts = inner(own, far, near, p2m)
+    *parts, far = inner(own, m2l_table, near, p2m)
     for trade, halo in zip(trades[:-1], halos):
         parts = outer(trade, *parts, halo, far, near, p2m)
     return last(trades[-1], density.shape, *parts, halos[-1], far, near, p2m, l2p)

time: 11.7 us -> 11.5 us (0.983)
  the two profiles are of different devices: /device:TPU:12 before, /device:TPU:4 now
where the time goes in v7:
time: 11.5 us; the launch traced here: 11.4 us
  Pallas kernels  4.14 us (36%)
  starting transfers between devices  3.82 us (33%)
  waiting for transfers between devices  3.31 us (29%)
    ppermute x5, starting transfers between devices, swapped(): return lax.ppermute(cells, AXES, pairs)  3.82 us
    ppermute x5, waiting for transfers between devices, swapped(): return lax.ppermute(cells, AXES, pairs)  3.31 us
    pallas_call x1, Pallas kernels, inner(): pl.pallas_call(inner_kernel, out_shape=[pltpu.VMEM((128, PAIR), F32), plt...  1.76 us
    pallas_call x1, Pallas kernels, last(): pl.pallas_call(functools.partial(last_kernel, trade), out_shape=jax.Shape...  1.44 us
    pallas_call x2, Pallas kernels, outer(): pl.pallas_call(functools.partial(outer_kernel, trade), out_shape=[pltpu.V...  0.64 us
  transfers between devices with their start and end apart: 5, of which 2 were waited for; matrix products, arithmetic and copies ran while one was open for 0% of the time, Pallas kernels for 23%

profile of v7, /device:TPU:4, one launch (start us, length us, event | category | flops | bytes accessed | tf_op | source)
XLA Modules:
  0.0 11.4 jit_solution(2222548870729971309)
XLA Ops:
  0.0 0.0 copy-start.2
  0.0 0.0 copy-start.4
  0.0 0.0 copy-start.1
  0.0 0.0 copy-start.3
  0.0 0.0 copy-start
  0.0 1.6 %collective-permute-start = (bf16[4,4,1024]{2,1,0:T(4,128)(2,1)}, bf16[4,4,1024]{2,1,0:T(4,128)(2,1)S(1)}, u32[]{:S(2)}, u32[]{:S(2)}) collective-permute-start(bf16[4,4,1024]{2,1,0:T(4,128)(2,1)} %own_ref.1), channel_id=1, source_target_pairs={{0,1},{1,0},{2,3},{3,2},{4,8},{5,9},{6,10},{7,11},{8,4},{9,5},{10,... | collective-permute-start | bytes 98312 | tf_op jit(solution)/shard_map/ppermute | solution.py:36
  1.6 0.2 %collective-permute-start.1 = (bf16[4,4,1024]{2,1,0:T(4,128)(2,1)}, bf16[4,4,1024]{2,1,0:T(4,128)(2,1)S(1)}, u32[]{:S(2)}, u32[]{:S(2)}) collective-permute-start(bf16[4,4,1024]{2,1,0:T(4,128)(2,1)} %own_ref.1), channel_id=1, source_target_pairs={{0,4},{1,5},{2,6},{3,7},{4,0},{5,1},{6,2},{7,3},{8,12},{9,13},{10,... | collective-permute-start | bytes 98312 | tf_op jit(solution)/shard_map/ppermute | solution.py:36
  1.8 0.0 copy-done.4
  1.8 0.0 copy-done.1
  1.8 0.0 copy-done.3
  1.8 0.2 %pack.1 = (bf16[3,3,2,128,128]{4,3,2,1,0:T(8,128)(2,1)S(1)}, bf16[128,128]{1,0:T(8,128)(2,1)S(1)}, bf16[128,128]{1,0:T(8,128)(2,1)S(1)}) custom-call(f32[8,128]{1,0:T(8,128)S(1)} %first.1.first_ref, bf16[56,64]{1,0:T(8,128)(2,1)S(1)} %bitcast.1, bf16[3,3,3,64,64]{4,3,2,1,0:T(8,128)(2,1)S(1)} %copy-done.1, bf16[56,64]{1,0:T(8,128)(2,1)S(1)} %copy-done.4), custom_call_target="tpu_custom_call" | custom-call | flops 4000000 | bytes 10000000 | tf_op jit(solution)/shard_map/pack/pallas_call | solution.py:99
  2.0 2.2 %collective-permute-done.odd_ref = bf16[4,4,1024]{2,1,0:T(4,128)(2,1)S(1)} collective-permute-done((bf16[4,4,1024]{2,1,0:T(4,128)(2,1)}, bf16[4,4,1024]{2,1,0:T(4,128)(2,1)S(1)}, u32[]{:S(2)}, u32[]{:S(2)}) %collective-permute-start) | collective-permute-done | bytes 32800 | tf_op jit(solution)/shard_map/ppermute | solution.py:36
  4.2 0.0 collective-permute-done.1.even_ref
  4.2 0.0 copy-done.2
  4.2 0.1 join.1
  4.3 0.1 collective-permute-start.2
  4.4 1.5 %collective-permute-start.3 = (bf16[128,128]{1,0:T(8,128)(2,1)S(1)}, bf16[128,128]{1,0:T(8,128)(2,1)S(1)}, u32[]{:S(2)}, u32[]{:S(2)}) collective-permute-start(bf16[128,128]{1,0:T(8,128)(2,1)S(1)} %get-tuple-element.28), channel_id=1, source_target_pairs={{0,4},{1,2},{2,1},{3,7},{4,0},{5,6},{6,5},{7,3},{8,12},{9,10},{10,... | collective-permute-start | bytes 98312 | tf_op jit(solution)/shard_map/ppermute | solution.py:36
  5.9 0.5 %collective-permute-start.4 = (bf16[128,128]{1,0:T(8,128)(2,1)S(1)}, bf16[128,128]{1,0:T(8,128)(2,1)S(1)}, u32[]{:S(2)}, u32[]{:S(2)}) collective-permute-start(bf16[128,128]{1,0:T(8,128)(2,1)S(1)} %get-tuple-element.31), channel_id=1, source_target_pairs={{0,4},{1,5},{2,3},{3,2},{4,0},{5,1},{6,7},{7,6},{8,12},{9,13},{10,... | collective-permute-start | bytes 98312 | tf_op jit(solution)/shard_map/ppermute | solution.py:36
  6.4 0.0 copy-done
  6.4 1.8 %inner.1 = (f32[128,128]{1,0:T(8,128)S(1)}, f32[128,128]{1,0:T(8,128)S(1)}, bf16[7,7,3,128,128]{4,3,2,1,0:T(8,128)(2,1)S(1)}) custom-call(bf16[256,128]{1,0:T(8,128)(2,1)S(1)} %get-tuple-element.20.own_ref, bf16[7,7,7,56,56]{4,3,2,1,0:T(8,128)(2,1)S(1)} %copy-done, bf16[3,3,2,128,128]{4,3,2,1,0:T(8,128)(2,1)S(1)} %get-tuple-element.21.near_ref, ...), custom_call_target="tpu_custom_call" | custom-call | flops 400000000 | bytes 6000000 | tf_op jit(solution)/shard_map/inner/pallas_call | solution.py:286
  8.2 0.0 collective-permute-done.2.cells_ref
  8.2 1.1 %collective-permute-done.3.cells_ref = bf16[128,128]{1,0:T(8,128)(2,1)S(1)} collective-permute-done((bf16[128,128]{1,0:T(8,128)(2,1)S(1)}, bf16[128,128]{1,0:T(8,128)(2,1)S(1)}, u32[]{:S(2)}, u32[]{:S(2)}) %collective-permute-start.3) | collective-permute-done | bytes 32800 | tf_op jit(solution)/shard_map/ppermute | solution.py:36
  9.3 0.6 %outer.3 = (f32[128,128]{1,0:T(8,128)S(1)}, f32[128,128]{1,0:T(8,128)S(1)}) custom-call(f32[128,128]{1,0:T(8,128)S(1)} %get-tuple-element.26.far_part, f32[128,128]{1,0:T(8,128)S(1)} %get-tuple-element.27.near_part, bf16[128,128]{1,0:T(8,128)(2,1)S(1)} %collective-permute-done.3.cells_ref, bf16[7,7,3,128,128]{4,3,2,1,0:T(8,128)(2,1)S(1)} %get-tuple-element.25.far_ref, ...), custom_call_target="tpu_custom_call" | custom-call | flops 200000000 | bytes 3000000 | tf_op jit(solution)/shard_map/outer/pallas_call | solution.py:303
  9.9 0.0 collective-permute-done.4.cells_ref
  9.9 1.4 %last.1 = f32[4,4,1024]{2,1,0:T(4,128)} custom-call(f32[128,128]{1,0:T(8,128)S(1)} %get-tuple-element.29.far_part, f32[128,128]{1,0:T(8,128)S(1)} %get-tuple-element.30.near_part, bf16[128,128]{1,0:T(8,128)(2,1)S(1)} %collective-permute-done.4.cells_ref, bf16[7,7,3,128,128]{4,3,2,1,0:T(8,128)(2,1)S(1)} %get-tuple-element.25.far_ref, ...), custom_call_target="tpu_custom_call" | custom-call | flops 200000000 | bytes 3000000 | tf_op jit(solution)/shard_map/last/pallas_call | solution.py:316
  (2 shorter events, 0.0 us)
Async XLA Ops:
  0.0 4.2 %copy-start.2 = (bf16[4,4,1024]{2,1,0:T(4,128)(2,1)S(1)}, bf16[4,4,1024]{2,1,0:T(4,128)(2,1)}, u32[]{:S(2)}) copy-start(bf16[4,4,1024]{2,1,0:T(4,128)(2,1)} %own_ref.1) | copy-start | bytes 98308
  0.0 1.8 %copy-start.4 = (bf16[56,64]{1,0:T(8,128)(2,1)S(1)}, bf16[56,64]{1,0:T(8,128)(2,1)}, u32[]{:S(2)}) copy-start(bf16[56,64]{1,0:T(8,128)(2,1)} %l2p_ref.1) | copy-start | bytes 21508
  0.0 1.8 %copy-start.1 = (bf16[3,3,3,64,64]{4,3,2,1,0:T(8,128)(2,1)S(1)}, bf16[3,3,3,64,64]{4,3,2,1,0:T(8,128)(2,1)}, u32[]{:S(2)}) copy-start(bf16[3,3,3,64,64]{4,3,2,1,0:T(8,128)(2,1)} %near_ref.1) | copy-start | bytes 663556
  0.0 1.8 %copy-start.3 = (bf16[64,56]{0,1:T(8,128)(2,1)S(1)}, bf16[64,56]{0,1:T(8,128)(2,1)}, u32[]{:S(2)}) copy-start(bf16[64,56]{0,1:T(8,128)(2,1)} %param.6) | copy-start | bytes 21508
  0.0 6.4 %copy-start = (bf16[7,7,7,56,56]{4,3,2,1,0:T(8,128)(2,1)S(1)}, bf16[7,7,7,56,56]{4,3,2,1,0:T(8,128)(2,1)}, u32[]{:S(2)}) copy-start(bf16[7,7,7,56,56]{4,3,2,1,0:T(8,128)(2,1)} %m2l_ref.1) | copy-start | bytes 6453892
  0.0 4.2 %collective-permute-start = (bf16[4,4,1024]{2,1,0:T(4,128)(2,1)}, bf16[4,4,1024]{2,1,0:T(4,128)(2,1)S(1)}, u32[]{:S(2)}, u32[]{:S(2)}) collective-permute-start(bf16[4,4,1024]{2,1,0:T(4,128)(2,1)} %own_ref.1), channel_id=1, source_target_pairs={{0,1},{1,0},{2,3},{3,2},{4,8},{5,9},{6,10},{7,11},{8,4},{9,5},{10,... | collective-permute-start | bytes 98312 | tf_op jit(solution)/shard_map/ppermute | solution.py:36
  1.6 2.6 %collective-permute-start.1 = (bf16[4,4,1024]{2,1,0:T(4,128)(2,1)}, bf16[4,4,1024]{2,1,0:T(4,128)(2,1)S(1)}, u32[]{:S(2)}, u32[]{:S(2)}) collective-permute-start(bf16[4,4,1024]{2,1,0:T(4,128)(2,1)} %own_ref.1), channel_id=1, source_target_pairs={{0,4},{1,5},{2,6},{3,7},{4,0},{5,1},{6,2},{7,3},{8,12},{9,13},{10,... | collective-permute-start | bytes 98312 | tf_op jit(solution)/shard_map/ppermute | solution.py:36
  4.3 3.8 %collective-permute-start.2 = (bf16[128,128]{1,0:T(8,128)(2,1)S(1)}, bf16[128,128]{1,0:T(8,128)(2,1)S(1)}, u32[]{:S(2)}, u32[]{:S(2)}) collective-permute-start(bf16[128,128]{1,0:T(8,128)(2,1)S(1)} %get-tuple-element.24), channel_id=1, source_target_pairs={{0,1},{1,0},{2,6},{3,7},{4,5},{5,4},{6,2},{7,3},{8,9},{9,8},{10,14... | collective-permute-start | bytes 98312 | tf_op jit(solution)/shard_map/ppermute | solution.py:36
  4.4 4.9 %collective-permute-start.3 = (bf16[128,128]{1,0:T(8,128)(2,1)S(1)}, bf16[128,128]{1,0:T(8,128)(2,1)S(1)}, u32[]{:S(2)}, u32[]{:S(2)}) collective-permute-start(bf16[128,128]{1,0:T(8,128)(2,1)S(1)} %get-tuple-element.28), channel_id=1, source_target_pairs={{0,4},{1,2},{2,1},{3,7},{4,0},{5,6},{6,5},{7,3},{8,12},{9,10},{10,... | collective-permute-start | bytes 98312 | tf_op jit(solution)/shard_map/ppermute | solution.py:36
  5.9 4.0 %collective-permute-start.4 = (bf16[128,128]{1,0:T(8,128)(2,1)S(1)}, bf16[128,128]{1,0:T(8,128)(2,1)S(1)}, u32[]{:S(2)}, u32[]{:S(2)}) collective-permute-start(bf16[128,128]{1,0:T(8,128)(2,1)S(1)} %get-tuple-element.31), channel_id=1, source_target_pairs={{0,4},{1,5},{2,3},{3,2},{4,0},{5,1},{6,7},{7,6},{8,12},{9,13},{10,... | collective-permute-start | bytes 98312 | tf_op jit(solution)/shard_map/ppermute | solution.py:36

commit v8 on v7

--- a/solution.py
+++ b/solution.py
@@ -116,7 +116,10 @@
     return low, high
 
 
-def join_kernel(after_ref, own_ref, odd_ref, even_ref, own_out, odd_out, even_out, again_out, rows_ref):
+def join_kernel(
+    trade, own_ref, odd_ref, even_ref, m2l_ref, near_ref, p2m_ref,
+    own_out, odd_out, even_out, sums_out, rows_ref, far_rows, near_rows,
+):
     pairs = own_ref.shape[2] // PAIR
     for pair in range(pairs):
         lanes = slice(pair * PAIR, (pair + 1) * PAIR)
@@ -141,20 +144,33 @@
     head, tail = rows[:128], rows[128:]
     even_out[...] = jnp.where(lower, tail, head).astype(BF16)
     odd_out[...] = jnp.where(lower, head, tail).astype(BF16)
-    again_out[...] = jnp.where(lower, tail, head).astype(BF16)
-
-
-def joined(after, own, odd, even):
-    return pl.pallas_call(
-        join_kernel,
+    sums_out[...] = jnp.where(lower, tail, head).astype(BF16)
+    before, _ = partners(trade)
+
+    @pl.when(before)
+    def _():
+        column_windows(rows_ref[:128], p2m_ref, far_rows, near_rows)
+        sums = halo_sums(lambda offset_x, index: far_blocks(m2l_ref, offset_x, 4 + index), far_rows)
+        sums_out[:64] = sums.astype(BF16)
+        sums_out[64:96] = near_product(near_rows, slice(0, 32), near_ref, 2).astype(BF16)
+        sums_out[96:] = jnp.zeros((32, PAIR), BF16)
+
+
+def joined(trade, own, odd, even, m2l_table, near, p2m):
+    return pl.pallas_call(
+        functools.partial(join_kernel, trade),
         out_shape=[pltpu.VMEM((rows, PAIR), BF16) for rows in (256, 128, 128, 128)],
-        in_specs=[pl.BlockSpec(memory_space=pltpu.VMEM)] * 4,
+        in_specs=[pl.BlockSpec(memory_space=pltpu.VMEM)] * 6,
         out_specs=[pl.BlockSpec(memory_space=pltpu.VMEM)] * 4,
-        scratch_shapes=[pltpu.VMEM((256, PAIR), F32)],
+        scratch_shapes=[
+            pltpu.VMEM((256, PAIR), F32),
+            pltpu.VMEM((7, 3, 64, PAIR), BF16),
+            pltpu.VMEM((3, 2, 64, PAIR), BF16),
+        ],
         compiler_params=pltpu.CompilerParams(vmem_limit_bytes=SMALL_LIMIT),
         cost_estimate=pl.CostEstimate(flops=1000000, bytes_accessed=100000, transcendentals=0),
         name="join",
-    )(after, own, odd, even)
+    )(own, odd, even, m2l_table, near, p2m)
 
 
 def shifted(rows):
@@ -236,26 +252,33 @@
     near_out[0:96] += near_product(near_rows, slice(32, 128), near_ref, 2)
 
 
-def add_halo(cells_ref, trade, far, near, table_ref, near_ref, p2m_ref, far_rows, near_rows):
+def halo_sums(blocks, far_rows):
+    pair = far_product(far_rows, slice(0, 64), lambda offset_x: blocks(offset_x, 1))
+    odd = far_product(far_rows, slice(0, 32), lambda offset_x: blocks(offset_x, 0))
+    even = far_product(far_rows, slice(32, 64), lambda offset_x: blocks(offset_x, 2))
+    return pair + jnp.concatenate([even, odd], axis=0)
+
+
+def add_halo(cells_ref, before, after, far, near, table_ref, near_ref, p2m_ref, far_rows, near_rows):
+    @pl.when(jnp.logical_or(before, after))
+    def _():
+        side = jnp.where(before, 0, 1)
+        column_windows(cells_ref[...].astype(F32), p2m_ref, far_rows, near_rows)
+
+        def blocks(offset_x, index):
+            return [table_ref[offset_x, 4 * side + index, b] for b in range(3)]
+
+        far[pl.ds(pl.multiple_of(64 * side, 64), 64)] += halo_sums(blocks, far_rows)
+        rows = pl.ds(pl.multiple_of(32 - 32 * side, 32), 32)
+        near[pl.ds(pl.multiple_of(96 * side, 32), 32)] += near_product(near_rows, rows, near_ref, 2 * side)
+
+
+def partners(trade):
     place = lax.axis_index("gy")
     first, step = trade
     after = jnp.logical_and(lax.rem(place, step) == first, place + 1 < lax.axis_size("gy"))
     before = jnp.logical_and(lax.rem(place + step - 1, step) == first, place > 0)
-
-    @pl.when(jnp.logical_or(before, after))
-    def _():
-        side = jnp.where(before, 0, 1)
-        column_windows(cells_ref[...].astype(F32), p2m_ref, far_rows, near_rows)
-
-        def blocks(index):
-            return lambda offset_x: [table_ref[offset_x, 4 * side + index, b] for b in range(3)]
-
-        pair = far_product(far_rows, slice(0, 64), blocks(1))
-        odd = far_product(far_rows, slice(0, 32), blocks(0))
-        even = far_product(far_rows, slice(32, 64), blocks(2))
-        far[pl.ds(pl.multiple_of(64 * side, 64), 64)] += pair + jnp.concatenate([even, odd], axis=0)
-        rows = pl.ds(pl.multiple_of(32 - 32 * side, 32), 32)
-        near[pl.ds(pl.multiple_of(96 * side, 32), 32)] += near_product(near_rows, rows, near_ref, 2 * side)
+    return before, after
 
 
 def outer_kernel(
@@ -263,7 +286,7 @@
 ):
     far_out[...] = far_part[...]
     near_out[...] = near_part[...]
-    add_halo(cells_ref, trade, far_out, near_out, far_ref, near_ref, p2m_ref, far_rows, near_rows)
+    add_halo(cells_ref, *partners(trade), far_out, near_out, far_ref, near_ref, p2m_ref, far_rows, near_rows)
 
 
 def last_kernel(
@@ -273,7 +296,14 @@
     pairs = out_ref.shape[2] // PAIR
     far[...] = far_part[...]
     near[...] = near_part[...]
-    add_halo(cells_ref, trade, far, near, far_ref, near_ref, p2m_ref, far_rows, near_rows)
+    before, after = partners(trade)
+    add_halo(cells_ref, before, False, far, near, far_ref, near_ref, p2m_ref, far_rows, near_rows)
+
+    @pl.when(after)
+    def _():
+        far[64:128] += cells_ref[:64].astype(F32)
+        near[96:128] += cells_ref[64:96].astype(F32)
+
     near[...] += jnp.dot(far[...].astype(BF16), l2p_ref[...], preferred_element_type=F32)
     for x in range(4):
         for pair in range(pairs):
@@ -333,9 +363,9 @@
 def local(density, p2m_operator, m2l_table, near_table, l2p_operator):
     odd, even = swapped(density, "gx", 1, 2), swapped(density, "gx", 0, 2)
     near, p2m, l2p = packed(first(), p2m_operator, near_table, l2p_operator)
-    own, to_odd, *to_even = joined(p2m, density, odd, even)
     trades = ((0, 4), (1, 2), (2, 4))
-    halos = [swapped(part, "gy", *trade) for part, trade in zip((to_even[0], to_odd, to_even[1]), trades)]
+    own, to_odd, to_even, sums = joined(trades[-1], density, odd, even, m2l_table, near, p2m)
+    halos = [swapped(part, "gy", *trade) for part, trade in zip((to_even, to_odd, sums), trades)]
     *parts, far = inner(own, m2l_table, near, p2m)
     for trade, halo in zip(trades[:-1], halos):
         parts = outer(trade, *parts, halo, far, near, p2m)

time: 11.5 us -> 11.3 us (0.983)
  the two profiles are of different devices: /device:TPU:4 before, /device:TPU:0 now
where the time goes in v8:
time: 11.3 us; the launch traced here: 11.2 us
  starting transfers between devices  5.81 us (51%)
  Pallas kernels  3.57 us (32%)
  waiting for transfers between devices  1.71 us (15%)
    ppermute x5, starting transfers between devices, swapped(): return lax.ppermute(cells, AXES, pairs)  5.81 us
    pallas_call x1, Pallas kernels, inner(): pl.pallas_call(inner_kernel, out_shape=[pltpu.VMEM((128, PAIR), F32), plt...  1.79 us
    ppermute x5, waiting for transfers between devices, swapped(): return lax.ppermute(cells, AXES, pairs)  1.71 us
    pallas_call x1, Pallas kernels, last(): pl.pallas_call(functools.partial(last_kernel, trade), out_shape=jax.Shape...  0.83 us
    pallas_call x2, Pallas kernels, outer(): pl.pallas_call(functools.partial(outer_kernel, trade), out_shape=[pltpu.V...  0.65 us
  transfers between devices with their start and end apart: 5, of which 1 were waited for; matrix products, arithmetic and copies ran while one was open for 0% of the time, Pallas kernels for 23%

profile of v8, /device:TPU:0, one launch (start us, length us, event | category | flops | bytes accessed | tf_op | source)
XLA Modules:
  0.0 11.2 jit_solution(8433853313533513367)
XLA Ops:
  0.0 0.0 copy-start.2
  0.0 0.0 copy-start.4
  0.0 0.0 copy-start.1
  0.0 0.0 copy-start.3
  0.0 0.0 copy-start
  0.0 3.0 %collective-permute-start = (bf16[4,4,1024]{2,1,0:T(4,128)(2,1)}, bf16[4,4,1024]{2,1,0:T(4,128)(2,1)S(1)}, u32[]{:S(2)}, u32[]{:S(2)}) collective-permute-start(bf16[4,4,1024]{2,1,0:T(4,128)(2,1)} %own_ref.1), channel_id=1, source_target_pairs={{0,1},{1,0},{2,3},{3,2},{4,8},{5,9},{6,10},{7,11},{8,4},{9,5},{10,... | collective-permute-start | bytes 98312 | tf_op jit(solution)/shard_map/ppermute | solution.py:36
  3.0 0.2 %collective-permute-start.1 = (bf16[4,4,1024]{2,1,0:T(4,128)(2,1)}, bf16[4,4,1024]{2,1,0:T(4,128)(2,1)S(1)}, u32[]{:S(2)}, u32[]{:S(2)}) collective-permute-start(bf16[4,4,1024]{2,1,0:T(4,128)(2,1)} %own_ref.1), channel_id=1, source_target_pairs={{0,4},{1,5},{2,6},{3,7},{4,0},{5,1},{6,2},{7,3},{8,12},{9,13},{10,... | collective-permute-start | bytes 98312 | tf_op jit(solution)/shard_map/ppermute | solution.py:36
  3.2 0.0 copy-done.4
  3.2 0.0 copy-done.1
  3.2 0.0 copy-done.3
  3.2 0.2 %pack.1 = (bf16[3,3,2,128,128]{4,3,2,1,0:T(8,128)(2,1)S(1)}, bf16[128,128]{1,0:T(8,128)(2,1)S(1)}, bf16[128,128]{1,0:T(8,128)(2,1)S(1)}) custom-call(f32[8,128]{1,0:T(8,128)S(1)} %first.1.first_ref, bf16[56,64]{1,0:T(8,128)(2,1)S(1)} %bitcast.1, bf16[3,3,3,64,64]{4,3,2,1,0:T(8,128)(2,1)S(1)} %copy-done.1, bf16[56,64]{1,0:T(8,128)(2,1)S(1)} %copy-done.4), custom_call_target="tpu_custom_call" | custom-call | flops 4000000 | bytes 10000000 | tf_op jit(solution)/shard_map/pack/pallas_call | solution.py:99
  3.4 1.7 %collective-permute-done.odd_ref = bf16[4,4,1024]{2,1,0:T(4,128)(2,1)S(1)} collective-permute-done((bf16[4,4,1024]{2,1,0:T(4,128)(2,1)}, bf16[4,4,1024]{2,1,0:T(4,128)(2,1)S(1)}, u32[]{:S(2)}, u32[]{:S(2)}) %collective-permute-start) | collective-permute-done | bytes 32800 | tf_op jit(solution)/shard_map/ppermute | solution.py:36
  5.1 0.0 collective-permute-done.1.even_ref
  5.1 0.0 copy-done.2
  5.1 0.0 copy-done
  5.1 0.1 join.1
  5.3 2.1 %collective-permute-start.2 = (bf16[128,128]{1,0:T(8,128)(2,1)S(1)}, bf16[128,128]{1,0:T(8,128)(2,1)S(1)}, u32[]{:S(2)}, u32[]{:S(2)}) collective-permute-start(bf16[128,128]{1,0:T(8,128)(2,1)S(1)} %get-tuple-element.24), channel_id=1, source_target_pairs={{0,1},{1,0},{2,6},{3,7},{4,5},{5,4},{6,2},{7,3},{8,9},{9,8},{10,14... | collective-permute-start | bytes 98312 | tf_op jit(solution)/shard_map/ppermute | solution.py:36
  7.4 0.0 collective-permute-start.3
  7.4 0.5 %collective-permute-start.4 = (bf16[128,128]{1,0:T(8,128)(2,1)S(1)}, bf16[128,128]{1,0:T(8,128)(2,1)S(1)}, u32[]{:S(2)}, u32[]{:S(2)}) collective-permute-start(bf16[128,128]{1,0:T(8,128)(2,1)S(1)} %get-tuple-element.31), channel_id=1, source_target_pairs={{0,4},{1,5},{2,3},{3,2},{4,0},{5,1},{6,7},{7,6},{8,12},{9,13},{10,... | collective-permute-start | bytes 98312 | tf_op jit(solution)/shard_map/ppermute | solution.py:36
  7.9 1.8 %inner.1 = (f32[128,128]{1,0:T(8,128)S(1)}, f32[128,128]{1,0:T(8,128)S(1)}, bf16[7,7,3,128,128]{4,3,2,1,0:T(8,128)(2,1)S(1)}) custom-call(bf16[256,128]{1,0:T(8,128)(2,1)S(1)} %get-tuple-element.21.own_ref, bf16[7,7,7,56,56]{4,3,2,1,0:T(8,128)(2,1)S(1)} %copy-done, bf16[3,3,2,128,128]{4,3,2,1,0:T(8,128)(2,1)S(1)} %get-tuple-element.19.near_ref, ...), custom_call_target="tpu_custom_call" | custom-call | flops 400000000 | bytes 6000000 | tf_op jit(solution)/shard_map/inner/pallas_call | solution.py:316
  9.7 0.0 collective-permute-done.2.cells_ref
  9.7 0.6 %outer.2 = (f32[128,128]{1,0:T(8,128)S(1)}, f32[128,128]{1,0:T(8,128)S(1)}) custom-call(f32[128,128]{1,0:T(8,128)S(1)} %get-tuple-element.22.far_part, f32[128,128]{1,0:T(8,128)S(1)} %get-tuple-element.23.near_part, bf16[128,128]{1,0:T(8,128)(2,1)S(1)} %collective-permute-done.2.cells_ref, bf16[7,7,3,128,128]{4,3,2,1,0:T(8,128)(2,1)S(1)} %get-tuple-element.25.far_ref, ...), custom_call_target="tpu_custom_call" | custom-call | flops 200000000 | bytes 3000000 | tf_op jit(solution)/shard_map/outer/pallas_call | solution.py:333
  10.3 0.0 collective-permute-done.3.cells_ref
  10.3 0.0 collective-permute-done.4.cells_ref
  10.4 0.8 %last.1 = f32[4,4,1024]{2,1,0:T(4,128)} custom-call(f32[128,128]{1,0:T(8,128)S(1)} %get-tuple-element.29.far_part, f32[128,128]{1,0:T(8,128)S(1)} %get-tuple-element.30.near_part, bf16[128,128]{1,0:T(8,128)(2,1)S(1)} %collective-permute-done.4.cells_ref, bf16[7,7,3,128,128]{4,3,2,1,0:T(8,128)(2,1)S(1)} %get-tuple-element.25.far_ref, ...), custom_call_target="tpu_custom_call" | custom-call | flops 200000000 | bytes 3000000 | tf_op jit(solution)/shard_map/last/pallas_call | solution.py:346
  (2 shorter events, 0.0 us)
Async XLA Ops:
  0.0 5.1 %copy-start.2 = (bf16[4,4,1024]{2,1,0:T(4,128)(2,1)S(1)}, bf16[4,4,1024]{2,1,0:T(4,128)(2,1)}, u32[]{:S(2)}) copy-start(bf16[4,4,1024]{2,1,0:T(4,128)(2,1)} %own_ref.1) | copy-start | bytes 98308
  0.0 3.2 %copy-start.4 = (bf16[56,64]{1,0:T(8,128)(2,1)S(1)}, bf16[56,64]{1,0:T(8,128)(2,1)}, u32[]{:S(2)}) copy-start(bf16[56,64]{1,0:T(8,128)(2,1)} %l2p_ref.1) | copy-start | bytes 21508
  0.0 3.2 %copy-start.1 = (bf16[3,3,3,64,64]{4,3,2,1,0:T(8,128)(2,1)S(1)}, bf16[3,3,3,64,64]{4,3,2,1,0:T(8,128)(2,1)}, u32[]{:S(2)}) copy-start(bf16[3,3,3,64,64]{4,3,2,1,0:T(8,128)(2,1)} %near_ref.1) | copy-start | bytes 663556
  0.0 3.2 %copy-start.3 = (bf16[64,56]{0,1:T(8,128)(2,1)S(1)}, bf16[64,56]{0,1:T(8,128)(2,1)}, u32[]{:S(2)}) copy-start(bf16[64,56]{0,1:T(8,128)(2,1)} %param.6) | copy-start | bytes 21508
  0.0 5.1 %copy-start = (bf16[7,7,7,56,56]{4,3,2,1,0:T(8,128)(2,1)S(1)}, bf16[7,7,7,56,56]{4,3,2,1,0:T(8,128)(2,1)}, u32[]{:S(2)}) copy-start(bf16[7,7,7,56,56]{4,3,2,1,0:T(8,128)(2,1)} %m2l_ref.3) | copy-start | bytes 6453892
  0.0 5.1 %collective-permute-start = (bf16[4,4,1024]{2,1,0:T(4,128)(2,1)}, bf16[4,4,1024]{2,1,0:T(4,128)(2,1)S(1)}, u32[]{:S(2)}, u32[]{:S(2)}) collective-permute-start(bf16[4,4,1024]{2,1,0:T(4,128)(2,1)} %own_ref.1), channel_id=1, source_target_pairs={{0,1},{1,0},{2,3},{3,2},{4,8},{5,9},{6,10},{7,11},{8,4},{9,5},{10,... | collective-permute-start | bytes 98312 | tf_op jit(solution)/shard_map/ppermute | solution.py:36
  3.0 2.1 %collective-permute-start.1 = (bf16[4,4,1024]{2,1,0:T(4,128)(2,1)}, bf16[4,4,1024]{2,1,0:T(4,128)(2,1)S(1)}, u32[]{:S(2)}, u32[]{:S(2)}) collective-permute-start(bf16[4,4,1024]{2,1,0:T(4,128)(2,1)} %own_ref.1), channel_id=1, source_target_pairs={{0,4},{1,5},{2,6},{3,7},{4,0},{5,1},{6,2},{7,3},{8,12},{9,13},{10,... | collective-permute-start | bytes 98312 | tf_op jit(solution)/shard_map/ppermute | solution.py:36
  5.3 4.4 %collective-permute-start.2 = (bf16[128,128]{1,0:T(8,128)(2,1)S(1)}, bf16[128,128]{1,0:T(8,128)(2,1)S(1)}, u32[]{:S(2)}, u32[]{:S(2)}) collective-permute-start(bf16[128,128]{1,0:T(8,128)(2,1)S(1)} %get-tuple-element.24), channel_id=1, source_target_pairs={{0,1},{1,0},{2,6},{3,7},{4,5},{5,4},{6,2},{7,3},{8,9},{9,8},{10,14... | collective-permute-start | bytes 98312 | tf_op jit(solution)/shard_map/ppermute | solution.py:36
  7.4 3.0 %collective-permute-start.3 = (bf16[128,128]{1,0:T(8,128)(2,1)S(1)}, bf16[128,128]{1,0:T(8,128)(2,1)S(1)}, u32[]{:S(2)}, u32[]{:S(2)}) collective-permute-start(bf16[128,128]{1,0:T(8,128)(2,1)S(1)} %get-tuple-element.28), channel_id=1, source_target_pairs={{0,4},{1,2},{2,1},{3,7},{4,0},{5,6},{6,5},{7,3},{8,12},{9,10},{10,... | collective-permute-start | bytes 98312 | tf_op jit(solution)/shard_map/ppermute | solution.py:36
  7.4 3.0 %collective-permute-start.4 = (bf16[128,128]{1,0:T(8,128)(2,1)S(1)}, bf16[128,128]{1,0:T(8,128)(2,1)S(1)}, u32[]{:S(2)}, u32[]{:S(2)}) collective-permute-start(bf16[128,128]{1,0:T(8,128)(2,1)S(1)} %get-tuple-element.31), channel_id=1, source_target_pairs={{0,4},{1,5},{2,3},{3,2},{4,0},{5,1},{6,7},{7,6},{8,12},{9,13},{10,... | collective-permute-start | bytes 98312 | tf_op jit(solution)/shard_map/ppermute | solution.py:36

commit v9 on v8

--- a/solution.py
+++ b/solution.py
@@ -152,8 +152,10 @@
         column_windows(rows_ref[:128], p2m_ref, far_rows, near_rows)
         sums = halo_sums(lambda offset_x, index: far_blocks(m2l_ref, offset_x, 4 + index), far_rows)
         sums_out[:64] = sums.astype(BF16)
-        sums_out[64:96] = near_product(near_rows, slice(0, 32), near_ref, 2).astype(BF16)
-        sums_out[96:] = jnp.zeros((32, PAIR), BF16)
+        near = near_product(near_rows, slice(0, 32), near_ref, 2)
+        rounded = near.astype(BF16)
+        sums_out[64:96] = rounded
+        sums_out[96:] = (near - rounded.astype(F32)).astype(BF16)
 
 
 def joined(trade, own, odd, even, m2l_table, near, p2m):
@@ -302,7 +304,7 @@
     @pl.when(after)
     def _():
         far[64:128] += cells_ref[:64].astype(F32)
-        near[96:128] += cells_ref[64:96].astype(F32)
+        near[96:128] += cells_ref[64:96].astype(F32) + cells_ref[96:128].astype(F32)
 
     near[...] += jnp.dot(far[...].astype(BF16), l2p_ref[...], preferred_element_type=F32)
     for x in range(4):

time: 11.3 us -> 11.3 us (level)
  no operation moved by 1% of the time
where the time goes in v9:
time: 11.3 us; the launch traced here: 11.2 us
  starting transfers between devices  5.81 us (51%)
  Pallas kernels  3.57 us (32%)
  waiting for transfers between devices  1.71 us (15%)
    ppermute x5, starting transfers between devices, swapped(): return lax.ppermute(cells, AXES, pairs)  5.81 us
    pallas_call x1, Pallas kernels, inner(): pl.pallas_call(inner_kernel, out_shape=[pltpu.VMEM((128, PAIR), F32), plt...  1.79 us
    ppermute x5, waiting for transfers between devices, swapped(): return lax.ppermute(cells, AXES, pairs)  1.71 us
    pallas_call x1, Pallas kernels, last(): pl.pallas_call(functools.partial(last_kernel, trade), out_shape=jax.Shape...  0.83 us
    pallas_call x2, Pallas kernels, outer(): pl.pallas_call(functools.partial(outer_kernel, trade), out_shape=[pltpu.V...  0.65 us
  transfers between devices with their start and end apart: 5, of which 1 were waited for; matrix products, arithmetic and copies ran while one was open for 0% of the time, Pallas kernels for 23%

profile of v9, /device:TPU:0, one launch (start us, length us, event | category | flops | bytes accessed | tf_op | source)
XLA Modules:
  0.0 11.2 jit_solution(3935385910758794738)
XLA Ops:
  0.0 0.0 copy-start.2
  0.0 0.0 copy-start.4
  0.0 0.0 copy-start.1
  0.0 0.0 copy-start.3
  0.0 0.0 copy-start
  0.0 3.0 %collective-permute-start = (bf16[4,4,1024]{2,1,0:T(4,128)(2,1)}, bf16[4,4,1024]{2,1,0:T(4,128)(2,1)S(1)}, u32[]{:S(2)}, u32[]{:S(2)}) collective-permute-start(bf16[4,4,1024]{2,1,0:T(4,128)(2,1)} %own_ref.1), channel_id=1, source_target_pairs={{0,1},{1,0},{2,3},{3,2},{4,8},{5,9},{6,10},{7,11},{8,4},{9,5},{10,... | collective-permute-start | bytes 98312 | tf_op jit(solution)/shard_map/ppermute | solution.py:36
  3.0 0.2 %collective-permute-start.1 = (bf16[4,4,1024]{2,1,0:T(4,128)(2,1)}, bf16[4,4,1024]{2,1,0:T(4,128)(2,1)S(1)}, u32[]{:S(2)}, u32[]{:S(2)}) collective-permute-start(bf16[4,4,1024]{2,1,0:T(4,128)(2,1)} %own_ref.1), channel_id=1, source_target_pairs={{0,4},{1,5},{2,6},{3,7},{4,0},{5,1},{6,2},{7,3},{8,12},{9,13},{10,... | collective-permute-start | bytes 98312 | tf_op jit(solution)/shard_map/ppermute | solution.py:36
  3.2 0.0 copy-done.4
  3.2 0.0 copy-done.1
  3.2 0.0 copy-done.3
  3.2 0.2 %pack.1 = (bf16[3,3,2,128,128]{4,3,2,1,0:T(8,128)(2,1)S(1)}, bf16[128,128]{1,0:T(8,128)(2,1)S(1)}, bf16[128,128]{1,0:T(8,128)(2,1)S(1)}) custom-call(f32[8,128]{1,0:T(8,128)S(1)} %first.1.first_ref, bf16[56,64]{1,0:T(8,128)(2,1)S(1)} %bitcast.1, bf16[3,3,3,64,64]{4,3,2,1,0:T(8,128)(2,1)S(1)} %copy-done.1, bf16[56,64]{1,0:T(8,128)(2,1)S(1)} %copy-done.4), custom_call_target="tpu_custom_call" | custom-call | flops 4000000 | bytes 10000000 | tf_op jit(solution)/shard_map/pack/pallas_call | solution.py:99
  3.4 1.7 %collective-permute-done.odd_ref = bf16[4,4,1024]{2,1,0:T(4,128)(2,1)S(1)} collective-permute-done((bf16[4,4,1024]{2,1,0:T(4,128)(2,1)}, bf16[4,4,1024]{2,1,0:T(4,128)(2,1)S(1)}, u32[]{:S(2)}, u32[]{:S(2)}) %collective-permute-start) | collective-permute-done | bytes 32800 | tf_op jit(solution)/shard_map/ppermute | solution.py:36
  5.1 0.0 collective-permute-done.1.even_ref
  5.1 0.0 copy-done.2
  5.1 0.0 copy-done
  5.1 0.1 join.1
  5.3 2.1 %collective-permute-start.2 = (bf16[128,128]{1,0:T(8,128)(2,1)S(1)}, bf16[128,128]{1,0:T(8,128)(2,1)S(1)}, u32[]{:S(2)}, u32[]{:S(2)}) collective-permute-start(bf16[128,128]{1,0:T(8,128)(2,1)S(1)} %get-tuple-element.24), channel_id=1, source_target_pairs={{0,1},{1,0},{2,6},{3,7},{4,5},{5,4},{6,2},{7,3},{8,9},{9,8},{10,14... | collective-permute-start | bytes 98312 | tf_op jit(solution)/shard_map/ppermute | solution.py:36
  7.4 0.0 collective-permute-start.3
  7.4 0.5 %collective-permute-start.4 = (bf16[128,128]{1,0:T(8,128)(2,1)S(1)}, bf16[128,128]{1,0:T(8,128)(2,1)S(1)}, u32[]{:S(2)}, u32[]{:S(2)}) collective-permute-start(bf16[128,128]{1,0:T(8,128)(2,1)S(1)} %get-tuple-element.31), channel_id=1, source_target_pairs={{0,4},{1,5},{2,3},{3,2},{4,0},{5,1},{6,7},{7,6},{8,12},{9,13},{10,... | collective-permute-start | bytes 98312 | tf_op jit(solution)/shard_map/ppermute | solution.py:36
  7.9 1.8 %inner.1 = (f32[128,128]{1,0:T(8,128)S(1)}, f32[128,128]{1,0:T(8,128)S(1)}, bf16[7,7,3,128,128]{4,3,2,1,0:T(8,128)(2,1)S(1)}) custom-call(bf16[256,128]{1,0:T(8,128)(2,1)S(1)} %get-tuple-element.21.own_ref, bf16[7,7,7,56,56]{4,3,2,1,0:T(8,128)(2,1)S(1)} %copy-done, bf16[3,3,2,128,128]{4,3,2,1,0:T(8,128)(2,1)S(1)} %get-tuple-element.19.near_ref, ...), custom_call_target="tpu_custom_call" | custom-call | flops 400000000 | bytes 6000000 | tf_op jit(solution)/shard_map/inner/pallas_call | solution.py:318
  9.7 0.0 collective-permute-done.2.cells_ref
  9.7 0.6 %outer.2 = (f32[128,128]{1,0:T(8,128)S(1)}, f32[128,128]{1,0:T(8,128)S(1)}) custom-call(f32[128,128]{1,0:T(8,128)S(1)} %get-tuple-element.22.far_part, f32[128,128]{1,0:T(8,128)S(1)} %get-tuple-element.23.near_part, bf16[128,128]{1,0:T(8,128)(2,1)S(1)} %collective-permute-done.2.cells_ref, bf16[7,7,3,128,128]{4,3,2,1,0:T(8,128)(2,1)S(1)} %get-tuple-element.25.far_ref, ...), custom_call_target="tpu_custom_call" | custom-call | flops 200000000 | bytes 3000000 | tf_op jit(solution)/shard_map/outer/pallas_call | solution.py:335
  10.3 0.0 collective-permute-done.3.cells_ref
  10.3 0.0 collective-permute-done.4.cells_ref
  10.4 0.8 %last.1 = f32[4,4,1024]{2,1,0:T(4,128)} custom-call(f32[128,128]{1,0:T(8,128)S(1)} %get-tuple-element.29.far_part, f32[128,128]{1,0:T(8,128)S(1)} %get-tuple-element.30.near_part, bf16[128,128]{1,0:T(8,128)(2,1)S(1)} %collective-permute-done.4.cells_ref, bf16[7,7,3,128,128]{4,3,2,1,0:T(8,128)(2,1)S(1)} %get-tuple-element.25.far_ref, ...), custom_call_target="tpu_custom_call" | custom-call | flops 200000000 | bytes 3000000 | tf_op jit(solution)/shard_map/last/pallas_call | solution.py:348
  (2 shorter events, 0.0 us)
Async XLA Ops:
  0.0 5.1 %copy-start.2 = (bf16[4,4,1024]{2,1,0:T(4,128)(2,1)S(1)}, bf16[4,4,1024]{2,1,0:T(4,128)(2,1)}, u32[]{:S(2)}) copy-start(bf16[4,4,1024]{2,1,0:T(4,128)(2,1)} %own_ref.1) | copy-start | bytes 98308
  0.0 3.2 %copy-start.4 = (bf16[56,64]{1,0:T(8,128)(2,1)S(1)}, bf16[56,64]{1,0:T(8,128)(2,1)}, u32[]{:S(2)}) copy-start(bf16[56,64]{1,0:T(8,128)(2,1)} %l2p_ref.1) | copy-start | bytes 21508
  0.0 3.2 %copy-start.1 = (bf16[3,3,3,64,64]{4,3,2,1,0:T(8,128)(2,1)S(1)}, bf16[3,3,3,64,64]{4,3,2,1,0:T(8,128)(2,1)}, u32[]{:S(2)}) copy-start(bf16[3,3,3,64,64]{4,3,2,1,0:T(8,128)(2,1)} %near_ref.1) | copy-start | bytes 663556
  0.0 3.2 %copy-start.3 = (bf16[64,56]{0,1:T(8,128)(2,1)S(1)}, bf16[64,56]{0,1:T(8,128)(2,1)}, u32[]{:S(2)}) copy-start(bf16[64,56]{0,1:T(8,128)(2,1)} %param.6) | copy-start | bytes 21508
  0.0 5.1 %copy-start = (bf16[7,7,7,56,56]{4,3,2,1,0:T(8,128)(2,1)S(1)}, bf16[7,7,7,56,56]{4,3,2,1,0:T(8,128)(2,1)}, u32[]{:S(2)}) copy-start(bf16[7,7,7,56,56]{4,3,2,1,0:T(8,128)(2,1)} %m2l_ref.3) | copy-start | bytes 6453892
  0.0 5.1 %collective-permute-start = (bf16[4,4,1024]{2,1,0:T(4,128)(2,1)}, bf16[4,4,1024]{2,1,0:T(4,128)(2,1)S(1)}, u32[]{:S(2)}, u32[]{:S(2)}) collective-permute-start(bf16[4,4,1024]{2,1,0:T(4,128)(2,1)} %own_ref.1), channel_id=1, source_target_pairs={{0,1},{1,0},{2,3},{3,2},{4,8},{5,9},{6,10},{7,11},{8,4},{9,5},{10,... | collective-permute-start | bytes 98312 | tf_op jit(solution)/shard_map/ppermute | solution.py:36
  3.0 2.1 %collective-permute-start.1 = (bf16[4,4,1024]{2,1,0:T(4,128)(2,1)}, bf16[4,4,1024]{2,1,0:T(4,128)(2,1)S(1)}, u32[]{:S(2)}, u32[]{:S(2)}) collective-permute-start(bf16[4,4,1024]{2,1,0:T(4,128)(2,1)} %own_ref.1), channel_id=1, source_target_pairs={{0,4},{1,5},{2,6},{3,7},{4,0},{5,1},{6,2},{7,3},{8,12},{9,13},{10,... | collective-permute-start | bytes 98312 | tf_op jit(solution)/shard_map/ppermute | solution.py:36
  5.3 4.4 %collective-permute-start.2 = (bf16[128,128]{1,0:T(8,128)(2,1)S(1)}, bf16[128,128]{1,0:T(8,128)(2,1)S(1)}, u32[]{:S(2)}, u32[]{:S(2)}) collective-permute-start(bf16[128,128]{1,0:T(8,128)(2,1)S(1)} %get-tuple-element.24), channel_id=1, source_target_pairs={{0,1},{1,0},{2,6},{3,7},{4,5},{5,4},{6,2},{7,3},{8,9},{9,8},{10,14... | collective-permute-start | bytes 98312 | tf_op jit(solution)/shard_map/ppermute | solution.py:36
  7.4 3.0 %collective-permute-start.3 = (bf16[128,128]{1,0:T(8,128)(2,1)S(1)}, bf16[128,128]{1,0:T(8,128)(2,1)S(1)}, u32[]{:S(2)}, u32[]{:S(2)}) collective-permute-start(bf16[128,128]{1,0:T(8,128)(2,1)S(1)} %get-tuple-element.28), channel_id=1, source_target_pairs={{0,4},{1,2},{2,1},{3,7},{4,0},{5,6},{6,5},{7,3},{8,12},{9,10},{10,... | collective-permute-start | bytes 98312 | tf_op jit(solution)/shard_map/ppermute | solution.py:36
  7.4 3.0 %collective-permute-start.4 = (bf16[128,128]{1,0:T(8,128)(2,1)S(1)}, bf16[128,128]{1,0:T(8,128)(2,1)S(1)}, u32[]{:S(2)}, u32[]{:S(2)}) collective-permute-start(bf16[128,128]{1,0:T(8,128)(2,1)S(1)} %get-tuple-element.31), channel_id=1, source_target_pairs={{0,4},{1,5},{2,3},{3,2},{4,0},{5,1},{6,7},{7,6},{8,12},{9,13},{10,... | collective-permute-start | bytes 98312 | tf_op jit(solution)/shard_map/ppermute | solution.py:36

commit v10 on v9

--- a/solution.py
+++ b/solution.py
@@ -118,7 +118,7 @@
 
 def join_kernel(
     trade, own_ref, odd_ref, even_ref, m2l_ref, near_ref, p2m_ref,
-    own_out, odd_out, even_out, sums_out, rows_ref, far_rows, near_rows,
+    own_out, odd_out, even_out, sums_out, ready_out, rows_ref, far_rows, near_rows, own_rows,
 ):
     pairs = own_ref.shape[2] // PAIR
     for pair in range(pairs):
@@ -147,6 +147,10 @@
     sums_out[...] = jnp.where(lower, tail, head).astype(BF16)
     before, _ = partners(trade)
 
+    @pl.when(waits_longest())
+    def _():
+        own_near(rows_ref[...], ready_out, near_ref, own_rows)
+
     @pl.when(before)
     def _():
         column_windows(rows_ref[:128], p2m_ref, far_rows, near_rows)
@@ -161,13 +165,15 @@
 def joined(trade, own, odd, even, m2l_table, near, p2m):
     return pl.pallas_call(
         functools.partial(join_kernel, trade),
-        out_shape=[pltpu.VMEM((rows, PAIR), BF16) for rows in (256, 128, 128, 128)],
+        out_shape=[pltpu.VMEM((rows, PAIR), BF16) for rows in (256, 128, 128, 128)]
+        + [pltpu.VMEM((128, PAIR), F32)],
         in_specs=[pl.BlockSpec(memory_space=pltpu.VMEM)] * 6,
-        out_specs=[pl.BlockSpec(memory_space=pltpu.VMEM)] * 4,
+        out_specs=[pl.BlockSpec(memory_space=pltpu.VMEM)] * 5,
         scratch_shapes=[
             pltpu.VMEM((256, PAIR), F32),
             pltpu.VMEM((7, 3, 64, PAIR), BF16),
             pltpu.VMEM((3, 2, 64, PAIR), BF16),
+            pltpu.VMEM((3, 2, 128, PAIR), BF16),
         ],
         compiler_params=pltpu.CompilerParams(vmem_limit_bytes=SMALL_LIMIT),
         cost_estimate=pl.CostEstimate(flops=1000000, bytes_accessed=100000, transcendentals=0),
@@ -182,7 +188,7 @@
     return before, rows, after
 
 
-def column_windows(cells, p2m_ref, far_rows, near_rows):
+def far_windows(cells, p2m_ref, far_rows):
     multipole = lax.dot_general(
         cells.astype(BF16), p2m_ref[...], (((1,), (1,)), ((), ())), preferred_element_type=F32
     )
@@ -200,6 +206,10 @@
                 else:
                     window = slab[8 * (offset_x - 1) : 8 * (offset_x + 3)]
                 far_rows[offset_x, b, 32 * y : 32 * y + 32] = window.astype(BF16)
+
+
+def near_windows(cells, near_rows):
+    count = cells.shape[0] // 64
     before, same, after = shifted(cells)
     lane = lax.broadcasted_iota(jnp.int32, cells.shape, 1)
     beside = jnp.where(lane < WIDTH, after, before)
@@ -211,6 +221,22 @@
                 ].astype(BF16)
 
 
+def column_windows(cells, p2m_ref, far_rows, near_rows):
+    far_windows(cells, p2m_ref, far_rows)
+    near_windows(cells, near_rows)
+
+
+def waits_longest():
+    return jnp.logical_and(lax.axis_index("gx") < 2, lax.axis_index("gy") == 0)
+
+
+def own_near(cells, near_out, near_ref, near_rows):
+    near_windows(cells, near_rows)
+    near_out[...] = near_product(near_rows, slice(0, 128), near_ref, 1)
+    near_out[32:128] += near_product(near_rows, slice(0, 96), near_ref, 0)
+    near_out[0:96] += near_product(near_rows, slice(32, 128), near_ref, 2)
+
+
 def far_product(far_rows, rows, blocks):
     chunks, weights = [], []
     for offset_x in range(7):
@@ -231,8 +257,10 @@
     )
 
 
-def inner_kernel(own_ref, m2l_ref, near_ref, p2m_ref, far_out, near_out, table_out, far_rows, near_rows):
-    column_windows(own_ref[...].astype(F32), p2m_ref, far_rows, near_rows)
+def inner_kernel(
+    own_ref, ready_ref, m2l_ref, near_ref, p2m_ref, far_out, near_out, table_out, far_rows, near_rows
+):
+    far_windows(own_ref[...].astype(F32), p2m_ref, far_rows)
     far_out[...] = jnp.zeros_like(far_out)
     for offset_y in range(7):
         targets = [3] if offset_y == 0 else [0] if offset_y == 6 else [
@@ -249,9 +277,15 @@
 
         product = far_product(far_rows, slice(32 * start, 32 * (start + len(targets))), packing)
         far_out[32 * targets[0] : 32 * (targets[-1] + 1)] += product
-    near_out[...] = near_product(near_rows, slice(0, 128), near_ref, 1)
-    near_out[32:128] += near_product(near_rows, slice(0, 96), near_ref, 0)
-    near_out[0:96] += near_product(near_rows, slice(32, 128), near_ref, 2)
+    early = waits_longest()
+
+    @pl.when(early)
+    def _():
+        near_out[...] = ready_ref[...]
+
+    @pl.when(jnp.logical_not(early))
+    def _():
+        own_near(own_ref[...].astype(F32), near_out, near_ref, near_rows)
 
 
 def halo_sums(blocks, far_rows):
@@ -314,7 +348,7 @@
             ]
 
 
-def inner(own, m2l_table, near, p2m):
+def inner(own, ready, m2l_table, near, p2m):
     return pl.pallas_call(
         inner_kernel,
         out_shape=[
@@ -322,13 +356,13 @@
             pltpu.VMEM((128, PAIR), F32),
             pltpu.VMEM((7, 7, 3, PAIR, PAIR), BF16),
         ],
-        in_specs=[pl.BlockSpec(memory_space=pltpu.VMEM)] * 4,
+        in_specs=[pl.BlockSpec(memory_space=pltpu.VMEM)] * 5,
         out_specs=[pl.BlockSpec(memory_space=pltpu.VMEM)] * 3,
         scratch_shapes=[pltpu.VMEM((7, 3, 128, PAIR), BF16), pltpu.VMEM((3, 2, 128, PAIR), BF16)],
         compiler_params=pltpu.CompilerParams(vmem_limit_bytes=VMEM_LIMIT),
         cost_estimate=pl.CostEstimate(flops=400000000, bytes_accessed=6000000, transcendentals=0),
         name="inner",
-    )(own, m2l_table, near, p2m)
+    )(own, ready, m2l_table, near, p2m)
 
 
 def outer(trade, far_part, near_part, cells, far, near, p2m):
@@ -366,9 +400,9 @@
     odd, even = swapped(density, "gx", 1, 2), swapped(density, "gx", 0, 2)
     near, p2m, l2p = packed(first(), p2m_operator, near_table, l2p_operator)
     trades = ((0, 4), (1, 2), (2, 4))
-    own, to_odd, to_even, sums = joined(trades[-1], density, odd, even, m2l_table, near, p2m)
+    own, to_odd, to_even, sums, ready = joined(trades[-1], density, odd, even, m2l_table, near, p2m)
     halos = [swapped(part, "gy", *trade) for part, trade in zip((to_even, to_odd, sums), trades)]
-    *parts, far = inner(own, m2l_table, near, p2m)
+    *parts, far = inner(own, ready, m2l_table, near, p2m)
     for trade, halo in zip(trades[:-1], halos):
         parts = outer(trade, *parts, halo, far, near, p2m)
     return last(trades[-1], density.shape, *parts, halos[-1], far, near, p2m, l2p)

time: 11.3 us -> 11.3 us (level)
  the two profiles are of different devices: /device:TPU:0 before, /device:TPU:6 now
where the time goes in v10:
time: 11.3 us; the launch traced here: 11.1 us
  Pallas kernels  4.47 us (40%)
  waiting for transfers between devices  3.31 us (29%)
  starting transfers between devices  3.23 us (29%)
    ppermute x5, waiting for transfers between devices, swapped(): return lax.ppermute(cells, AXES, pairs)  3.31 us
    ppermute x5, starting transfers between devices, swapped(): return lax.ppermute(cells, AXES, pairs)  3.23 us
    pallas_call x1, Pallas kernels, inner(): pl.pallas_call(inner_kernel, out_shape=[pltpu.VMEM((128, PAIR), F32), plt...  1.84 us
    pallas_call x1, Pallas kernels, last(): pl.pallas_call(functools.partial(last_kernel, trade), out_shape=jax.Shape...  1.44 us
    pallas_call x1, Pallas kernels, joined(): pl.pallas_call(functools.partial(join_kernel, trade), out_shape=[pltpu.VM...  0.95 us
  transfers between devices with their start and end apart: 5, of which 2 were waited for; matrix products, arithmetic and copies ran while one was open for 0% of the time, Pallas kernels for 19%

profile of v10, /device:TPU:6, one launch (start us, length us, event | category | flops | bytes accessed | tf_op | source)
XLA Modules:
  0.0 11.1 jit_solution(11166024582796330451)
XLA Ops:
  0.0 0.0 copy-start.2
  0.0 0.0 copy-start.4
  0.0 0.0 copy-start.1
  0.0 0.0 copy-start.3
  0.0 0.0 copy-start
  0.0 0.6 %collective-permute-start = (bf16[4,4,1024]{2,1,0:T(4,128)(2,1)}, bf16[4,4,1024]{2,1,0:T(4,128)(2,1)S(1)}, u32[]{:S(2)}, u32[]{:S(2)}) collective-permute-start(bf16[4,4,1024]{2,1,0:T(4,128)(2,1)} %own_ref.1), channel_id=1, source_target_pairs={{0,1},{1,0},{2,3},{3,2},{4,8},{5,9},{6,10},{7,11},{8,4},{9,5},{10,... | collective-permute-start | bytes 98312 | tf_op jit(solution)/shard_map/ppermute | solution.py:36
  0.6 1.2 %collective-permute-start.1 = (bf16[4,4,1024]{2,1,0:T(4,128)(2,1)}, bf16[4,4,1024]{2,1,0:T(4,128)(2,1)S(1)}, u32[]{:S(2)}, u32[]{:S(2)}) collective-permute-start(bf16[4,4,1024]{2,1,0:T(4,128)(2,1)} %own_ref.1), channel_id=1, source_target_pairs={{0,4},{1,5},{2,6},{3,7},{4,0},{5,1},{6,2},{7,3},{8,12},{9,13},{10,... | collective-permute-start | bytes 98312 | tf_op jit(solution)/shard_map/ppermute | solution.py:36
  1.8 0.0 copy-done.4
  1.8 0.0 copy-done.1
  1.8 0.0 copy-done.3
  1.8 0.2 %pack.1 = (bf16[3,3,2,128,128]{4,3,2,1,0:T(8,128)(2,1)S(1)}, bf16[128,128]{1,0:T(8,128)(2,1)S(1)}, bf16[128,128]{1,0:T(8,128)(2,1)S(1)}) custom-call(f32[8,128]{1,0:T(8,128)S(1)} %first.1.first_ref, bf16[56,64]{1,0:T(8,128)(2,1)S(1)} %bitcast.1, bf16[3,3,3,64,64]{4,3,2,1,0:T(8,128)(2,1)S(1)} %copy-done.1, bf16[56,64]{1,0:T(8,128)(2,1)S(1)} %copy-done.4), custom_call_target="tpu_custom_call" | custom-call | flops 4000000 | bytes 10000000 | tf_op jit(solution)/shard_map/pack/pallas_call | solution.py:99
  2.0 2.2 %collective-permute-done.odd_ref = bf16[4,4,1024]{2,1,0:T(4,128)(2,1)S(1)} collective-permute-done((bf16[4,4,1024]{2,1,0:T(4,128)(2,1)}, bf16[4,4,1024]{2,1,0:T(4,128)(2,1)S(1)}, u32[]{:S(2)}, u32[]{:S(2)}) %collective-permute-start) | collective-permute-done | bytes 32800 | tf_op jit(solution)/shard_map/ppermute | solution.py:36
  4.2 0.0 collective-permute-done.1.even_ref
  4.2 0.0 copy-done.2
  4.2 0.0 copy-done
  4.2 1.0 %join.1 = (bf16[256,128]{1,0:T(8,128)(2,1)S(1)}, bf16[128,128]{1,0:T(8,128)(2,1)S(1)}, bf16[128,128]{1,0:T(8,128)(2,1)S(1)}, bf16[128,128]{1,0:T(8,128)(2,1)S(1)}, f32[128,128]{1,0:T(8,128)S(1)}) custom-call(bf16[4,4,1024]{2,1,0:T(4,128)(2,1)S(1)} %copy-done.2, bf16[4,4,1024]{2,1,0:T(4,128)(2,1)S(1)} %collective-permute-done.odd_ref, ...), custom_call_target="tpu_custom_call" | custom-call | flops 1000000 | bytes 100000 | tf_op jit(solution)/shard_map/join/pallas_call | solution.py:166
  5.2 0.1 collective-permute-start.2
  5.3 0.5 %collective-permute-start.3 = (bf16[128,128]{1,0:T(8,128)(2,1)S(1)}, bf16[128,128]{1,0:T(8,128)(2,1)S(1)}, u32[]{:S(2)}, u32[]{:S(2)}) collective-permute-start(bf16[128,128]{1,0:T(8,128)(2,1)S(1)} %get-tuple-element.30), channel_id=1, source_target_pairs={{0,4},{1,2},{2,1},{3,7},{4,0},{5,6},{6,5},{7,3},{8,12},{9,10},{10,... | collective-permute-start | bytes 98312 | tf_op jit(solution)/shard_map/ppermute | solution.py:36
  5.8 0.9 %collective-permute-start.4 = (bf16[128,128]{1,0:T(8,128)(2,1)S(1)}, bf16[128,128]{1,0:T(8,128)(2,1)S(1)}, u32[]{:S(2)}, u32[]{:S(2)}) collective-permute-start(bf16[128,128]{1,0:T(8,128)(2,1)S(1)} %get-tuple-element.33), channel_id=1, source_target_pairs={{0,4},{1,5},{2,3},{3,2},{4,0},{5,1},{6,7},{7,6},{8,12},{9,13},{10,... | collective-permute-start | bytes 98312 | tf_op jit(solution)/shard_map/ppermute | solution.py:36
  6.7 1.8 %inner.1 = (f32[128,128]{1,0:T(8,128)S(1)}, f32[128,128]{1,0:T(8,128)S(1)}, bf16[7,7,3,128,128]{4,3,2,1,0:T(8,128)(2,1)S(1)}) custom-call(bf16[256,128]{1,0:T(8,128)(2,1)S(1)} %get-tuple-element.22.own_ref, f32[128,128]{1,0:T(8,128)S(1)} %get-tuple-element.23.ready_ref, bf16[7,7,7,56,56]{4,3,2,1,0:T(8,128)(2,1)S(1)} %copy-done, ...), custom_call_target="tpu_custom_call" | custom-call | flops 400000000 | bytes 6000000 | tf_op jit(solution)/shard_map/inner/pallas_call | solution.py:352
  8.5 0.0 collective-permute-done.2.cells_ref
  8.6 0.0 collective-permute-done.3.cells_ref
  8.6 1.1 %collective-permute-done.4.cells_ref = bf16[128,128]{1,0:T(8,128)(2,1)S(1)} collective-permute-done((bf16[128,128]{1,0:T(8,128)(2,1)S(1)}, bf16[128,128]{1,0:T(8,128)(2,1)S(1)}, u32[]{:S(2)}, u32[]{:S(2)}) %collective-permute-start.4) | collective-permute-done | bytes 32800 | tf_op jit(solution)/shard_map/ppermute | solution.py:36
  9.7 1.4 %last.1 = f32[4,4,1024]{2,1,0:T(4,128)} custom-call(f32[128,128]{1,0:T(8,128)S(1)} %get-tuple-element.31.far_part, f32[128,128]{1,0:T(8,128)S(1)} %get-tuple-element.32.near_part, bf16[128,128]{1,0:T(8,128)(2,1)S(1)} %collective-permute-done.4.cells_ref, bf16[7,7,3,128,128]{4,3,2,1,0:T(8,128)(2,1)S(1)} %get-tuple-element.27.far_ref, ...), custom_call_target="tpu_custom_call" | custom-call | flops 200000000 | bytes 3000000 | tf_op jit(solution)/shard_map/last/pallas_call | solution.py:382
  (3 shorter events, 0.0 us)
Async XLA Ops:
  0.0 4.2 %copy-start.2 = (bf16[4,4,1024]{2,1,0:T(4,128)(2,1)S(1)}, bf16[4,4,1024]{2,1,0:T(4,128)(2,1)}, u32[]{:S(2)}) copy-start(bf16[4,4,1024]{2,1,0:T(4,128)(2,1)} %own_ref.1) | copy-start | bytes 98308
  0.0 1.8 %copy-start.4 = (bf16[56,64]{1,0:T(8,128)(2,1)S(1)}, bf16[56,64]{1,0:T(8,128)(2,1)}, u32[]{:S(2)}) copy-start(bf16[56,64]{1,0:T(8,128)(2,1)} %l2p_ref.1) | copy-start | bytes 21508
  0.0 1.8 %copy-start.1 = (bf16[3,3,3,64,64]{4,3,2,1,0:T(8,128)(2,1)S(1)}, bf16[3,3,3,64,64]{4,3,2,1,0:T(8,128)(2,1)}, u32[]{:S(2)}) copy-start(bf16[3,3,3,64,64]{4,3,2,1,0:T(8,128)(2,1)} %near_ref.1) | copy-start | bytes 663556
  0.0 1.8 %copy-start.3 = (bf16[64,56]{0,1:T(8,128)(2,1)S(1)}, bf16[64,56]{0,1:T(8,128)(2,1)}, u32[]{:S(2)}) copy-start(bf16[64,56]{0,1:T(8,128)(2,1)} %param.6) | copy-start | bytes 21508
  0.0 4.2 %copy-start = (bf16[7,7,7,56,56]{4,3,2,1,0:T(8,128)(2,1)S(1)}, bf16[7,7,7,56,56]{4,3,2,1,0:T(8,128)(2,1)}, u32[]{:S(2)}) copy-start(bf16[7,7,7,56,56]{4,3,2,1,0:T(8,128)(2,1)} %m2l_ref.3) | copy-start | bytes 6453892
  0.0 4.2 %collective-permute-start = (bf16[4,4,1024]{2,1,0:T(4,128)(2,1)}, bf16[4,4,1024]{2,1,0:T(4,128)(2,1)S(1)}, u32[]{:S(2)}, u32[]{:S(2)}) collective-permute-start(bf16[4,4,1024]{2,1,0:T(4,128)(2,1)} %own_ref.1), channel_id=1, source_target_pairs={{0,1},{1,0},{2,3},{3,2},{4,8},{5,9},{6,10},{7,11},{8,4},{9,5},{10,... | collective-permute-start | bytes 98312 | tf_op jit(solution)/shard_map/ppermute | solution.py:36
  0.6 3.6 %collective-permute-start.1 = (bf16[4,4,1024]{2,1,0:T(4,128)(2,1)}, bf16[4,4,1024]{2,1,0:T(4,128)(2,1)S(1)}, u32[]{:S(2)}, u32[]{:S(2)}) collective-permute-start(bf16[4,4,1024]{2,1,0:T(4,128)(2,1)} %own_ref.1), channel_id=1, source_target_pairs={{0,4},{1,5},{2,6},{3,7},{4,0},{5,1},{6,2},{7,3},{8,12},{9,13},{10,... | collective-permute-start | bytes 98312 | tf_op jit(solution)/shard_map/ppermute | solution.py:36
  5.2 3.3 %collective-permute-start.2 = (bf16[128,128]{1,0:T(8,128)(2,1)S(1)}, bf16[128,128]{1,0:T(8,128)(2,1)S(1)}, u32[]{:S(2)}, u32[]{:S(2)}) collective-permute-start(bf16[128,128]{1,0:T(8,128)(2,1)S(1)} %get-tuple-element.26), channel_id=1, source_target_pairs={{0,1},{1,0},{2,6},{3,7},{4,5},{5,4},{6,2},{7,3},{8,9},{9,8},{10,14... | collective-permute-start | bytes 98312 | tf_op jit(solution)/shard_map/ppermute | solution.py:36
  5.3 3.3 %collective-permute-start.3 = (bf16[128,128]{1,0:T(8,128)(2,1)S(1)}, bf16[128,128]{1,0:T(8,128)(2,1)S(1)}, u32[]{:S(2)}, u32[]{:S(2)}) collective-permute-start(bf16[128,128]{1,0:T(8,128)(2,1)S(1)} %get-tuple-element.30), channel_id=1, source_target_pairs={{0,4},{1,2},{2,1},{3,7},{4,0},{5,6},{6,5},{7,3},{8,12},{9,10},{10,... | collective-permute-start | bytes 98312 | tf_op jit(solution)/shard_map/ppermute | solution.py:36
  5.8 3.9 %collective-permute-start.4 = (bf16[128,128]{1,0:T(8,128)(2,1)S(1)}, bf16[128,128]{1,0:T(8,128)(2,1)S(1)}, u32[]{:S(2)}, u32[]{:S(2)}) collective-permute-start(bf16[128,128]{1,0:T(8,128)(2,1)S(1)} %get-tuple-element.33), channel_id=1, source_target_pairs={{0,4},{1,5},{2,3},{3,2},{4,0},{5,1},{6,7},{7,6},{8,12},{9,13},{10,... | collective-permute-start | bytes 98312 | tf_op jit(solution)/shard_map/ppermute | solution.py:36

commit v11 on v10

--- a/solution.py
+++ b/solution.py
@@ -153,7 +153,8 @@
 
     @pl.when(before)
     def _():
-        column_windows(rows_ref[:128], p2m_ref, far_rows, near_rows)
+        near_windows(rows_ref[:64], near_rows)
+        far_windows(rows_ref[:128], p2m_ref, far_rows)
         sums = halo_sums(lambda offset_x, index: far_blocks(m2l_ref, offset_x, 4 + index), far_rows)
         sums_out[:64] = sums.astype(BF16)
         near = near_product(near_rows, slice(0, 32), near_ref, 2)
@@ -221,11 +222,6 @@
                 ].astype(BF16)
 
 
-def column_windows(cells, p2m_ref, far_rows, near_rows):
-    far_windows(cells, p2m_ref, far_rows)
-    near_windows(cells, near_rows)
-
-
 def waits_longest():
     return jnp.logical_and(lax.axis_index("gx") < 2, lax.axis_index("gy") == 0)
 
@@ -289,24 +285,26 @@
 
 
 def halo_sums(blocks, far_rows):
-    pair = far_product(far_rows, slice(0, 64), lambda offset_x: blocks(offset_x, 1))
     odd = far_product(far_rows, slice(0, 32), lambda offset_x: blocks(offset_x, 0))
     even = far_product(far_rows, slice(32, 64), lambda offset_x: blocks(offset_x, 2))
+    pair = far_product(far_rows, slice(0, 64), lambda offset_x: blocks(offset_x, 1))
     return pair + jnp.concatenate([even, odd], axis=0)
 
 
-def add_halo(cells_ref, before, after, far, near, table_ref, near_ref, p2m_ref, far_rows, near_rows):
-    @pl.when(jnp.logical_or(before, after))
-    def _():
-        side = jnp.where(before, 0, 1)
-        column_windows(cells_ref[...].astype(F32), p2m_ref, far_rows, near_rows)
-
-        def blocks(offset_x, index):
-            return [table_ref[offset_x, 4 * side + index, b] for b in range(3)]
-
-        far[pl.ds(pl.multiple_of(64 * side, 64), 64)] += halo_sums(blocks, far_rows)
-        rows = pl.ds(pl.multiple_of(32 - 32 * side, 32), 32)
-        near[pl.ds(pl.multiple_of(96 * side, 32), 32)] += near_product(near_rows, rows, near_ref, 2 * side)
+def add_halo(cells_ref, side, far, near, table_ref, near_ref, p2m_ref, far_rows, near_rows):
+    cells = cells_ref[...].astype(F32)
+    far_windows(cells, p2m_ref, far_rows)
+    near_windows(cells[64 - 64 * side : 128 - 64 * side], near_rows)
+
+    def blocks(offset_x, index):
+        offset_y = 4 * side + index
+        inner = 2 <= offset_x <= 4 and 2 <= offset_y <= 4
+        return [None if inner and b == 1 else table_ref[offset_x, offset_y, b] for b in range(3)]
+
+    far[64 * side : 64 * side + 64] += halo_sums(blocks, far_rows)
+    near[96 * side : 96 * side + 32] += near_product(
+        near_rows, slice(0, 32), near_ref, 2 * side
+    )
 
 
 def partners(trade):
@@ -322,7 +320,11 @@
 ):
     far_out[...] = far_part[...]
     near_out[...] = near_part[...]
-    add_halo(cells_ref, *partners(trade), far_out, near_out, far_ref, near_ref, p2m_ref, far_rows, near_rows)
+    for side, used in enumerate(partners(trade)):
+
+        @pl.when(used)
+        def _():
+            add_halo(cells_ref, side, far_out, near_out, far_ref, near_ref, p2m_ref, far_rows, near_rows)
 
 
 def last_kernel(
@@ -333,7 +335,10 @@
     far[...] = far_part[...]
     near[...] = near_part[...]
     before, after = partners(trade)
-    add_halo(cells_ref, before, False, far, near, far_ref, near_ref, p2m_ref, far_rows, near_rows)
+
+    @pl.when(before)
+    def _():
+        add_halo(cells_ref, 0, far, near, far_ref, near_ref, p2m_ref, far_rows, near_rows)
 
     @pl.when(after)
     def _():

time: 11.3 us -> 11.3 us (level)
  the two profiles are of different devices: /device:TPU:6 before, /device:TPU:2 now
where the time goes in v11:
time: 11.3 us; the launch traced here: 11.1 us
  Pallas kernels  4.2 us (37%)
  starting transfers between devices  3.55 us (31%)
  waiting for transfers between devices  3.27 us (29%)
    ppermute x5, starting transfers between devices, swapped(): return lax.ppermute(cells, AXES, pairs)  3.55 us
    ppermute x5, waiting for transfers between devices, swapped(): return lax.ppermute(cells, AXES, pairs)  3.27 us
    pallas_call x1, Pallas kernels, inner(): pl.pallas_call(inner_kernel, out_shape=[pltpu.VMEM((128, PAIR), F32), plt...  1.84 us
    pallas_call x2, Pallas kernels, outer(): pl.pallas_call(functools.partial(outer_kernel, trade), out_shape=[pltpu.V...  1.23 us
    pallas_call x1, Pallas kernels, last(): pl.pallas_call(functools.partial(last_kernel, trade), out_shape=jax.Shape...  0.83 us
  transfers between devices with their start and end apart: 5, of which 3 were waited for; matrix products, arithmetic and copies ran while one was open for 0% of the time, Pallas kernels for 29%

profile of v11, /device:TPU:2, one launch (start us, length us, event | category | flops | bytes accessed | tf_op | source)
XLA Modules:
  0.0 11.1 jit_solution(776746869541274291)
XLA Ops:
  0.0 0.0 copy-start.2
  0.0 0.0 copy-start.4
  0.0 0.0 copy-start.1
  0.0 0.0 copy-start.3
  0.0 0.0 copy-start
  0.0 0.1 collective-permute-start
  0.1 1.7 %collective-permute-start.1 = (bf16[4,4,1024]{2,1,0:T(4,128)(2,1)}, bf16[4,4,1024]{2,1,0:T(4,128)(2,1)S(1)}, u32[]{:S(2)}, u32[]{:S(2)}) collective-permute-start(bf16[4,4,1024]{2,1,0:T(4,128)(2,1)} %own_ref.1), channel_id=1, source_target_pairs={{0,4},{1,5},{2,6},{3,7},{4,0},{5,1},{6,2},{7,3},{8,12},{9,13},{10,... | collective-permute-start | bytes 98312 | tf_op jit(solution)/shard_map/ppermute | solution.py:36
  1.8 0.0 copy-done.4
  1.8 0.0 copy-done.1
  1.8 0.0 copy-done.3
  1.8 0.2 %pack.1 = (bf16[3,3,2,128,128]{4,3,2,1,0:T(8,128)(2,1)S(1)}, bf16[128,128]{1,0:T(8,128)(2,1)S(1)}, bf16[128,128]{1,0:T(8,128)(2,1)S(1)}) custom-call(f32[8,128]{1,0:T(8,128)S(1)} %first.1.first_ref, bf16[56,64]{1,0:T(8,128)(2,1)S(1)} %bitcast.1, bf16[3,3,3,64,64]{4,3,2,1,0:T(8,128)(2,1)S(1)} %copy-done.1, bf16[56,64]{1,0:T(8,128)(2,1)S(1)} %copy-done.4), custom_call_target="tpu_custom_call" | custom-call | flops 4000000 | bytes 10000000 | tf_op jit(solution)/shard_map/pack/pallas_call | solution.py:99
  2.0 2.2 %collective-permute-done.odd_ref = bf16[4,4,1024]{2,1,0:T(4,128)(2,1)S(1)} collective-permute-done((bf16[4,4,1024]{2,1,0:T(4,128)(2,1)}, bf16[4,4,1024]{2,1,0:T(4,128)(2,1)S(1)}, u32[]{:S(2)}, u32[]{:S(2)}) %collective-permute-start) | collective-permute-done | bytes 32800 | tf_op jit(solution)/shard_map/ppermute | solution.py:36
  4.2 0.0 collective-permute-done.1.even_ref
  4.2 0.0 copy-done.2
  4.2 0.0 copy-done
  4.2 0.1 %join.1 = (bf16[256,128]{1,0:T(8,128)(2,1)S(1)}, bf16[128,128]{1,0:T(8,128)(2,1)S(1)}, bf16[128,128]{1,0:T(8,128)(2,1)S(1)}, bf16[128,128]{1,0:T(8,128)(2,1)S(1)}, f32[128,128]{1,0:T(8,128)S(1)}) custom-call(bf16[4,4,1024]{2,1,0:T(4,128)(2,1)S(1)} %copy-done.2, bf16[4,4,1024]{2,1,0:T(4,128)(2,1)S(1)} %collective-permute-done.odd_ref, ...), custom_call_target="tpu_custom_call" | custom-call | flops 1000000 | bytes 100000 | tf_op jit(solution)/shard_map/join/pallas_call | solution.py:167
  4.4 0.4 %collective-permute-start.2 = (bf16[128,128]{1,0:T(8,128)(2,1)S(1)}, bf16[128,128]{1,0:T(8,128)(2,1)S(1)}, u32[]{:S(2)}, u32[]{:S(2)}) collective-permute-start(bf16[128,128]{1,0:T(8,128)(2,1)S(1)} %get-tuple-element.26), channel_id=1, source_target_pairs={{0,1},{1,0},{2,6},{3,7},{4,5},{5,4},{6,2},{7,3},{8,9},{9,8},{10,14... | collective-permute-start | bytes 98312 | tf_op jit(solution)/shard_map/ppermute | solution.py:36
  4.7 1.3 %collective-permute-start.3 = (bf16[128,128]{1,0:T(8,128)(2,1)S(1)}, bf16[128,128]{1,0:T(8,128)(2,1)S(1)}, u32[]{:S(2)}, u32[]{:S(2)}) collective-permute-start(bf16[128,128]{1,0:T(8,128)(2,1)S(1)} %get-tuple-element.30), channel_id=1, source_target_pairs={{0,4},{1,2},{2,1},{3,7},{4,0},{5,6},{6,5},{7,3},{8,12},{9,10},{10,... | collective-permute-start | bytes 98312 | tf_op jit(solution)/shard_map/ppermute | solution.py:36
  6.0 0.2 %collective-permute-start.4 = (bf16[128,128]{1,0:T(8,128)(2,1)S(1)}, bf16[128,128]{1,0:T(8,128)(2,1)S(1)}, u32[]{:S(2)}, u32[]{:S(2)}) collective-permute-start(bf16[128,128]{1,0:T(8,128)(2,1)S(1)} %get-tuple-element.33), channel_id=1, source_target_pairs={{0,4},{1,5},{2,3},{3,2},{4,0},{5,1},{6,7},{7,6},{8,12},{9,13},{10,... | collective-permute-start | bytes 98312 | tf_op jit(solution)/shard_map/ppermute | solution.py:36
  6.2 1.8 %inner.1 = (f32[128,128]{1,0:T(8,128)S(1)}, f32[128,128]{1,0:T(8,128)S(1)}, bf16[7,7,3,128,128]{4,3,2,1,0:T(8,128)(2,1)S(1)}) custom-call(bf16[256,128]{1,0:T(8,128)(2,1)S(1)} %get-tuple-element.22.own_ref, f32[128,128]{1,0:T(8,128)S(1)} %get-tuple-element.23.ready_ref, bf16[7,7,7,56,56]{4,3,2,1,0:T(8,128)(2,1)S(1)} %copy-done, ...), custom_call_target="tpu_custom_call" | custom-call | flops 400000000 | bytes 6000000 | tf_op jit(solution)/shard_map/inner/pallas_call | solution.py:357
  8.0 0.3 %collective-permute-done.2.cells_ref = bf16[128,128]{1,0:T(8,128)(2,1)S(1)} collective-permute-done((bf16[128,128]{1,0:T(8,128)(2,1)S(1)}, bf16[128,128]{1,0:T(8,128)(2,1)S(1)}, u32[]{:S(2)}, u32[]{:S(2)}) %collective-permute-start.2) | collective-permute-done | bytes 32800 | tf_op jit(solution)/shard_map/ppermute | solution.py:36
  8.3 0.6 %outer.2 = (f32[128,128]{1,0:T(8,128)S(1)}, f32[128,128]{1,0:T(8,128)S(1)}) custom-call(f32[128,128]{1,0:T(8,128)S(1)} %get-tuple-element.24.far_part, f32[128,128]{1,0:T(8,128)S(1)} %get-tuple-element.25.near_part, bf16[128,128]{1,0:T(8,128)(2,1)S(1)} %collective-permute-done.2.cells_ref, bf16[7,7,3,128,128]{4,3,2,1,0:T(8,128)(2,1)S(1)} %get-tuple-element.27.far_ref, ...), custom_call_target="tpu_custom_call" | custom-call | flops 200000000 | bytes 3000000 | tf_op jit(solution)/shard_map/outer/pallas_call | solution.py:374
  8.9 0.7 %collective-permute-done.3.cells_ref = bf16[128,128]{1,0:T(8,128)(2,1)S(1)} collective-permute-done((bf16[128,128]{1,0:T(8,128)(2,1)S(1)}, bf16[128,128]{1,0:T(8,128)(2,1)S(1)}, u32[]{:S(2)}, u32[]{:S(2)}) %collective-permute-start.3) | collective-permute-done | bytes 32800 | tf_op jit(solution)/shard_map/ppermute | solution.py:36
  9.7 0.6 %outer.3 = (f32[128,128]{1,0:T(8,128)S(1)}, f32[128,128]{1,0:T(8,128)S(1)}) custom-call(f32[128,128]{1,0:T(8,128)S(1)} %get-tuple-element.28.far_part, f32[128,128]{1,0:T(8,128)S(1)} %get-tuple-element.29.near_part, bf16[128,128]{1,0:T(8,128)(2,1)S(1)} %collective-permute-done.3.cells_ref, bf16[7,7,3,128,128]{4,3,2,1,0:T(8,128)(2,1)S(1)} %get-tuple-element.27.far_ref, ...), custom_call_target="tpu_custom_call" | custom-call | flops 200000000 | bytes 3000000 | tf_op jit(solution)/shard_map/outer/pallas_call | solution.py:374
  10.3 0.0 collective-permute-done.4.cells_ref
  10.3 0.8 %last.1 = f32[4,4,1024]{2,1,0:T(4,128)} custom-call(f32[128,128]{1,0:T(8,128)S(1)} %get-tuple-element.31.far_part, f32[128,128]{1,0:T(8,128)S(1)} %get-tuple-element.32.near_part, bf16[128,128]{1,0:T(8,128)(2,1)S(1)} %collective-permute-done.4.cells_ref, bf16[7,7,3,128,128]{4,3,2,1,0:T(8,128)(2,1)S(1)} %get-tuple-element.27.far_ref, ...), custom_call_target="tpu_custom_call" | custom-call | flops 200000000 | bytes 3000000 | tf_op jit(solution)/shard_map/last/pallas_call | solution.py:387
  (1 shorter events, 0.0 us)
Async XLA Ops:
  0.0 4.2 %copy-start.2 = (bf16[4,4,1024]{2,1,0:T(4,128)(2,1)S(1)}, bf16[4,4,1024]{2,1,0:T(4,128)(2,1)}, u32[]{:S(2)}) copy-start(bf16[4,4,1024]{2,1,0:T(4,128)(2,1)} %own_ref.1) | copy-start | bytes 98308
  0.0 1.8 %copy-start.4 = (bf16[56,64]{1,0:T(8,128)(2,1)S(1)}, bf16[56,64]{1,0:T(8,128)(2,1)}, u32[]{:S(2)}) copy-start(bf16[56,64]{1,0:T(8,128)(2,1)} %l2p_ref.1) | copy-start | bytes 21508
  0.0 1.8 %copy-start.1 = (bf16[3,3,3,64,64]{4,3,2,1,0:T(8,128)(2,1)S(1)}, bf16[3,3,3,64,64]{4,3,2,1,0:T(8,128)(2,1)}, u32[]{:S(2)}) copy-start(bf16[3,3,3,64,64]{4,3,2,1,0:T(8,128)(2,1)} %near_ref.1) | copy-start | bytes 663556
  0.0 1.8 %copy-start.3 = (bf16[64,56]{0,1:T(8,128)(2,1)S(1)}, bf16[64,56]{0,1:T(8,128)(2,1)}, u32[]{:S(2)}) copy-start(bf16[64,56]{0,1:T(8,128)(2,1)} %param.6) | copy-start | bytes 21508
  0.0 4.2 %copy-start = (bf16[7,7,7,56,56]{4,3,2,1,0:T(8,128)(2,1)S(1)}, bf16[7,7,7,56,56]{4,3,2,1,0:T(8,128)(2,1)}, u32[]{:S(2)}) copy-start(bf16[7,7,7,56,56]{4,3,2,1,0:T(8,128)(2,1)} %m2l_ref.3) | copy-start | bytes 6453892
  0.0 4.2 %collective-permute-start = (bf16[4,4,1024]{2,1,0:T(4,128)(2,1)}, bf16[4,4,1024]{2,1,0:T(4,128)(2,1)S(1)}, u32[]{:S(2)}, u32[]{:S(2)}) collective-permute-start(bf16[4,4,1024]{2,1,0:T(4,128)(2,1)} %own_ref.1), channel_id=1, source_target_pairs={{0,1},{1,0},{2,3},{3,2},{4,8},{5,9},{6,10},{7,11},{8,4},{9,5},{10,... | collective-permute-start | bytes 98312 | tf_op jit(solution)/shard_map/ppermute | solution.py:36
  0.1 4.1 %collective-permute-start.1 = (bf16[4,4,1024]{2,1,0:T(4,128)(2,1)}, bf16[4,4,1024]{2,1,0:T(4,128)(2,1)S(1)}, u32[]{:S(2)}, u32[]{:S(2)}) collective-permute-start(bf16[4,4,1024]{2,1,0:T(4,128)(2,1)} %own_ref.1), channel_id=1, source_target_pairs={{0,4},{1,5},{2,6},{3,7},{4,0},{5,1},{6,2},{7,3},{8,12},{9,13},{10,... | collective-permute-start | bytes 98312 | tf_op jit(solution)/shard_map/ppermute | solution.py:36
  4.4 4.0 %collective-permute-start.2 = (bf16[128,128]{1,0:T(8,128)(2,1)S(1)}, bf16[128,128]{1,0:T(8,128)(2,1)S(1)}, u32[]{:S(2)}, u32[]{:S(2)}) collective-permute-start(bf16[128,128]{1,0:T(8,128)(2,1)S(1)} %get-tuple-element.26), channel_id=1, source_target_pairs={{0,1},{1,0},{2,6},{3,7},{4,5},{5,4},{6,2},{7,3},{8,9},{9,8},{10,14... | collective-permute-start | bytes 98312 | tf_op jit(solution)/shard_map/ppermute | solution.py:36
  4.7 5.0 %collective-permute-start.3 = (bf16[128,128]{1,0:T(8,128)(2,1)S(1)}, bf16[128,128]{1,0:T(8,128)(2,1)S(1)}, u32[]{:S(2)}, u32[]{:S(2)}) collective-permute-start(bf16[128,128]{1,0:T(8,128)(2,1)S(1)} %get-tuple-element.30), channel_id=1, source_target_pairs={{0,4},{1,2},{2,1},{3,7},{4,0},{5,6},{6,5},{7,3},{8,12},{9,10},{10,... | collective-permute-start | bytes 98312 | tf_op jit(solution)/shard_map/ppermute | solution.py:36
  6.0 4.3 %collective-permute-start.4 = (bf16[128,128]{1,0:T(8,128)(2,1)S(1)}, bf16[128,128]{1,0:T(8,128)(2,1)S(1)}, u32[]{:S(2)}, u32[]{:S(2)}) collective-permute-start(bf16[128,128]{1,0:T(8,128)(2,1)S(1)} %get-tuple-element.33), channel_id=1, source_target_pairs={{0,4},{1,5},{2,3},{3,2},{4,0},{5,1},{6,7},{7,6},{8,12},{9,13},{10,... | collective-permute-start | bytes 98312 | tf_op jit(solution)/shard_map/ppermute | solution.py:36

commit v12 on v9

--- a/solution.py
+++ b/solution.py
@@ -117,7 +117,7 @@
 
 
 def join_kernel(
-    trade, own_ref, odd_ref, even_ref, m2l_ref, near_ref, p2m_ref,
+    trade, own_ref, even_ref, odd_ref, m2l_ref, near_ref, p2m_ref,
     own_out, odd_out, even_out, sums_out, rows_ref, far_rows, near_rows,
 ):
     pairs = own_ref.shape[2] // PAIR
@@ -172,7 +172,7 @@
         compiler_params=pltpu.CompilerParams(vmem_limit_bytes=SMALL_LIMIT),
         cost_estimate=pl.CostEstimate(flops=1000000, bytes_accessed=100000, transcendentals=0),
         name="join",
-    )(own, odd, even, m2l_table, near, p2m)
+    )(own, even, odd, m2l_table, near, p2m)
 
 
 def shifted(rows):

time: 11.3 us -> 11.4 us (level)
  waiting for transfers between devices: 1.71 us -> 1.9 us
  starting transfers between devices: 5.81 us -> 5.69 us
    ppermute x5, waiting for transfers between devices: 1.71 us -> 1.9 us  [swapped(): return lax.ppermute(cells, AXES, pairs)]
    ppermute x5, starting transfers between devices: 5.81 us -> 5.69 us  [swapped(): return lax.ppermute(cells, AXES, pairs)]
where the time goes in v12:
time: 11.4 us; the launch traced here: 11.2 us
  starting transfers between devices  5.69 us (50%)
  Pallas kernels  3.57 us (31%)
  waiting for transfers between devices  1.9 us (17%)
    ppermute x5, starting transfers between devices, swapped(): return lax.ppermute(cells, AXES, pairs)  5.69 us
    ppermute x5, waiting for transfers between devices, swapped(): return lax.ppermute(cells, AXES, pairs)  1.9 us
    pallas_call x1, Pallas kernels, inner(): pl.pallas_call(inner_kernel, out_shape=[pltpu.VMEM((128, PAIR), F32), plt...  1.79 us
    pallas_call x1, Pallas kernels, last(): pl.pallas_call(functools.partial(last_kernel, trade), out_shape=jax.Shape...  0.83 us
    pallas_call x2, Pallas kernels, outer(): pl.pallas_call(functools.partial(outer_kernel, trade), out_shape=[pltpu.V...  0.65 us
  transfers between devices with their start and end apart: 5, of which 1 were waited for; matrix products, arithmetic and copies ran while one was open for 0% of the time, Pallas kernels for 23%

profile of v12, /device:TPU:0, one launch (start us, length us, event | category | flops | bytes accessed | tf_op | source)
XLA Modules:
  0.0 11.2 jit_solution(4293171703560878495)
XLA Ops:
  0.0 0.0 copy-start.2
  0.0 0.0 copy-start.4
  0.0 0.0 copy-start.1
  0.0 0.0 copy-start.3
  0.0 0.0 copy-start
  0.0 0.5 %collective-permute-start = (bf16[4,4,1024]{2,1,0:T(4,128)(2,1)}, bf16[4,4,1024]{2,1,0:T(4,128)(2,1)S(1)}, u32[]{:S(2)}, u32[]{:S(2)}) collective-permute-start(bf16[4,4,1024]{2,1,0:T(4,128)(2,1)} %own_ref.1), channel_id=1, source_target_pairs={{0,4},{1,5},{2,6},{3,7},{4,0},{5,1},{6,2},{7,3},{8,12},{9,13},{10,... | collective-permute-start | bytes 98312 | tf_op jit(solution)/shard_map/ppermute | solution.py:36
  0.5 2.6 %collective-permute-start.1 = (bf16[4,4,1024]{2,1,0:T(4,128)(2,1)}, bf16[4,4,1024]{2,1,0:T(4,128)(2,1)S(1)}, u32[]{:S(2)}, u32[]{:S(2)}) collective-permute-start(bf16[4,4,1024]{2,1,0:T(4,128)(2,1)} %own_ref.1), channel_id=1, source_target_pairs={{0,1},{1,0},{2,3},{3,2},{4,8},{5,9},{6,10},{7,11},{8,4},{9,5},{10,... | collective-permute-start | bytes 98312 | tf_op jit(solution)/shard_map/ppermute | solution.py:36
  3.1 0.0 copy-done.4
  3.1 0.0 copy-done.1
  3.1 0.0 copy-done.3
  3.1 0.2 %pack.1 = (bf16[3,3,2,128,128]{4,3,2,1,0:T(8,128)(2,1)S(1)}, bf16[128,128]{1,0:T(8,128)(2,1)S(1)}, bf16[128,128]{1,0:T(8,128)(2,1)S(1)}) custom-call(f32[8,128]{1,0:T(8,128)S(1)} %first.1.first_ref, bf16[56,64]{1,0:T(8,128)(2,1)S(1)} %bitcast.1, bf16[3,3,3,64,64]{4,3,2,1,0:T(8,128)(2,1)S(1)} %copy-done.1, bf16[56,64]{1,0:T(8,128)(2,1)S(1)} %copy-done.4), custom_call_target="tpu_custom_call" | custom-call | flops 4000000 | bytes 10000000 | tf_op jit(solution)/shard_map/pack/pallas_call | solution.py:99
  3.3 0.0 collective-permute-done.even_ref
  3.3 1.9 %collective-permute-done.1.odd_ref = bf16[4,4,1024]{2,1,0:T(4,128)(2,1)S(1)} collective-permute-done((bf16[4,4,1024]{2,1,0:T(4,128)(2,1)}, bf16[4,4,1024]{2,1,0:T(4,128)(2,1)S(1)}, u32[]{:S(2)}, u32[]{:S(2)}) %collective-permute-start.1) | collective-permute-done | bytes 32800 | tf_op jit(solution)/shard_map/ppermute | solution.py:36
  5.2 0.0 copy-done.2
  5.2 0.0 copy-done
  5.2 0.1 join.1
  5.3 2.1 %collective-permute-start.2 = (bf16[128,128]{1,0:T(8,128)(2,1)S(1)}, bf16[128,128]{1,0:T(8,128)(2,1)S(1)}, u32[]{:S(2)}, u32[]{:S(2)}) collective-permute-start(bf16[128,128]{1,0:T(8,128)(2,1)S(1)} %get-tuple-element.24), channel_id=1, source_target_pairs={{0,1},{1,0},{2,6},{3,7},{4,5},{5,4},{6,2},{7,3},{8,9},{9,8},{10,14... | collective-permute-start | bytes 98312 | tf_op jit(solution)/shard_map/ppermute | solution.py:36
  7.4 0.0 collective-permute-start.3
  7.4 0.5 %collective-permute-start.4 = (bf16[128,128]{1,0:T(8,128)(2,1)S(1)}, bf16[128,128]{1,0:T(8,128)(2,1)S(1)}, u32[]{:S(2)}, u32[]{:S(2)}) collective-permute-start(bf16[128,128]{1,0:T(8,128)(2,1)S(1)} %get-tuple-element.31), channel_id=1, source_target_pairs={{0,4},{1,5},{2,3},{3,2},{4,0},{5,1},{6,7},{7,6},{8,12},{9,13},{10,... | collective-permute-start | bytes 98312 | tf_op jit(solution)/shard_map/ppermute | solution.py:36
  7.9 1.8 %inner.1 = (f32[128,128]{1,0:T(8,128)S(1)}, f32[128,128]{1,0:T(8,128)S(1)}, bf16[7,7,3,128,128]{4,3,2,1,0:T(8,128)(2,1)S(1)}) custom-call(bf16[256,128]{1,0:T(8,128)(2,1)S(1)} %get-tuple-element.21.own_ref, bf16[7,7,7,56,56]{4,3,2,1,0:T(8,128)(2,1)S(1)} %copy-done, bf16[3,3,2,128,128]{4,3,2,1,0:T(8,128)(2,1)S(1)} %get-tuple-element.19.near_ref, ...), custom_call_target="tpu_custom_call" | custom-call | flops 400000000 | bytes 6000000 | tf_op jit(solution)/shard_map/inner/pallas_call | solution.py:318
  9.7 0.0 collective-permute-done.2.cells_ref
  9.7 0.6 %outer.2 = (f32[128,128]{1,0:T(8,128)S(1)}, f32[128,128]{1,0:T(8,128)S(1)}) custom-call(f32[128,128]{1,0:T(8,128)S(1)} %get-tuple-element.22.far_part, f32[128,128]{1,0:T(8,128)S(1)} %get-tuple-element.23.near_part, bf16[128,128]{1,0:T(8,128)(2,1)S(1)} %collective-permute-done.2.cells_ref, bf16[7,7,3,128,128]{4,3,2,1,0:T(8,128)(2,1)S(1)} %get-tuple-element.25.far_ref, ...), custom_call_target="tpu_custom_call" | custom-call | flops 200000000 | bytes 3000000 | tf_op jit(solution)/shard_map/outer/pallas_call | solution.py:335
  10.4 0.0 collective-permute-done.3.cells_ref
  10.4 0.0 collective-permute-done.4.cells_ref
  10.4 0.8 %last.1 = f32[4,4,1024]{2,1,0:T(4,128)} custom-call(f32[128,128]{1,0:T(8,128)S(1)} %get-tuple-element.29.far_part, f32[128,128]{1,0:T(8,128)S(1)} %get-tuple-element.30.near_part, bf16[128,128]{1,0:T(8,128)(2,1)S(1)} %collective-permute-done.4.cells_ref, bf16[7,7,3,128,128]{4,3,2,1,0:T(8,128)(2,1)S(1)} %get-tuple-element.25.far_ref, ...), custom_call_target="tpu_custom_call" | custom-call | flops 200000000 | bytes 3000000 | tf_op jit(solution)/shard_map/last/pallas_call | solution.py:348
  (2 shorter events, 0.0 us)
Async XLA Ops:
  0.0 5.2 %copy-start.2 = (bf16[4,4,1024]{2,1,0:T(4,128)(2,1)S(1)}, bf16[4,4,1024]{2,1,0:T(4,128)(2,1)}, u32[]{:S(2)}) copy-start(bf16[4,4,1024]{2,1,0:T(4,128)(2,1)} %own_ref.1) | copy-start | bytes 98308
  0.0 3.1 %copy-start.4 = (bf16[56,64]{1,0:T(8,128)(2,1)S(1)}, bf16[56,64]{1,0:T(8,128)(2,1)}, u32[]{:S(2)}) copy-start(bf16[56,64]{1,0:T(8,128)(2,1)} %l2p_ref.1) | copy-start | bytes 21508
  0.0 3.1 %copy-start.1 = (bf16[3,3,3,64,64]{4,3,2,1,0:T(8,128)(2,1)S(1)}, bf16[3,3,3,64,64]{4,3,2,1,0:T(8,128)(2,1)}, u32[]{:S(2)}) copy-start(bf16[3,3,3,64,64]{4,3,2,1,0:T(8,128)(2,1)} %near_ref.1) | copy-start | bytes 663556
  0.0 3.1 %copy-start.3 = (bf16[64,56]{0,1:T(8,128)(2,1)S(1)}, bf16[64,56]{0,1:T(8,128)(2,1)}, u32[]{:S(2)}) copy-start(bf16[64,56]{0,1:T(8,128)(2,1)} %param.6) | copy-start | bytes 21508
  0.0 5.2 %copy-start = (bf16[7,7,7,56,56]{4,3,2,1,0:T(8,128)(2,1)S(1)}, bf16[7,7,7,56,56]{4,3,2,1,0:T(8,128)(2,1)}, u32[]{:S(2)}) copy-start(bf16[7,7,7,56,56]{4,3,2,1,0:T(8,128)(2,1)} %m2l_ref.3) | copy-start | bytes 6453892
  0.0 3.3 %collective-permute-start = (bf16[4,4,1024]{2,1,0:T(4,128)(2,1)}, bf16[4,4,1024]{2,1,0:T(4,128)(2,1)S(1)}, u32[]{:S(2)}, u32[]{:S(2)}) collective-permute-start(bf16[4,4,1024]{2,1,0:T(4,128)(2,1)} %own_ref.1), channel_id=1, source_target_pairs={{0,4},{1,5},{2,6},{3,7},{4,0},{5,1},{6,2},{7,3},{8,12},{9,13},{10,... | collective-permute-start | bytes 98312 | tf_op jit(solution)/shard_map/ppermute | solution.py:36
  0.5 4.7 %collective-permute-start.1 = (bf16[4,4,1024]{2,1,0:T(4,128)(2,1)}, bf16[4,4,1024]{2,1,0:T(4,128)(2,1)S(1)}, u32[]{:S(2)}, u32[]{:S(2)}) collective-permute-start(bf16[4,4,1024]{2,1,0:T(4,128)(2,1)} %own_ref.1), channel_id=1, source_target_pairs={{0,1},{1,0},{2,3},{3,2},{4,8},{5,9},{6,10},{7,11},{8,4},{9,5},{10,... | collective-permute-start | bytes 98312 | tf_op jit(solution)/shard_map/ppermute | solution.py:36
  5.3 4.4 %collective-permute-start.2 = (bf16[128,128]{1,0:T(8,128)(2,1)S(1)}, bf16[128,128]{1,0:T(8,128)(2,1)S(1)}, u32[]{:S(2)}, u32[]{:S(2)}) collective-permute-start(bf16[128,128]{1,0:T(8,128)(2,1)S(1)} %get-tuple-element.24), channel_id=1, source_target_pairs={{0,1},{1,0},{2,6},{3,7},{4,5},{5,4},{6,2},{7,3},{8,9},{9,8},{10,14... | collective-permute-start | bytes 98312 | tf_op jit(solution)/shard_map/ppermute | solution.py:36
  7.4 2.9 %collective-permute-start.3 = (bf16[128,128]{1,0:T(8,128)(2,1)S(1)}, bf16[128,128]{1,0:T(8,128)(2,1)S(1)}, u32[]{:S(2)}, u32[]{:S(2)}) collective-permute-start(bf16[128,128]{1,0:T(8,128)(2,1)S(1)} %get-tuple-element.28), channel_id=1, source_target_pairs={{0,4},{1,2},{2,1},{3,7},{4,0},{5,6},{6,5},{7,3},{8,12},{9,10},{10,... | collective-permute-start | bytes 98312 | tf_op jit(solution)/shard_map/ppermute | solution.py:36
  7.4 3.0 %collective-permute-start.4 = (bf16[128,128]{1,0:T(8,128)(2,1)S(1)}, bf16[128,128]{1,0:T(8,128)(2,1)S(1)}, u32[]{:S(2)}, u32[]{:S(2)}) collective-permute-start(bf16[128,128]{1,0:T(8,128)(2,1)S(1)} %get-tuple-element.31), channel_id=1, source_target_pairs={{0,4},{1,5},{2,3},{3,2},{4,0},{5,1},{6,7},{7,6},{8,12},{9,13},{10,... | collective-permute-start | bytes 98312 | tf_op jit(solution)/shard_map/ppermute | solution.py:36

commit v13 on v11

--- a/solution.py
+++ b/solution.py
@@ -118,7 +118,7 @@
 
 def join_kernel(
     trade, own_ref, odd_ref, even_ref, m2l_ref, near_ref, p2m_ref,
-    own_out, odd_out, even_out, sums_out, ready_out, rows_ref, far_rows, near_rows, own_rows,
+    own_out, odd_out, even_out, sums_out, rows_ref, far_rows, near_rows,
 ):
     pairs = own_ref.shape[2] // PAIR
     for pair in range(pairs):
@@ -147,10 +147,6 @@
     sums_out[...] = jnp.where(lower, tail, head).astype(BF16)
     before, _ = partners(trade)
 
-    @pl.when(waits_longest())
-    def _():
-        own_near(rows_ref[...], ready_out, near_ref, own_rows)
-
     @pl.when(before)
     def _():
         near_windows(rows_ref[:64], near_rows)
@@ -166,15 +162,13 @@
 def joined(trade, own, odd, even, m2l_table, near, p2m):
     return pl.pallas_call(
         functools.partial(join_kernel, trade),
-        out_shape=[pltpu.VMEM((rows, PAIR), BF16) for rows in (256, 128, 128, 128)]
-        + [pltpu.VMEM((128, PAIR), F32)],
+        out_shape=[pltpu.VMEM((rows, PAIR), BF16) for rows in (256, 128, 128, 128)],
         in_specs=[pl.BlockSpec(memory_space=pltpu.VMEM)] * 6,
-        out_specs=[pl.BlockSpec(memory_space=pltpu.VMEM)] * 5,
+        out_specs=[pl.BlockSpec(memory_space=pltpu.VMEM)] * 4,
         scratch_shapes=[
             pltpu.VMEM((256, PAIR), F32),
             pltpu.VMEM((7, 3, 64, PAIR), BF16),
             pltpu.VMEM((3, 2, 64, PAIR), BF16),
-            pltpu.VMEM((3, 2, 128, PAIR), BF16),
         ],
         compiler_params=pltpu.CompilerParams(vmem_limit_bytes=SMALL_LIMIT),
         cost_estimate=pl.CostEstimate(flops=1000000, bytes_accessed=100000, transcendentals=0),
@@ -222,10 +216,6 @@
                 ].astype(BF16)
 
 
-def waits_longest():
-    return jnp.logical_and(lax.axis_index("gx") < 2, lax.axis_index("gy") == 0)
-
-
 def own_near(cells, near_out, near_ref, near_rows):
     near_windows(cells, near_rows)
     near_out[...] = near_product(near_rows, slice(0, 128), near_ref, 1)
@@ -254,7 +244,7 @@
 
 
 def inner_kernel(
-    own_ref, ready_ref, m2l_ref, near_ref, p2m_ref, far_out, near_out, table_out, far_rows, near_rows
+    own_ref, m2l_ref, near_ref, p2m_ref, far_out, near_out, table_out, far_rows, near_rows
 ):
     far_windows(own_ref[...].astype(F32), p2m_ref, far_rows)
     far_out[...] = jnp.zeros_like(far_out)
@@ -273,15 +263,7 @@
 
         product = far_product(far_rows, slice(32 * start, 32 * (start + len(targets))), packing)
         far_out[32 * targets[0] : 32 * (targets[-1] + 1)] += product
-    early = waits_longest()
-
-    @pl.when(early)
-    def _():
-        near_out[...] = ready_ref[...]
-
-    @pl.when(jnp.logical_not(early))
-    def _():
-        own_near(own_ref[...].astype(F32), near_out, near_ref, near_rows)
+    own_near(own_ref[...].astype(F32), near_out, near_ref, near_rows)
 
 
 def halo_sums(blocks, far_rows):
@@ -353,7 +335,7 @@
             ]
 
 
-def inner(own, ready, m2l_table, near, p2m):
+def inner(own, m2l_table, near, p2m):
     return pl.pallas_call(
         inner_kernel,
         out_shape=[
@@ -361,13 +343,13 @@
             pltpu.VMEM((128, PAIR), F32),
             pltpu.VMEM((7, 7, 3, PAIR, PAIR), BF16),
         ],
-        in_specs=[pl.BlockSpec(memory_space=pltpu.VMEM)] * 5,
+        in_specs=[pl.BlockSpec(memory_space=pltpu.VMEM)] * 4,
         out_specs=[pl.BlockSpec(memory_space=pltpu.VMEM)] * 3,
         scratch_shapes=[pltpu.VMEM((7, 3, 128, PAIR), BF16), pltpu.VMEM((3, 2, 128, PAIR), BF16)],
         compiler_params=pltpu.CompilerParams(vmem_limit_bytes=VMEM_LIMIT),
         cost_estimate=pl.CostEstimate(flops=400000000, bytes_accessed=6000000, transcendentals=0),
         name="inner",
-    )(own, ready, m2l_table, near, p2m)
+    )(own, m2l_table, near, p2m)
 
 
 def outer(trade, far_part, near_part, cells, far, near, p2m):
@@ -405,9 +387,9 @@
     odd, even = swapped(density, "gx", 1, 2), swapped(density, "gx", 0, 2)
     near, p2m, l2p = packed(first(), p2m_operator, near_table, l2p_operator)
     trades = ((0, 4), (1, 2), (2, 4))
-    own, to_odd, to_even, sums, ready = joined(trades[-1], density, odd, even, m2l_table, near, p2m)
+    own, to_odd, to_even, sums = joined(trades[-1], density, odd, even, m2l_table, near, p2m)
     halos = [swapped(part, "gy", *trade) for part, trade in zip((to_even, to_odd, sums), trades)]
-    *parts, far = inner(own, ready, m2l_table, near, p2m)
+    *parts, far = inner(own, m2l_table, near, p2m)
     for trade, halo in zip(trades[:-1], halos):
         parts = outer(trade, *parts, halo, far, near, p2m)
     return last(trades[-1], density.shape, *parts, halos[-1], far, near, p2m, l2p)

time: 11.3 us -> 11.4 us (level)
  the two profiles are of different devices: /device:TPU:2 before, /device:TPU:0 now
where the time goes in v13:
time: 11.4 us; the launch traced here: 11.2 us
  starting transfers between devices  5.81 us (51%)
  Pallas kernels  3.62 us (32%)
  waiting for transfers between devices  1.71 us (15%)
    ppermute x5, starting transfers between devices, swapped(): return lax.ppermute(cells, AXES, pairs)  5.81 us
    pallas_call x1, Pallas kernels, inner(): pl.pallas_call(inner_kernel, out_shape=[pltpu.VMEM((128, PAIR), F32), plt...  1.85 us
    ppermute x5, waiting for transfers between devices, swapped(): return lax.ppermute(cells, AXES, pairs)  1.71 us
    pallas_call x1, Pallas kernels, last(): pl.pallas_call(functools.partial(last_kernel, trade), out_shape=jax.Shape...  0.83 us
    pallas_call x2, Pallas kernels, outer(): pl.pallas_call(functools.partial(outer_kernel, trade), out_shape=[pltpu.V...  0.64 us
  transfers between devices with their start and end apart: 5, of which 1 were waited for; matrix products, arithmetic and copies ran while one was open for 0% of the time, Pallas kernels for 24%

profile of v13, /device:TPU:0, one launch (start us, length us, event | category | flops | bytes accessed | tf_op | source)
XLA Modules:
  0.0 11.2 jit_solution(16349298863789474524)
XLA Ops:
  0.0 0.0 copy-start.2
  0.0 0.0 copy-start.4
  0.0 0.0 copy-start.1
  0.0 0.0 copy-start.3
  0.0 0.0 copy-start
  0.0 3.0 %collective-permute-start = (bf16[4,4,1024]{2,1,0:T(4,128)(2,1)}, bf16[4,4,1024]{2,1,0:T(4,128)(2,1)S(1)}, u32[]{:S(2)}, u32[]{:S(2)}) collective-permute-start(bf16[4,4,1024]{2,1,0:T(4,128)(2,1)} %own_ref.1), channel_id=1, source_target_pairs={{0,1},{1,0},{2,3},{3,2},{4,8},{5,9},{6,10},{7,11},{8,4},{9,5},{10,... | collective-permute-start | bytes 98312 | tf_op jit(solution)/shard_map/ppermute | solution.py:36
  3.0 0.2 %collective-permute-start.1 = (bf16[4,4,1024]{2,1,0:T(4,128)(2,1)}, bf16[4,4,1024]{2,1,0:T(4,128)(2,1)S(1)}, u32[]{:S(2)}, u32[]{:S(2)}) collective-permute-start(bf16[4,4,1024]{2,1,0:T(4,128)(2,1)} %own_ref.1), channel_id=1, source_target_pairs={{0,4},{1,5},{2,6},{3,7},{4,0},{5,1},{6,2},{7,3},{8,12},{9,13},{10,... | collective-permute-start | bytes 98312 | tf_op jit(solution)/shard_map/ppermute | solution.py:36
  3.2 0.0 copy-done.4
  3.2 0.0 copy-done.1
  3.2 0.0 copy-done.3
  3.2 0.2 %pack.1 = (bf16[3,3,2,128,128]{4,3,2,1,0:T(8,128)(2,1)S(1)}, bf16[128,128]{1,0:T(8,128)(2,1)S(1)}, bf16[128,128]{1,0:T(8,128)(2,1)S(1)}) custom-call(f32[8,128]{1,0:T(8,128)S(1)} %first.1.first_ref, bf16[56,64]{1,0:T(8,128)(2,1)S(1)} %bitcast.1, bf16[3,3,3,64,64]{4,3,2,1,0:T(8,128)(2,1)S(1)} %copy-done.1, bf16[56,64]{1,0:T(8,128)(2,1)S(1)} %copy-done.4), custom_call_target="tpu_custom_call" | custom-call | flops 4000000 | bytes 10000000 | tf_op jit(solution)/shard_map/pack/pallas_call | solution.py:99
  3.4 1.7 %collective-permute-done.odd_ref = bf16[4,4,1024]{2,1,0:T(4,128)(2,1)S(1)} collective-permute-done((bf16[4,4,1024]{2,1,0:T(4,128)(2,1)}, bf16[4,4,1024]{2,1,0:T(4,128)(2,1)S(1)}, u32[]{:S(2)}, u32[]{:S(2)}) %collective-permute-start) | collective-permute-done | bytes 32800 | tf_op jit(solution)/shard_map/ppermute | solution.py:36
  5.1 0.0 collective-permute-done.1.even_ref
  5.1 0.0 copy-done.2
  5.1 0.0 copy-done
  5.1 0.1 join.1
  5.3 2.1 %collective-permute-start.2 = (bf16[128,128]{1,0:T(8,128)(2,1)S(1)}, bf16[128,128]{1,0:T(8,128)(2,1)S(1)}, u32[]{:S(2)}, u32[]{:S(2)}) collective-permute-start(bf16[128,128]{1,0:T(8,128)(2,1)S(1)} %get-tuple-element.24), channel_id=1, source_target_pairs={{0,1},{1,0},{2,6},{3,7},{4,5},{5,4},{6,2},{7,3},{8,9},{9,8},{10,14... | collective-permute-start | bytes 98312 | tf_op jit(solution)/shard_map/ppermute | solution.py:36
  7.4 0.0 collective-permute-start.3
  7.4 0.5 %collective-permute-start.4 = (bf16[128,128]{1,0:T(8,128)(2,1)S(1)}, bf16[128,128]{1,0:T(8,128)(2,1)S(1)}, u32[]{:S(2)}, u32[]{:S(2)}) collective-permute-start(bf16[128,128]{1,0:T(8,128)(2,1)S(1)} %get-tuple-element.31), channel_id=1, source_target_pairs={{0,4},{1,5},{2,3},{3,2},{4,0},{5,1},{6,7},{7,6},{8,12},{9,13},{10,... | collective-permute-start | bytes 98312 | tf_op jit(solution)/shard_map/ppermute | solution.py:36
  7.9 1.8 %inner.1 = (f32[128,128]{1,0:T(8,128)S(1)}, f32[128,128]{1,0:T(8,128)S(1)}, bf16[7,7,3,128,128]{4,3,2,1,0:T(8,128)(2,1)S(1)}) custom-call(bf16[256,128]{1,0:T(8,128)(2,1)S(1)} %get-tuple-element.21.own_ref, bf16[7,7,7,56,56]{4,3,2,1,0:T(8,128)(2,1)S(1)} %copy-done, bf16[3,3,2,128,128]{4,3,2,1,0:T(8,128)(2,1)S(1)} %get-tuple-element.19.near_ref, ...), custom_call_target="tpu_custom_call" | custom-call | flops 400000000 | bytes 6000000 | tf_op jit(solution)/shard_map/inner/pallas_call | solution.py:339
  9.7 0.0 collective-permute-done.2.cells_ref
  9.7 0.6 %outer.2 = (f32[128,128]{1,0:T(8,128)S(1)}, f32[128,128]{1,0:T(8,128)S(1)}) custom-call(f32[128,128]{1,0:T(8,128)S(1)} %get-tuple-element.22.far_part, f32[128,128]{1,0:T(8,128)S(1)} %get-tuple-element.23.near_part, bf16[128,128]{1,0:T(8,128)(2,1)S(1)} %collective-permute-done.2.cells_ref, bf16[7,7,3,128,128]{4,3,2,1,0:T(8,128)(2,1)S(1)} %get-tuple-element.25.far_ref, ...), custom_call_target="tpu_custom_call" | custom-call | flops 200000000 | bytes 3000000 | tf_op jit(solution)/shard_map/outer/pallas_call | solution.py:356
  10.3 0.0 collective-permute-done.3.cells_ref
  10.4 0.0 collective-permute-done.4.cells_ref
  10.4 0.8 %last.1 = f32[4,4,1024]{2,1,0:T(4,128)} custom-call(f32[128,128]{1,0:T(8,128)S(1)} %get-tuple-element.29.far_part, f32[128,128]{1,0:T(8,128)S(1)} %get-tuple-element.30.near_part, bf16[128,128]{1,0:T(8,128)(2,1)S(1)} %collective-permute-done.4.cells_ref, bf16[7,7,3,128,128]{4,3,2,1,0:T(8,128)(2,1)S(1)} %get-tuple-element.25.far_ref, ...), custom_call_target="tpu_custom_call" | custom-call | flops 200000000 | bytes 3000000 | tf_op jit(solution)/shard_map/last/pallas_call | solution.py:369
  (2 shorter events, 0.0 us)
Async XLA Ops:
  0.0 5.1 %copy-start.2 = (bf16[4,4,1024]{2,1,0:T(4,128)(2,1)S(1)}, bf16[4,4,1024]{2,1,0:T(4,128)(2,1)}, u32[]{:S(2)}) copy-start(bf16[4,4,1024]{2,1,0:T(4,128)(2,1)} %own_ref.1) | copy-start | bytes 98308
  0.0 3.2 %copy-start.4 = (bf16[56,64]{1,0:T(8,128)(2,1)S(1)}, bf16[56,64]{1,0:T(8,128)(2,1)}, u32[]{:S(2)}) copy-start(bf16[56,64]{1,0:T(8,128)(2,1)} %l2p_ref.1) | copy-start | bytes 21508
  0.0 3.2 %copy-start.1 = (bf16[3,3,3,64,64]{4,3,2,1,0:T(8,128)(2,1)S(1)}, bf16[3,3,3,64,64]{4,3,2,1,0:T(8,128)(2,1)}, u32[]{:S(2)}) copy-start(bf16[3,3,3,64,64]{4,3,2,1,0:T(8,128)(2,1)} %near_ref.1) | copy-start | bytes 663556
  0.0 3.2 %copy-start.3 = (bf16[64,56]{0,1:T(8,128)(2,1)S(1)}, bf16[64,56]{0,1:T(8,128)(2,1)}, u32[]{:S(2)}) copy-start(bf16[64,56]{0,1:T(8,128)(2,1)} %param.6) | copy-start | bytes 21508
  0.0 5.1 %copy-start = (bf16[7,7,7,56,56]{4,3,2,1,0:T(8,128)(2,1)S(1)}, bf16[7,7,7,56,56]{4,3,2,1,0:T(8,128)(2,1)}, u32[]{:S(2)}) copy-start(bf16[7,7,7,56,56]{4,3,2,1,0:T(8,128)(2,1)} %m2l_ref.3) | copy-start | bytes 6453892
  0.0 5.1 %collective-permute-start = (bf16[4,4,1024]{2,1,0:T(4,128)(2,1)}, bf16[4,4,1024]{2,1,0:T(4,128)(2,1)S(1)}, u32[]{:S(2)}, u32[]{:S(2)}) collective-permute-start(bf16[4,4,1024]{2,1,0:T(4,128)(2,1)} %own_ref.1), channel_id=1, source_target_pairs={{0,1},{1,0},{2,3},{3,2},{4,8},{5,9},{6,10},{7,11},{8,4},{9,5},{10,... | collective-permute-start | bytes 98312 | tf_op jit(solution)/shard_map/ppermute | solution.py:36
  3.0 2.1 %collective-permute-start.1 = (bf16[4,4,1024]{2,1,0:T(4,128)(2,1)}, bf16[4,4,1024]{2,1,0:T(4,128)(2,1)S(1)}, u32[]{:S(2)}, u32[]{:S(2)}) collective-permute-start(bf16[4,4,1024]{2,1,0:T(4,128)(2,1)} %own_ref.1), channel_id=1, source_target_pairs={{0,4},{1,5},{2,6},{3,7},{4,0},{5,1},{6,2},{7,3},{8,12},{9,13},{10,... | collective-permute-start | bytes 98312 | tf_op jit(solution)/shard_map/ppermute | solution.py:36
  5.3 4.5 %collective-permute-start.2 = (bf16[128,128]{1,0:T(8,128)(2,1)S(1)}, bf16[128,128]{1,0:T(8,128)(2,1)S(1)}, u32[]{:S(2)}, u32[]{:S(2)}) collective-permute-start(bf16[128,128]{1,0:T(8,128)(2,1)S(1)} %get-tuple-element.24), channel_id=1, source_target_pairs={{0,1},{1,0},{2,6},{3,7},{4,5},{5,4},{6,2},{7,3},{8,9},{9,8},{10,14... | collective-permute-start | bytes 98312 | tf_op jit(solution)/shard_map/ppermute | solution.py:36
  7.4 3.0 %collective-permute-start.3 = (bf16[128,128]{1,0:T(8,128)(2,1)S(1)}, bf16[128,128]{1,0:T(8,128)(2,1)S(1)}, u32[]{:S(2)}, u32[]{:S(2)}) collective-permute-start(bf16[128,128]{1,0:T(8,128)(2,1)S(1)} %get-tuple-element.28), channel_id=1, source_target_pairs={{0,4},{1,2},{2,1},{3,7},{4,0},{5,6},{6,5},{7,3},{8,12},{9,10},{10,... | collective-permute-start | bytes 98312 | tf_op jit(solution)/shard_map/ppermute | solution.py:36
  7.4 3.0 %collective-permute-start.4 = (bf16[128,128]{1,0:T(8,128)(2,1)S(1)}, bf16[128,128]{1,0:T(8,128)(2,1)S(1)}, u32[]{:S(2)}, u32[]{:S(2)}) collective-permute-start(bf16[128,128]{1,0:T(8,128)(2,1)S(1)} %get-tuple-element.31), channel_id=1, source_target_pairs={{0,4},{1,5},{2,3},{3,2},{4,0},{5,1},{6,7},{7,6},{8,12},{9,13},{10,... | collective-permute-start | bytes 98312 | tf_op jit(solution)/shard_map/ppermute | solution.py:36

commit v14 on v9

--- a/solution.py
+++ b/solution.py
@@ -233,6 +233,9 @@
 
 def inner_kernel(own_ref, m2l_ref, near_ref, p2m_ref, far_out, near_out, table_out, far_rows, near_rows):
     column_windows(own_ref[...].astype(F32), p2m_ref, far_rows, near_rows)
+    near_out[...] = near_product(near_rows, slice(0, 128), near_ref, 1)
+    near_out[32:128] += near_product(near_rows, slice(0, 96), near_ref, 0)
+    near_out[0:96] += near_product(near_rows, slice(32, 128), near_ref, 2)
     far_out[...] = jnp.zeros_like(far_out)
     for offset_y in range(7):
         targets = [3] if offset_y == 0 else [0] if offset_y == 6 else [
@@ -249,9 +252,6 @@
 
         product = far_product(far_rows, slice(32 * start, 32 * (start + len(targets))), packing)
         far_out[32 * targets[0] : 32 * (targets[-1] + 1)] += product
-    near_out[...] = near_product(near_rows, slice(0, 128), near_ref, 1)
-    near_out[32:128] += near_product(near_rows, slice(0, 96), near_ref, 0)
-    near_out[0:96] += near_product(near_rows, slice(32, 128), near_ref, 2)
 
 
 def halo_sums(blocks, far_rows):

time: 11.3 us -> 11.3 us (level)
  the two profiles are of different devices: /device:TPU:0 before, /device:TPU:6 now
where the time goes in v14:
time: 11.3 us; the launch traced here: 11.1 us
  Pallas kernels  4.25 us (38%)
  waiting for transfers between devices  3.75 us (33%)
  starting transfers between devices  3.02 us (27%)
    ppermute x5, waiting for transfers between devices, swapped(): return lax.ppermute(cells, AXES, pairs)  3.75 us
    ppermute x5, starting transfers between devices, swapped(): return lax.ppermute(cells, AXES, pairs)  3.02 us
    pallas_call x1, Pallas kernels, inner(): pl.pallas_call(inner_kernel, out_shape=[pltpu.VMEM((128, PAIR), F32), plt...  1.62 us
    pallas_call x1, Pallas kernels, last(): pl.pallas_call(functools.partial(last_kernel, trade), out_shape=jax.Shape...  1.44 us
    pallas_call x1, Pallas kernels, joined(): pl.pallas_call(functools.partial(join_kernel, trade), out_shape=[pltpu.VM...  0.95 us
  transfers between devices with their start and end apart: 5, of which 2 were waited for; matrix products, arithmetic and copies ran while one was open for 0% of the time, Pallas kernels for 17%

profile of v14, /device:TPU:6, one launch (start us, length us, event | category | flops | bytes accessed | tf_op | source)
XLA Modules:
  0.0 11.1 jit_solution(3655956343059947526)
XLA Ops:
  0.0 0.0 copy-start.2
  0.0 0.0 copy-start.4
  0.0 0.0 copy-start.1
  0.0 0.0 copy-start.3
  0.0 0.0 copy-start
  0.0 0.6 %collective-permute-start = (bf16[4,4,1024]{2,1,0:T(4,128)(2,1)}, bf16[4,4,1024]{2,1,0:T(4,128)(2,1)S(1)}, u32[]{:S(2)}, u32[]{:S(2)}) collective-permute-start(bf16[4,4,1024]{2,1,0:T(4,128)(2,1)} %own_ref.1), channel_id=1, source_target_pairs={{0,1},{1,0},{2,3},{3,2},{4,8},{5,9},{6,10},{7,11},{8,4},{9,5},{10,... | collective-permute-start | bytes 98312 | tf_op jit(solution)/shard_map/ppermute | solution.py:36
  0.6 1.2 %collective-permute-start.1 = (bf16[4,4,1024]{2,1,0:T(4,128)(2,1)}, bf16[4,4,1024]{2,1,0:T(4,128)(2,1)S(1)}, u32[]{:S(2)}, u32[]{:S(2)}) collective-permute-start(bf16[4,4,1024]{2,1,0:T(4,128)(2,1)} %own_ref.1), channel_id=1, source_target_pairs={{0,4},{1,5},{2,6},{3,7},{4,0},{5,1},{6,2},{7,3},{8,12},{9,13},{10,... | collective-permute-start | bytes 98312 | tf_op jit(solution)/shard_map/ppermute | solution.py:36
  1.8 0.0 copy-done.4
  1.8 0.0 copy-done.1
  1.8 0.0 copy-done.3
  1.8 0.2 %pack.1 = (bf16[3,3,2,128,128]{4,3,2,1,0:T(8,128)(2,1)S(1)}, bf16[128,128]{1,0:T(8,128)(2,1)S(1)}, bf16[128,128]{1,0:T(8,128)(2,1)S(1)}) custom-call(f32[8,128]{1,0:T(8,128)S(1)} %first.1.first_ref, bf16[56,64]{1,0:T(8,128)(2,1)S(1)} %bitcast.1, bf16[3,3,3,64,64]{4,3,2,1,0:T(8,128)(2,1)S(1)} %copy-done.1, bf16[56,64]{1,0:T(8,128)(2,1)S(1)} %copy-done.4), custom_call_target="tpu_custom_call" | custom-call | flops 4000000 | bytes 10000000 | tf_op jit(solution)/shard_map/pack/pallas_call | solution.py:99
  2.0 2.2 %collective-permute-done.odd_ref = bf16[4,4,1024]{2,1,0:T(4,128)(2,1)S(1)} collective-permute-done((bf16[4,4,1024]{2,1,0:T(4,128)(2,1)}, bf16[4,4,1024]{2,1,0:T(4,128)(2,1)S(1)}, u32[]{:S(2)}, u32[]{:S(2)}) %collective-permute-start) | collective-permute-done | bytes 32800 | tf_op jit(solution)/shard_map/ppermute | solution.py:36
  4.2 0.0 collective-permute-done.1.even_ref
  4.2 0.0 copy-done.2
  4.2 0.0 copy-done
  4.2 1.0 %join.1 = (bf16[256,128]{1,0:T(8,128)(2,1)S(1)}, bf16[128,128]{1,0:T(8,128)(2,1)S(1)}, bf16[128,128]{1,0:T(8,128)(2,1)S(1)}, bf16[128,128]{1,0:T(8,128)(2,1)S(1)}) custom-call(bf16[4,4,1024]{2,1,0:T(4,128)(2,1)S(1)} %copy-done.2, bf16[4,4,1024]{2,1,0:T(4,128)(2,1)S(1)} %collective-permute-done.odd_ref, ...), custom_call_target="tpu_custom_call" | custom-call | flops 1000000 | bytes 100000 | tf_op jit(solution)/shard_map/join/pallas_call | solution.py:162
  5.2 0.1 collective-permute-start.2
  5.3 0.5 %collective-permute-start.3 = (bf16[128,128]{1,0:T(8,128)(2,1)S(1)}, bf16[128,128]{1,0:T(8,128)(2,1)S(1)}, u32[]{:S(2)}, u32[]{:S(2)}) collective-permute-start(bf16[128,128]{1,0:T(8,128)(2,1)S(1)} %get-tuple-element.28), channel_id=1, source_target_pairs={{0,4},{1,2},{2,1},{3,7},{4,0},{5,6},{6,5},{7,3},{8,12},{9,10},{10,... | collective-permute-start | bytes 98312 | tf_op jit(solution)/shard_map/ppermute | solution.py:36
  5.8 0.7 %collective-permute-start.4 = (bf16[128,128]{1,0:T(8,128)(2,1)S(1)}, bf16[128,128]{1,0:T(8,128)(2,1)S(1)}, u32[]{:S(2)}, u32[]{:S(2)}) collective-permute-start(bf16[128,128]{1,0:T(8,128)(2,1)S(1)} %get-tuple-element.31), channel_id=1, source_target_pairs={{0,4},{1,5},{2,3},{3,2},{4,0},{5,1},{6,7},{7,6},{8,12},{9,13},{10,... | collective-permute-start | bytes 98312 | tf_op jit(solution)/shard_map/ppermute | solution.py:36
  6.5 1.6 %inner.1 = (f32[128,128]{1,0:T(8,128)S(1)}, f32[128,128]{1,0:T(8,128)S(1)}, bf16[7,7,3,128,128]{4,3,2,1,0:T(8,128)(2,1)S(1)}) custom-call(bf16[256,128]{1,0:T(8,128)(2,1)S(1)} %get-tuple-element.21.own_ref, bf16[7,7,7,56,56]{4,3,2,1,0:T(8,128)(2,1)S(1)} %copy-done, bf16[3,3,2,128,128]{4,3,2,1,0:T(8,128)(2,1)S(1)} %get-tuple-element.19.near_ref, ...), custom_call_target="tpu_custom_call" | custom-call | flops 400000000 | bytes 6000000 | tf_op jit(solution)/shard_map/inner/pallas_call | solution.py:318
  8.1 0.0 collective-permute-done.2.cells_ref
  8.1 0.0 collective-permute-done.3.cells_ref
  8.2 1.5 %collective-permute-done.4.cells_ref = bf16[128,128]{1,0:T(8,128)(2,1)S(1)} collective-permute-done((bf16[128,128]{1,0:T(8,128)(2,1)S(1)}, bf16[128,128]{1,0:T(8,128)(2,1)S(1)}, u32[]{:S(2)}, u32[]{:S(2)}) %collective-permute-start.4) | collective-permute-done | bytes 32800 | tf_op jit(solution)/shard_map/ppermute | solution.py:36
  9.7 1.4 %last.1 = f32[4,4,1024]{2,1,0:T(4,128)} custom-call(f32[128,128]{1,0:T(8,128)S(1)} %get-tuple-element.29.far_part, f32[128,128]{1,0:T(8,128)S(1)} %get-tuple-element.30.near_part, bf16[128,128]{1,0:T(8,128)(2,1)S(1)} %collective-permute-done.4.cells_ref, bf16[7,7,3,128,128]{4,3,2,1,0:T(8,128)(2,1)S(1)} %get-tuple-element.25.far_ref, ...), custom_call_target="tpu_custom_call" | custom-call | flops 200000000 | bytes 3000000 | tf_op jit(solution)/shard_map/last/pallas_call | solution.py:348
  (3 shorter events, 0.0 us)
Async XLA Ops:
  0.0 4.2 %copy-start.2 = (bf16[4,4,1024]{2,1,0:T(4,128)(2,1)S(1)}, bf16[4,4,1024]{2,1,0:T(4,128)(2,1)}, u32[]{:S(2)}) copy-start(bf16[4,4,1024]{2,1,0:T(4,128)(2,1)} %own_ref.1) | copy-start | bytes 98308
  0.0 1.8 %copy-start.4 = (bf16[56,64]{1,0:T(8,128)(2,1)S(1)}, bf16[56,64]{1,0:T(8,128)(2,1)}, u32[]{:S(2)}) copy-start(bf16[56,64]{1,0:T(8,128)(2,1)} %l2p_ref.1) | copy-start | bytes 21508
  0.0 1.8 %copy-start.1 = (bf16[3,3,3,64,64]{4,3,2,1,0:T(8,128)(2,1)S(1)}, bf16[3,3,3,64,64]{4,3,2,1,0:T(8,128)(2,1)}, u32[]{:S(2)}) copy-start(bf16[3,3,3,64,64]{4,3,2,1,0:T(8,128)(2,1)} %near_ref.1) | copy-start | bytes 663556
  0.0 1.8 %copy-start.3 = (bf16[64,56]{0,1:T(8,128)(2,1)S(1)}, bf16[64,56]{0,1:T(8,128)(2,1)}, u32[]{:S(2)}) copy-start(bf16[64,56]{0,1:T(8,128)(2,1)} %param.6) | copy-start | bytes 21508
  0.0 4.2 %copy-start = (bf16[7,7,7,56,56]{4,3,2,1,0:T(8,128)(2,1)S(1)}, bf16[7,7,7,56,56]{4,3,2,1,0:T(8,128)(2,1)}, u32[]{:S(2)}) copy-start(bf16[7,7,7,56,56]{4,3,2,1,0:T(8,128)(2,1)} %m2l_ref.3) | copy-start | bytes 6453892
  0.0 4.2 %collective-permute-start = (bf16[4,4,1024]{2,1,0:T(4,128)(2,1)}, bf16[4,4,1024]{2,1,0:T(4,128)(2,1)S(1)}, u32[]{:S(2)}, u32[]{:S(2)}) collective-permute-start(bf16[4,4,1024]{2,1,0:T(4,128)(2,1)} %own_ref.1), channel_id=1, source_target_pairs={{0,1},{1,0},{2,3},{3,2},{4,8},{5,9},{6,10},{7,11},{8,4},{9,5},{10,... | collective-permute-start | bytes 98312 | tf_op jit(solution)/shard_map/ppermute | solution.py:36
  0.6 3.6 %collective-permute-start.1 = (bf16[4,4,1024]{2,1,0:T(4,128)(2,1)}, bf16[4,4,1024]{2,1,0:T(4,128)(2,1)S(1)}, u32[]{:S(2)}, u32[]{:S(2)}) collective-permute-start(bf16[4,4,1024]{2,1,0:T(4,128)(2,1)} %own_ref.1), channel_id=1, source_target_pairs={{0,4},{1,5},{2,6},{3,7},{4,0},{5,1},{6,2},{7,3},{8,12},{9,13},{10,... | collective-permute-start | bytes 98312 | tf_op jit(solution)/shard_map/ppermute | solution.py:36
  5.2 2.9 %collective-permute-start.2 = (bf16[128,128]{1,0:T(8,128)(2,1)S(1)}, bf16[128,128]{1,0:T(8,128)(2,1)S(1)}, u32[]{:S(2)}, u32[]{:S(2)}) collective-permute-start(bf16[128,128]{1,0:T(8,128)(2,1)S(1)} %get-tuple-element.24), channel_id=1, source_target_pairs={{0,1},{1,0},{2,6},{3,7},{4,5},{5,4},{6,2},{7,3},{8,9},{9,8},{10,14... | collective-permute-start | bytes 98312 | tf_op jit(solution)/shard_map/ppermute | solution.py:36
  5.3 2.9 %collective-permute-start.3 = (bf16[128,128]{1,0:T(8,128)(2,1)S(1)}, bf16[128,128]{1,0:T(8,128)(2,1)S(1)}, u32[]{:S(2)}, u32[]{:S(2)}) collective-permute-start(bf16[128,128]{1,0:T(8,128)(2,1)S(1)} %get-tuple-element.28), channel_id=1, source_target_pairs={{0,4},{1,2},{2,1},{3,7},{4,0},{5,6},{6,5},{7,3},{8,12},{9,10},{10,... | collective-permute-start | bytes 98312 | tf_op jit(solution)/shard_map/ppermute | solution.py:36
  5.8 3.9 %collective-permute-start.4 = (bf16[128,128]{1,0:T(8,128)(2,1)S(1)}, bf16[128,128]{1,0:T(8,128)(2,1)S(1)}, u32[]{:S(2)}, u32[]{:S(2)}) collective-permute-start(bf16[128,128]{1,0:T(8,128)(2,1)S(1)} %get-tuple-element.31), channel_id=1, source_target_pairs={{0,4},{1,5},{2,3},{3,2},{4,0},{5,1},{6,7},{7,6},{8,12},{9,13},{10,... | collective-permute-start | bytes 98312 | tf_op jit(solution)/shard_map/ppermute | solution.py:36
